TPU v7x, 256 devices: a whole 4x4x8 slice. The times are simulated.
256 devices in a mesh: space: 8 (over y, core), tm: 32 (over x, z).
Axes of the slice: x: 4, y: 4, z: 8, core: 2. Of those that a mesh axis runs over, the one named last changes fastest.
Arguments:
- snapshots: float32 [8192, 61440], P('tm', 'space'), may hold values from -6 to 6
- closing: float32 [128, 61440], P(None, 'space'), may hold values from -6 to 6
- weights: float32 [61440], P('space'), may hold values from 0.25 to 36, as said below
- bin_index: int32 [64], replicated, may hold values from 0 to 128, as said below
Outputs:
- spectra: float32 [64, 2, 64, 64], P('tm', None, 'space')
Inputs may be any that keep to these rules, and one draw needn't show every extreme that they name: `bin_index`: distinct bins. Positive weights.
All inputs are finite; a program needn't handle non-finite values.
Results may differ from a plain program's by a relative error of at most 0.0003.
Values sent between devices are 32-bit elements; how exact they have to be, the bound alone decides.
No kernel may reach another device: no remote copies, remote signals or barrier semaphores. Data moves between devices by JAX's collectives and lax.ppermute only.
A program may use at most 128 MiB of HBM per device.

v0:
```python
import jax
import jax.numpy as jnp
from jax import lax
from jax.sharding import PartitionSpec as P

NFFT = 256
NBINS = 64


def passed_along(array, axis, by):
    peers = lax.axis_size(axis)
    pairs = [(i, i + by) for i in range(peers) if 0 <= i + by < peers]
    return lax.ppermute(array, axis, pairs)


def split_up(array, dim, peers):
    before, after = (array.shape[:dim], array.shape[dim + 1 :])
    return jnp.moveaxis(array.reshape(*before, peers, -1, *after), dim, 0)


def sent_and_summed(array, axis, dim):
    peers = lax.axis_size(axis)
    parts = lax.all_to_all(split_up(array, dim, peers), axis, 0, 0, tiled=True)
    return jnp.sum(parts, axis=0)


def sent_to_all(array, axis):
    peers = lax.axis_size(axis)
    return lax.all_to_all(
        jnp.broadcast_to(array[None], (peers, *array.shape)), axis, 0, 0, tiled=True
    )


def of_everyone(array, axis):
    return sent_to_all(array, axis).sum(axis=0)


def spectral_table(bin_index, length):
    sample = jnp.arange(length, dtype=jnp.int32)
    window = 0.5 - 0.5 * jnp.cos(2.0 * jnp.pi * sample.astype(jnp.float32) / length)
    phase_turns = sample[:, None] * bin_index[None, :] % length
    phase_angle = 2.0 * jnp.pi * phase_turns.astype(jnp.float32) / length
    paired = jnp.stack(
        [window[:, None] * jnp.cos(phase_angle), -window[:, None] * jnp.sin(phase_angle)], axis=2
    )
    return paired.reshape(length, 2 * bin_index.shape[0])


def cross_spectra(first_set, second_set):
    products = jnp.einsum(
        "kaip,kbjp->kabij", first_set, second_set, precision=lax.Precision.HIGHEST
    )
    real_part = products[:, 0, 0] + products[:, 1, 1]
    imag_part = products[:, 0, 1] - products[:, 1, 0]
    return jnp.stack([real_part, imag_part], axis=1)


def body(snapshots, closing, weights, bin_index):
    stride_rows = NFFT // 2
    tail_rows = closing.shape[0]
    blocks_here = snapshots.shape[0] // stride_rows
    points = snapshots.shape[1]
    width_tm = lax.axis_size("tm")
    width_space = lax.axis_size("space")
    blocks_all = blocks_here * width_tm
    own_rows = blocks_all // width_space
    basis_table = spectral_table(bin_index, NFFT)
    incoming = passed_along(snapshots[:tail_rows], "tm", -1)
    last_device = lax.axis_index("tm") == width_tm - 1
    series = jnp.concatenate([snapshots, jnp.where(last_device, closing, incoming)], axis=0)
    leading = series[: blocks_here * stride_rows].reshape(blocks_here, stride_rows, points)
    trailing = series[stride_rows:].reshape(blocks_here, stride_rows, points)
    pieces = jnp.concatenate([leading, trailing], axis=1)
    spectrum = jnp.einsum("nc,bnp->cbp", basis_table, pieces, precision=lax.Precision.HIGHEST)
    spectrum = spectrum.reshape(NBINS, 2, blocks_here, points)
    gathered = lax.all_to_all(spectrum, "tm", split_axis=0, concat_axis=2, tiled=True)
    weighted = gathered * weights
    summed = sent_and_summed(cross_spectra(gathered, weighted).transpose(2, 0, 1, 3), "space", 0)
    row_ids = lax.axis_index("space") * own_rows + jnp.arange(own_rows, dtype=jnp.int32)
    diagonal = (row_ids[:, None] == jnp.arange(blocks_all, dtype=jnp.int32)[None, :]).astype(
        jnp.float32
    )
    local_trace = jnp.einsum(
        "rkj,rj->k", summed[:, :, 0, :], diagonal, precision=lax.Precision.HIGHEST
    )
    energy = of_everyone(local_trace, "space")
    spectra = summed * (blocks_all / energy)[None, :, None, None]
    return spectra.transpose(1, 2, 0, 3)


def solution(mesh):
    return jax.shard_map(
        body,
        mesh=mesh,
        in_specs=(P("tm", "space"), P(None, "space"), P("space"), P()),
        out_specs=P("tm", None, "space", None),
        check_vma=False,
    )
```

profile of v0, /device:TPU:2, one launch (start us, length us, event | category | flops | bytes accessed | tf_op | source)
XLA Modules:
  0.0 373.2 jit_solution(3427054506885563299)
XLA Ops:
  0.0 4.3 %slice.21 = f32[128,7680]{1,0:T(8,128)} slice(f32[256,7680]{1,0:T(8,128)} %param.4), slice={[0:128], [0:7680]} | slice | bytes 7864320 | tf_op jit(solution)/shard_map/slice | solution.py:68
  4.3 7.7 %collective-permute-start = (f32[128,7680]{1,0:T(8,128)}, f32[128,7680]{1,0:T(8,128)}, u32[]{:S(2)}, u32[]{:S(2)}) collective-permute-start(f32[128,7680]{1,0:T(8,128)} %slice.21), channel_id=1, source_target_pairs={{1,0},{2,1},{3,2},{4,3},{5,4},{6,5},{7,6},{8,7},{9,8},{10,9},{11,1... | collective-permute-start | bytes 11796488 | tf_op jit(solution)/shard_map/ppermute | solution.py:13
  12.1 0.0 copy-done.1
  12.1 0.3 cosine_multiply_fusion
  12.5 0.1 copy.35
  12.6 0.1 reshape.217
  12.7 0.1 dot_general.14
  12.8 83.8 %collective-permute-done = f32[128,7680]{1,0:T(8,128)} collective-permute-done((f32[128,7680]{1,0:T(8,128)}, f32[128,7680]{1,0:T(8,128)}, u32[]{:S(2)}, u32[]{:S(2)}) %collective-permute-start) | collective-permute-done | bytes 3932192 | tf_op jit(solution)/shard_map/ppermute | solution.py:13
  96.5 4.6 %broadcast_select_fusion = f32[128,7680]{1,0:T(8,128)} fusion(f32[128,7680]{1,0:T(8,128)} %param.5, f32[128,7680]{1,0:T(8,128)} %collective-permute-done, pred[]{:T(512)S(6)} %eq.18), kind=kLoop, calls=%fused_computation.11 | loop fusion | flops 983040 | bytes 11796481 | tf_op jit(solution)/shard_map/jit(_where)/select_n | solution.py:70
  101.1 4.0 %pad_maximum_fusion = f32[256,7680]{1,0:T(8,128)S(1)} fusion(f32[128,7680]{1,0:T(8,128)} %broadcast_select_fusion, f32[256,7680]{1,0:T(8,128)} %param.4), kind=kLoop, calls=%fused_computation.4 | loop fusion | flops 1966080 | bytes 19660800 | tf_op jit(solution)/shard_map/concatenate | solution.py:70
  105.1 0.0 slice-done
  105.1 0.3 slice-done.1
  105.5 10.9 %fusion = f32[64,2,2,7680]{3,0,2,1:T(8,128)} fusion(f32[2,128,7680]{2,1,0:T(8,128)S(1)} %bitcast.63, f32[2,128,7680]{2,1,0:T(8,128)S(1)} %bitcast.62, f32[64,2,256,1]{2,1,0,3:T(2,128)S(1)} %bitcast.64), kind=kOutput, calls=%fused_computation.1 | convolution fusion | flops 6043729920 | bytes 23724032 | tf_op jit(solution)/shard_map/nc,bnp->cbp/dot_general | solution.py:74
  116.4 12.4 %copy.37 = f32[64,2,2,7680]{3,2,1,0:T(2,128)} copy(f32[64,2,2,7680]{3,0,2,1:T(8,128)} %fusion) | data formatting | bytes 15728640 | tf_op jit(solution)/shard_map/nc,bnp->cbp/dot_general | solution.py:74
  128.8 9.1 %all-to-all-start = ((f32[64,2,2,7680]{3,2,1,0:T(2,128)}), f32[64,2,2,7680]{3,2,1,0:T(2,128)}, u32[]{:S(2)}, u32[]{:S(2)}) async-start(f32[64,2,2,7680]{3,2,1,0:T(2,128)} %copy.37), calls=%async_computation | async-start | bytes 15728640 | tf_op jit(solution)/shard_map/all_to_all | solution.py:76
  137.9 173.1 %all-to-all-done = f32[64,2,2,7680]{3,2,1,0:T(2,128)} async-done(((f32[64,2,2,7680]{3,2,1,0:T(2,128)}), f32[64,2,2,7680]{3,2,1,0:T(2,128)}, u32[]{:S(2)}, u32[]{:S(2)}) %all-to-all-start) | async-done | bytes 7864352 | tf_op jit(solution)/shard_map/all_to_all | solution.py:76
  311.0 6.8 %copy.62 = f32[32,2,2,2,7680]{4,3,0,2,1:T(2,128)} copy(f32[32,2,2,2,7680]{4,3,2,1,0:T(2,128)} %bitcast.5) | data formatting | bytes 15728640 | tf_op jit(solution)/shard_map/all_to_all | solution.py:76
  317.8 9.9 %all_to_all.23 = f32[2,2,64,7680]{3,2,1,0:T(8,128)} reshape(f32[2,2,32,2,7680]{4,3,2,1,0:T(2,128)} %bitcast.58) | data formatting | bytes 15728640 | tf_op jit(solution)/shard_map/all_to_all | solution.py:76
  327.8 9.9 %reshape.224 = f32[2,2,64,7680,1]{3,2,1,0,4:T(8,128)} reshape(f32[2,2,32,2,7680]{4,3,2,1,0:T(2,128)} %bitcast.59) | data formatting | bytes 15728640 | tf_op jit(solution)/shard_map/all_to_all | solution.py:76
  337.7 0.0 copy-done
  337.7 14.4 %fusion.8 = f32[2,2,2,64,64]{3,4,1,2,0:T(8,128)S(1)} fusion(f32[2,2,64,7680,1]{3,2,1,0,4:T(8,128)} %reshape.224, f32[2,2,64,7680]{3,2,1,0:T(8,128)} %all_to_all.23, f32[7680]{0:T(1024)S(1)} %copy-done), kind=kOutput, calls=%fused_computation.12 | convolution fusion | flops 3021864960 | bytes 15890432 | tf_op jit(solution)/shard_map/kaip,kbjp->kabij/dot_general | solution.py:50
  352.2 0.1 copy.41
  352.3 0.7 reshape.228
  353.1 4.5 %all-to-all-start.1 = ((f32[8,1,2048]{2,1,0:T(1,128)}), f32[8,1,2048]{2,1,0:T(1,128)S(1)}, u32[]{:S(2)}, u32[]{:S(2)}) async-start(f32[8,1,2048]{2,1,0:T(1,128)} %reshape.228), calls=%async_computation.1 | async-start | bytes 131072 | tf_op jit(solution)/shard_map/all_to_all | solution.py:23
  357.6 0.1 fusion.25
  357.7 5.5 %all-to-all-done.1 = f32[8,1,2048]{2,1,0:T(1,128)S(1)} async-done(((f32[8,1,2048]{2,1,0:T(1,128)}), f32[8,1,2048]{2,1,0:T(1,128)S(1)}, u32[]{:S(2)}, u32[]{:S(2)}) %all-to-all-start.1) | async-done | bytes 65568 | tf_op jit(solution)/shard_map/all_to_all | solution.py:23
  363.2 0.5 broadcast.207
  363.7 0.8 reduce.1
  364.6 0.1 reshape.229
  364.7 0.1 convolution_bitcast_fusion
  364.8 7.6 %all_to_all.29 = f32[8,1,2]{2,1,0:T(1,128)S(1)} all-to-all(f32[8,1,2]{2,1,0:T(1,128)S(1)} %broadcast_in_dim.2), channel_id=1, replica_groups=mesh['space'=8,'tm'=32] {'space'}, dimensions={0} | all-to-all | bytes 128 | tf_op jit(solution)/shard_map/all_to_all | solution.py:29
  372.5 0.7 multiply_bitcast_fusion
  (17 shorter events, 0.2 us)
Async XLA Ops:
  0.0 12.1 %copy-start.1 = (s32[64]{0:T(128)S(1)}, s32[64]{0:T(128)}, u32[]{:S(2)}) copy-start(s32[64]{0:T(128)} %param.7) | copy-start | bytes 772
  4.3 92.2 %collective-permute-start = (f32[128,7680]{1,0:T(8,128)}, f32[128,7680]{1,0:T(8,128)}, u32[]{:S(2)}, u32[]{:S(2)}) collective-permute-start(f32[128,7680]{1,0:T(8,128)} %slice.21), channel_id=1, source_target_pairs={{1,0},{2,1},{3,2},{4,3},{5,4},{6,5},{7,6},{8,7},{9,8},{10,9},{11,1... | collective-permute-start | bytes 11796488 | tf_op jit(solution)/shard_map/ppermute | solution.py:13
  96.5 8.6 %slice-start = ((s8[7864320]{0:T(1024)(128)(4,1)}), s8[4194304]{0:T(1024)(128)(4,1)S(1)}, s32[]{:S(2)}) async-start(s8[7864320]{0:T(1024)(128)(4,1)} %bitcast.60), calls=%async_computation.3 | async-start | bytes 8388608
  101.1 4.3 %slice-start.1 = ((s8[7864320]{0:T(1024)(128)(4,1)}), s8[3670016]{0:T(1024)(128)(4,1)S(1)}, s32[]{:S(2)}) async-start(s8[7864320]{0:T(1024)(128)(4,1)} %bitcast.60), calls=%async_computation.4 | async-start | bytes 7340032
  128.8 182.3 %all-to-all-start = ((f32[64,2,2,7680]{3,2,1,0:T(2,128)}), f32[64,2,2,7680]{3,2,1,0:T(2,128)}, u32[]{:S(2)}, u32[]{:S(2)}) async-start(f32[64,2,2,7680]{3,2,1,0:T(2,128)} %copy.37), calls=%async_computation | async-start | bytes 15728640 | tf_op jit(solution)/shard_map/all_to_all | solution.py:76
  327.8 10.0 %copy-start = (f32[7680]{0:T(1024)S(1)}, f32[7680]{0:T(1024)}, u32[]{:S(2)}) copy-start(f32[7680]{0:T(1024)} %param.6) | copy-start | bytes 92164
  353.1 10.2 %all-to-all-start.1 = ((f32[8,1,2048]{2,1,0:T(1,128)}), f32[8,1,2048]{2,1,0:T(1,128)S(1)}, u32[]{:S(2)}, u32[]{:S(2)}) async-start(f32[8,1,2048]{2,1,0:T(1,128)} %reshape.228), calls=%async_computation.1 | async-start | bytes 131072 | tf_op jit(solution)/shard_map/all_to_all | solution.py:23
where the time goes:
time: 377 us; the launch traced here: 373 us
  waiting for transfers between devices  262 us (69%)
  local copies, waits for them, and re-layouts  45.4 us (12%)
  matrix products  25.5 us (7%)
  starting transfers between devices  21.4 us (6%)
  other arithmetic  10.6 us (3%)
  blocking collectives  7.64 us (2%)
    all_to_all x1, waiting for transfers between devices, body(): lax.all_to_all(spectrum, 'tm', split_axis=0, concat_axis=2, tiled=True)  173 us
    ppermute x1, waiting for transfers between devices, passed_along(): return lax.ppermute(array, axis, pairs)  83.8 us
    all_to_all x3, local copies, waits for them, and re-layouts, body(): lax.all_to_all(spectrum, 'tm', split_axis=0, concat_axis=2, tiled=True)  26.7 us
    dot_general x1, matrix products, cross_spectra(): jnp.einsum('kaip,kbjp->kabij', first_set, second_set, precision=lax.Preci...  14.4 us
    dot_general x2, local copies, waits for them, and re-layouts, body(): jnp.einsum('nc,bnp->cbp', basis_table, pieces, precision=lax.Precision.HI...  12.4 us
    dot_general x1, matrix products, body(): jnp.einsum('nc,bnp->cbp', basis_table, pieces, precision=lax.Precision.HI...  10.9 us
    all_to_all x1, starting transfers between devices, body(): lax.all_to_all(spectrum, 'tm', split_axis=0, concat_axis=2, tiled=True)  9.12 us
    ppermute x1, starting transfers between devices, passed_along(): return lax.ppermute(array, axis, pairs)  7.73 us
  transfers between devices with their start and end apart: 3, of which 3 were waited for; matrix products, arithmetic and copies ran while one was open for 0% of the time, Pallas kernels for 0%

commit v1 on v0

v1 whole, which is shorter than its diff:
```python
import jax
import jax.numpy as jnp
from jax import lax
from jax.experimental import pallas as pl
from jax.experimental.pallas import tpu as pltpu
from jax.sharding import PartitionSpec as P

NFFT = 256
NBINS = 64
HOP = NFFT // 2
BLOCKS = 64
LANES = 128
PTS_TM = 192
F32, BF16 = jnp.float32, jnp.bfloat16
VMEM_BYTES = 50 * 2**20


def split(a):
    hi = a.astype(BF16)
    return hi, (a - hi.astype(F32)).astype(BF16)


def dot3(a, b, dims):
    dg = lambda u, v: lax.dot_general(u, v, (dims, ((), ())), preferred_element_type=F32)
    return dg(a[0], b[0]) + dg(a[0], b[1]) + dg(a[1], b[0])


NN, NT = ((1,), (0,)), ((1,), (1,))


def table_rows(bin_index, length):
    sample = jnp.arange(length, dtype=jnp.int32)
    window = 0.5 - 0.5 * jnp.cos(2.0 * jnp.pi * sample.astype(F32) / length)
    turns = sample[None, :] * bin_index[:, None] % length
    angle = 2.0 * jnp.pi * turns.astype(F32) / length
    paired = jnp.stack([window * jnp.cos(angle), -window * jnp.sin(angle)], axis=1)
    return paired.reshape(2 * bin_index.shape[0], length)


def turn_kernel(x_ref, o_ref):
    o_ref[...] = x_ref[...].T


def turned(x, cols):
    rows, step = x.shape[0], 768
    return pl.pallas_call(
        turn_kernel,
        grid=(cols // step,),
        in_specs=[pl.BlockSpec((rows, step), lambda i: (0, i))],
        out_specs=pl.BlockSpec((step, rows), lambda i: (i, 0)),
        out_shape=jax.ShapeDtypeStruct((cols, rows), F32),
        cost_estimate=pl.CostEstimate(flops=0, bytes_accessed=8 * rows * cols, transcendentals=0),
        compiler_params=pltpu.CompilerParams(vmem_limit_bytes=VMEM_BYTES),
        name="turn_samples",
    )(x)


def lane_tile(a, n):
    return a[:, n * LANES : (n + 1) * LANES]


def coef_kernel(t_ref, x_ref, h_ref, o_ref, s_ref):
    table = split(t_ref[...])
    x = x_ref[...]
    tiles = s_ref.shape[0]
    for e, part in enumerate((x, jnp.concatenate([x[HOP:], h_ref[...]], axis=0))):
        got = dot3(table, split(part), NN)
        for n in range(tiles):
            s_ref.at[n][pl.ds(e, 2 * NBINS, stride=2), :] = lane_tile(got, n)
    for n in range(tiles):
        o_ref[:, n] = s_ref[n].reshape(-1, 8, LANES)


def coefs(table, x, halo, first):
    rows, cols = x.shape[0], x.shape[1] - first
    step = 512
    return pl.pallas_call(
        coef_kernel,
        grid=(cols // step,),
        in_specs=[
            pl.BlockSpec((2 * NBINS, rows), lambda i: (0, 0)),
            pl.BlockSpec((rows, step), lambda i: (0, first // step + i)),
            pl.BlockSpec((HOP, step), lambda i: (0, i)),
        ],
        out_specs=pl.BlockSpec((NBINS // 2, step // LANES, 8, LANES), lambda i: (0, i, 0, 0)),
        out_shape=jax.ShapeDtypeStruct((NBINS // 2, cols // LANES, 8, LANES), F32),
        scratch_shapes=[pltpu.VMEM((step // LANES, 4 * NBINS, LANES), F32)],
        cost_estimate=pl.CostEstimate(
            flops=12 * 2 * NBINS * rows * cols, bytes_accessed=10 * rows * cols, transcendentals=0
        ),
        compiler_params=pltpu.CompilerParams(vmem_limit_bytes=VMEM_BYTES),
        name="coefs_by_bin",
    )(table, x, halo)


def re_im(gram):
    half = gram.shape[0] // 2
    other = pltpu.roll(gram[half:], half, 1)
    lane = lax.broadcasted_iota(jnp.int32, other.shape, 1)
    return gram[:half] + jnp.where(lane < half, other, -other)


def points_kernel(where_ref, t_ref, x_ref, c_ref, w_ref, o_ref, s_ref):
    tm_count, pts = x_ref.shape[0], x_ref.shape[1]
    tiles = s_ref.shape[0]
    table = split(t_ref[...])
    blank = jnp.zeros((tiles * LANES - pts, NFFT), F32)

    def transform(j, samples):
        got = dot3(table, split(jnp.concatenate([samples, blank], axis=0)), NT)
        for n in range(tiles):
            s_ref.at[n][pl.ds(j, 2 * NBINS, stride=BLOCKS), :] = lane_tile(got, n)

    def both(t, following):
        x = x_ref[t]
        transform(2 * t, x)
        transform(2 * t + 1, jnp.concatenate([x[:, HOP:], following], axis=1))

    @pl.loop(0, tm_count - 1)
    def _(t):
        both(t, x_ref[t + 1][:, :HOP])

    both(tm_count - 1, c_ref[...])

    y, core, x_at, z_at = (where_ref[n] for n in range(4))
    weights = w_ref[...]

    @pl.loop(0, NBINS)
    def _(k):
        mine = pl.ds(pl.multiple_of(2 * BLOCKS * k, 2 * BLOCKS), 2 * BLOCKS)
        rows = jnp.concatenate([s_ref[n, mine] for n in range(tiles)], axis=1)
        out = re_im(dot3(split(rows), split(rows * weights), NT))
        xr = lax.rem(k // 16 - x_at + 4, 4)
        zr = lax.rem(lax.rem(k // 2, 8) - z_at + 8, 8)
        for s in range(8):
            cr = lax.rem(s % 2 + core, 2)
            yr = lax.rem(s // 2 - y + 4, 4)
            o_ref[cr, yr, xr, zr, lax.rem(k, 2)] = out[8 * s : 8 * s + 8]


def points_gram(where, table, samples, closing, weights):
    wide = -(-samples.shape[1] // NFFT) * NFFT
    vmem = pl.BlockSpec(memory_space=pltpu.VMEM)
    return pl.pallas_call(
        points_kernel,
        in_specs=[pl.BlockSpec(memory_space=pltpu.SMEM), vmem, vmem, vmem, vmem],
        out_specs=vmem,
        out_shape=jax.ShapeDtypeStruct((2, 4, 4, 8, 2, 8, LANES), F32),
        scratch_shapes=[pltpu.VMEM((wide // LANES, 2 * NBINS * BLOCKS, LANES), F32)],
        cost_estimate=pl.CostEstimate(
            flops=6 * 10**9, bytes_accessed=20 * 10**6, transcendentals=0
        ),
        compiler_params=pltpu.CompilerParams(vmem_limit_bytes=VMEM_BYTES),
        name="points_gram",
    )(where, table, samples, closing, weights)


def bins_kernel(where_ref, a_ref, w_ref, b_ref, o_ref, s_ref):
    tiles = s_ref.shape[0]
    tm_count = a_ref.shape[0] // (8 * tiles)
    for n in range(tiles):
        for c in range(4):
            for e in range(2):
                got = a_ref[pl.ds(8 * n + 2 * c + e, tm_count, stride=8 * tiles), :]
                s_ref.at[n][pl.ds(c * BLOCKS + e, tm_count, stride=2), :] = got
    weights = w_ref[...]
    own = 2 * where_ref[0] + where_ref[1]
    row = lax.broadcasted_iota(jnp.int32, (BLOCKS, LANES), 0)
    lane = lax.broadcasted_iota(jnp.int32, (BLOCKS, LANES), 1)
    traces = []
    for b in range(2):
        mine = pl.ds(2 * BLOCKS * b, 2 * BLOCKS)
        rows = jnp.concatenate([s_ref[n, mine] for n in range(tiles)], axis=1)
        out = re_im(dot3(split(rows), split(rows * weights), NT))
        for s in range(8):
            o_ref[s, b] = out[8 * s : 8 * s + 8]
        others = jnp.where(lane[:8] == row[:8] + 8 * own, b_ref[b], 0.0)
        trace = jnp.sum(jnp.where(lane == row, out, 0.0)) + jnp.sum(others)
        traces.append(trace)
    tile = jnp.where(row[:8] == 0, traces[0], traces[1])
    for s in range(8):
        o_ref[s, 2] = tile


def bins_gram(where, coef, weights, others):
    vmem = pl.BlockSpec(memory_space=pltpu.VMEM)
    return pl.pallas_call(
        bins_kernel,
        in_specs=[pl.BlockSpec(memory_space=pltpu.SMEM), vmem, vmem, vmem],
        out_specs=vmem,
        out_shape=jax.ShapeDtypeStruct((8, 3, 8, LANES), F32),
        scratch_shapes=[pltpu.VMEM((weights.shape[1] // LANES, 4 * BLOCKS, LANES), F32)],
        cost_estimate=pl.CostEstimate(
            flops=5 * 10**8, bytes_accessed=2 * 10**6, transcendentals=0
        ),
        compiler_params=pltpu.CompilerParams(vmem_limit_bytes=VMEM_BYTES),
        name="bins_gram",
    )(where, coef, weights, others)


def norm_kernel(r_ref, b_ref, o_ref):
    total = r_ref[0]
    for s in range(1, 8):
        total = total + r_ref[s]
    for b in range(2):
        out = (total[b] + b_ref[b]) * (BLOCKS / total[2, b : b + 1, :])
        o_ref[b, 0] = out[:, :BLOCKS]
        o_ref[b, 1] = out[:, BLOCKS:]


def normalized(parts, others):
    vmem = pl.BlockSpec(memory_space=pltpu.VMEM)
    return pl.pallas_call(
        norm_kernel,
        in_specs=[vmem, vmem],
        out_specs=vmem,
        out_shape=jax.ShapeDtypeStruct((2, 2, 8, BLOCKS), F32),
        name="normalize",
    )(parts, others)


def by_y(d):
    return [(2 * y + c, 2 * ((y + d) % 4) + c) for y in range(4) for c in range(2)]


def by_x(d):
    return [(8 * x + z, 8 * ((x + d) % 4) + z) for x in range(4) for z in range(8)]


def by_z(d):
    return [(8 * x + z, 8 * x + (z + d) % 8) for x in range(4) for z in range(8)]


def reduced(parts):
    held = parts[0] + lax.ppermute(parts[1], "space", [(s, s ^ 1) for s in range(8)])
    for axis, steps, pairs in (("space", 4, by_y), ("tm", 4, by_x), ("tm", 8, by_z)):
        held = sum([lax.ppermute(held[d], axis, pairs(d)) for d in range(1, steps)], held[0])
    return held


def body(snapshots, closing, weights, bin_index):
    tm_count = lax.axis_size("tm")
    tm, space = lax.axis_index("tm"), lax.axis_index("space")
    where = jnp.stack([space // 2, space % 2, tm // 8, tm % 8]).astype(jnp.int32)
    first = tm_count * PTS_TM
    incoming = lax.ppermute(
        snapshots[:HOP, first:], "tm", [(t, t - 1) for t in range(1, tm_count)]
    )
    sent = turned(snapshots, first).reshape(tm_count, PTS_TM, NFFT)
    samples = lax.all_to_all(sent, "tm", 0, 0, tiled=True)
    table = table_rows(bin_index, NFFT)
    halo = jnp.where(tm == tm_count - 1, closing[:, first:], incoming)
    coef = coefs(table, snapshots, halo, first)
    own_closing = lax.dynamic_slice(closing, (0, tm * PTS_TM), (HOP, PTS_TM)).T
    wide = -(-PTS_TM // NFFT) * NFFT
    own_weights = lax.dynamic_slice(weights, (tm * PTS_TM,), (PTS_TM,))
    own_weights = jnp.pad(own_weights, (0, wide - PTS_TM))[None, :]
    samples, coef, own_closing, own_weights, table = lax.optimization_barrier(
        (samples, coef, own_closing, own_weights, table)
    )
    by_bin = lax.all_to_all(coef, "tm", 0, 0, tiled=True)
    others = reduced(points_gram(where, table, samples, own_closing, own_weights))
    parts = bins_gram(where, by_bin.reshape(-1, LANES), weights[None, first:], others)
    return normalized(lax.all_to_all(parts, "space", 0, 0, tiled=True), others)


def solution(mesh):
    return jax.shard_map(
        body,
        mesh=mesh,
        in_specs=(P("tm", "space"), P(None, "space"), P("space"), P()),
        out_specs=P("tm", None, "space", None),
        check_vma=False,
    )
```

time: 377 us -> 295 us (0.78)
  waiting for transfers between devices: 262 us -> 169 us
  Pallas kernels: 0 us -> 55 us
  local copies, waits for them, and re-layouts: 45.4 us -> 3.77 us
  starting transfers between devices: 21.4 us -> 51.5 us
  matrix products: 25.5 us -> 0 us
  other arithmetic: 10.6 us -> 1.95 us
    all_to_all x2, waiting for transfers between devices: 179 us -> 0.01 us  [the longest x1 0.01 us: body(): by_bin = lax.all_to_all(coef, 'tm', 0, 0, tiled=True)]
    ppermute x1 -> x15, waiting for transfers between devices: 83.8 us -> 169 us  [the longest x1 146 us: body(): lax.ppermute(snapshots[:HOP, first:], 'tm', [(t, t - 1) for t in range(1,...]
    pallas_call x0 -> x5, Pallas kernels: none -> 55 us  [the longest x1 37.3 us: points_gram(): pl.pallas_call(points_kernel, in_specs=[pl.BlockSpec(memory_space=pltpu.S...]
    all_to_all x4 -> x0, local copies, waits for them, and re-layouts: 27.2 us -> none  [the longest x3 26.7 us: body(): lax.all_to_all(spectrum, 'tm', split_axis=0, concat_axis=2, tiled=True)]
    dot_general x3 -> x0, matrix products: 25.5 us -> none  [the longest x1 14.4 us: cross_spectra(): jnp.einsum('kaip,kbjp->kabij', first_set, second_set, precision=lax.Preci...]
    ppermute x1 -> x15, starting transfers between devices: 7.73 us -> 28.8 us  [the longest x13 24.2 us: reduced(): lax.ppermute(held[d], axis, pairs(d))]
    dot_general x2 -> x0, local copies, waits for them, and re-layouts: 12.4 us -> none  [body(): jnp.einsum('nc,bnp->cbp', basis_table, pieces, precision=lax.Precision.HI...]
    all_to_all x2, starting transfers between devices: 13.6 us -> 22.7 us  [the longest x1 11.8 us: body(): samples = lax.all_to_all(sent, 'tm', 0, 0, tiled=True)]
  transfers between devices with their start and end apart: 3 -> 17, of which waited for: 3 -> 8; matrix products, arithmetic and copies ran while one was open for 0% -> 2% of each run, Pallas kernels for 0% -> 1%
where the time goes in v1:
time: 295 us; the launch traced here: 291 us
  waiting for transfers between devices  169 us (57%)
  Pallas kernels  55 us (19%)
  starting transfers between devices  51.5 us (17%)
  blocking collectives  8.86 us (3%)
  local copies, waits for them, and re-layouts  3.77 us (1%)
    ppermute x1, waiting for transfers between devices, body(): lax.ppermute(snapshots[:HOP, first:], 'tm', [(t, t - 1) for t in range(1,...  146 us
    pallas_call x1, Pallas kernels, points_gram(): pl.pallas_call(points_kernel, in_specs=[pl.BlockSpec(memory_space=pltpu.S...  37.3 us
    ppermute x13, starting transfers between devices, reduced(): lax.ppermute(held[d], axis, pairs(d))  24.2 us
    ppermute x13, waiting for transfers between devices, reduced(): lax.ppermute(held[d], axis, pairs(d))  23.1 us
    all_to_all x1, starting transfers between devices, body(): samples = lax.all_to_all(sent, 'tm', 0, 0, tiled=True)  11.8 us
    all_to_all x1, starting transfers between devices, body(): by_bin = lax.all_to_all(coef, 'tm', 0, 0, tiled=True)  10.9 us
    all_to_all x1, blocking collectives, body(): return normalized(lax.all_to_all(parts, 'space', 0, 0, tiled=True), others)  8.86 us
    pallas_call x1, Pallas kernels, turned(): pl.pallas_call(turn_kernel, grid=(cols // step,), in_specs=[pl.BlockSpec(...  8.61 us
  transfers between devices with their start and end apart: 17, of which 8 were waited for; matrix products, arithmetic and copies ran while one was open for 2% of the time, Pallas kernels for 1%

profile of v1, /device:TPU:2, one launch (start us, length us, event | category | flops | bytes accessed | tf_op | source)
XLA Modules:
  0.0 290.8 jit_solution(8752043511339076349)
XLA Ops:
  0.0 8.6 %turn_samples.1 = f32[6144,256]{1,0:T(8,128)} custom-call(f32[256,7680]{1,0:T(8,128)} %x_ref.3), custom_call_target="tpu_custom_call" | custom-call | bytes 12582912 | tf_op jit(solution)/shard_map/turn_samples/pallas_call | solution.py:46
  8.6 11.8 %all-to-all-start = ((f32[32,192,256]{2,1,0:T(8,128)}), f32[32,192,256]{2,1,0:T(8,128)}, u32[]{:S(2)}, u32[]{:S(2)}) async-start(f32[32,192,256]{2,1,0:T(8,128)} %bitcast.74), calls=%async_computation | async-start | bytes 12582912 | tf_op jit(solution)/shard_map/all_to_all | solution.py:250
  20.4 1.2 slice.64
  21.6 4.6 %collective-permute-start = (f32[128,1536]{1,0:T(8,128)S(1)}, f32[128,1536]{1,0:T(8,128)S(1)}, u32[]{:S(2)}, u32[]{:S(2)}) collective-permute-start(f32[128,1536]{1,0:T(8,128)S(1)} %slice.64), channel_id=1, source_target_pairs={{1,0},{2,1},{3,2},{4,3},{5,4},{6,5},{7,6},{8,7},{9,8},{10,9},{11,1... | collective-permute-start | bytes 2359304 | tf_op jit(solution)/shard_map/ppermute | solution.py:246
  26.9 1.0 constant_dynamic-slice_fusion
  28.2 146.4 %collective-permute-done = f32[128,1536]{1,0:T(8,128)S(1)} collective-permute-done((f32[128,1536]{1,0:T(8,128)S(1)}, f32[128,1536]{1,0:T(8,128)S(1)}, u32[]{:S(2)}, u32[]{:S(2)}) %collective-permute-start) | collective-permute-done | bytes 786464 | tf_op jit(solution)/shard_map/ppermute | solution.py:246
  174.6 1.2 slice_select_fusion.h_ref
  175.8 4.1 %coefs_by_bin.1 = f32[32,12,8,128]{3,2,1,0:T(8,128)} custom-call(f32[128,256]{1,0:T(8,128)S(1)} %reshape.154.t_ref, f32[256,7680]{1,0:T(8,128)} %x_ref.3, f32[128,1536]{1,0:T(8,128)S(1)} %slice_select_fusion.h_ref), custom_call_target="tpu_custom_call" | custom-call | flops 603979776 | bytes 3932160 | tf_op jit(solution)/shard_map/coefs_by_bin/pallas_call | solution.py:77
  179.8 37.3 %points_gram.1 = f32[2,4,4,8,2,8,128]{6,5,4,3,2,1,0:T(8,128)S(1)} custom-call(s32[4]{0:T(128)S(1)} %pad_add_fusion.where_ref, f32[128,256]{1,0:T(8,128)S(1)} %reshape.154.t_ref, f32[32,192,256]{2,1,0:T(8,128)} %all-to-all-done.x_ref, f32[192,128]{1,0:T(8,128)S(1)} %bitcast.72, f32[1,256]{1,0:T(1,128)S(1)} %bitcast.73), custom_call_target="tpu_custom_call" | custom-call | flops 6000000000 | bytes 20000000 | tf_op jit(solution)/shard_map/points_gram/pallas_call | solution.py:144
  217.2 1.1 slice_bitcast_fusion
  218.2 10.9 %all-to-all-start.1 = ((f32[32,12,8,128]{3,2,1,0:T(8,128)}), f32[32,12,8,128]{3,2,1,0:T(8,128)}, u32[]{:S(2)}, u32[]{:S(2)}) async-start(f32[32,12,8,128]{3,2,1,0:T(8,128)} %coefs_by_bin.1), calls=%async_computation.1 | async-start | bytes 3145728 | tf_op jit(solution)/shard_map/all_to_all | solution.py:261
  229.4 3.1 %collective-permute-start.4 = (f32[4,8,2,8,128]{4,3,2,1,0:T(8,128)S(1)}, f32[4,8,2,8,128]{4,3,2,1,0:T(8,128)S(1)}, u32[]{:S(2)}, u32[]{:S(2)}) collective-permute-start(f32[4,8,2,8,128]{4,3,2,1,0:T(8,128)S(1)} %get-tuple-element.16), channel_id=1, source_target_pairs={{0,192},{32,224},{64,0},{96,32},{128,64},{160,96},{192,128},{224,1... | collective-permute-start | bytes 786440 | tf_op jit(solution)/shard_map/ppermute | solution.py:237
  233.1 1.0 collective-permute-start.2
  234.1 9.7 %collective-permute-done.4 = f32[4,8,2,8,128]{4,3,2,1,0:T(8,128)S(1)} collective-permute-done((f32[4,8,2,8,128]{4,3,2,1,0:T(8,128)S(1)}, f32[4,8,2,8,128]{4,3,2,1,0:T(8,128)S(1)}, u32[]{:S(2)}, u32[]{:S(2)}) %collective-permute-start.4) | collective-permute-done | bytes 262176 | tf_op jit(solution)/shard_map/ppermute | solution.py:237
  243.8 3.7 %collective-permute-done.2 = f32[4,8,2,8,128]{4,3,2,1,0:T(8,128)S(1)} collective-permute-done((f32[4,8,2,8,128]{4,3,2,1,0:T(8,128)S(1)}, f32[4,8,2,8,128]{4,3,2,1,0:T(8,128)S(1)}, u32[]{:S(2)}, u32[]{:S(2)}) %collective-permute-start.2) | collective-permute-done | bytes 262176 | tf_op jit(solution)/shard_map/ppermute | solution.py:237
  247.6 0.7 collective-permute-start.7
  248.2 2.4 collective-permute-start.6
  250.6 1.8 collective-permute-start.5
  252.4 1.7 collective-permute-done.7
  254.1 3.9 %collective-permute-done.6 = f32[8,2,8,128]{3,2,1,0:T(8,128)S(1)} collective-permute-done((f32[8,2,8,128]{3,2,1,0:T(8,128)S(1)}, f32[8,2,8,128]{3,2,1,0:T(8,128)S(1)}, u32[]{:S(2)}, u32[]{:S(2)}) %collective-permute-start.6) | collective-permute-done | bytes 65568 | tf_op jit(solution)/shard_map/ppermute | solution.py:237
  258.1 2.7 collective-permute-start.14
  260.8 2.2 collective-permute-start.13
  263.0 1.1 collective-permute-start.12
  264.1 2.9 %collective-permute-start.11 = (f32[2,8,128]{2,1,0:T(8,128)S(1)}, f32[2,8,128]{2,1,0:T(8,128)S(1)}, u32[]{:S(2)}, u32[]{:S(2)}) collective-permute-start(f32[2,8,128]{2,1,0:T(8,128)S(1)} %get-tuple-element.25), channel_id=1, source_target_pairs={{0,4},{1,5},{2,6},{3,7},{4,0},{5,1},{6,2},{7,3},{8,12},{9,13},{10,... | collective-permute-start | bytes 24584 | tf_op jit(solution)/shard_map/ppermute | solution.py:237
  267.1 1.4 collective-permute-start.10
  268.5 3.5 %collective-permute-start.9 = (f32[2,8,128]{2,1,0:T(8,128)S(1)}, f32[2,8,128]{2,1,0:T(8,128)S(1)}, u32[]{:S(2)}, u32[]{:S(2)}) collective-permute-start(f32[2,8,128]{2,1,0:T(8,128)S(1)} %get-tuple-element.27), channel_id=1, source_target_pairs={{0,2},{1,3},{2,4},{3,5},{4,6},{5,7},{6,0},{7,1},{8,10},{9,11},{10,... | collective-permute-start | bytes 24584 | tf_op jit(solution)/shard_map/ppermute | solution.py:237
  272.0 0.8 collective-permute-start.8
  272.8 0.9 collective-permute-done.10
  274.2 2.6 collective-permute-done.8
  276.9 3.5 %bins_gram.1 = f32[8,3,8,128]{3,2,1,0:T(8,128)S(1)} custom-call(s32[4]{0:T(128)S(1)} %pad_add_fusion.where_ref, f32[3072,128]{1,0:T(8,128)} %bitcast.7.a_ref, f32[1,1536]{1,0:T(1,128)S(1)} %broadcast_in_dim.5.w_ref, f32[2,8,128]{2,1,0:T(8,128)S(1)} %fusion.19.b_ref), custom_call_target="tpu_custom_call" | custom-call | flops 500000000 | bytes 2000000 | tf_op jit(solution)/shard_map/bins_gram/pallas_call | solution.py:187
  280.4 8.9 %all_to_all.15.r_ref = f32[8,3,8,128]{3,2,1,0:T(8,128)} all-to-all(f32[8,3,8,128]{3,2,1,0:T(8,128)S(1)} %bins_gram.1), channel_id=1, replica_groups=mesh['space'=8,'tm'=32] {'space'}, dimensions={0} | all-to-all | bytes 196608 | tf_op jit(solution)/shard_map/all_to_all | solution.py:264
  289.2 1.6 normalize.1
  (37 shorter events, 2.4 us)
Async XLA Ops:
  8.6 17.7 %copy-start.2 = (s32[64]{0:T(128)S(1)}, s32[64]{0:T(128)}, u32[]{:S(2)}) copy-start(s32[64]{0:T(128)} %param.7) | copy-start | bytes 772
  8.6 19.4 %copy-start.1 = (f32[7680]{0:T(1024)S(1)}, f32[7680]{0:T(1024)}, u32[]{:S(2)}) copy-start(f32[7680]{0:T(1024)} %param.6) | copy-start | bytes 92164
  8.6 171.2 %all-to-all-start = ((f32[32,192,256]{2,1,0:T(8,128)}), f32[32,192,256]{2,1,0:T(8,128)}, u32[]{:S(2)}, u32[]{:S(2)}) async-start(f32[32,192,256]{2,1,0:T(8,128)} %bitcast.74), calls=%async_computation | async-start | bytes 12582912 | tf_op jit(solution)/shard_map/all_to_all | solution.py:250
  21.6 152.9 %collective-permute-start = (f32[128,1536]{1,0:T(8,128)S(1)}, f32[128,1536]{1,0:T(8,128)S(1)}, u32[]{:S(2)}, u32[]{:S(2)}) collective-permute-start(f32[128,1536]{1,0:T(8,128)S(1)} %slice.64), channel_id=1, source_target_pairs={{1,0},{2,1},{3,2},{4,3},{5,4},{6,5},{7,6},{8,7},{9,8},{10,9},{11,1... | collective-permute-start | bytes 2359304 | tf_op jit(solution)/shard_map/ppermute | solution.py:246
  218.2 10.9 %collective-permute-start.1 = (f32[4,4,8,2,8,128]{5,4,3,2,1,0:T(8,128)}, f32[4,4,8,2,8,128]{5,4,3,2,1,0:T(8,128)S(1)}, u32[]{:S(2)}, u32[]{:S(2)}) collective-permute-start(f32[4,4,8,2,8,128]{5,4,3,2,1,0:T(8,128)} %slice_bitcast_fusion), channel_id=1, source_target_pairs={{0,32},{32,0},{64,96},{96,64},{128,160},{160,128},{192,224},{224,1... | collective-permute-start | bytes 3145736 | tf_op jit(solution)/shard_map/ppermute | solution.py:235
  218.2 58.7 %all-to-all-start.1 = ((f32[32,12,8,128]{3,2,1,0:T(8,128)}), f32[32,12,8,128]{3,2,1,0:T(8,128)}, u32[]{:S(2)}, u32[]{:S(2)}) async-start(f32[32,12,8,128]{3,2,1,0:T(8,128)} %coefs_by_bin.1), calls=%async_computation.1 | async-start | bytes 3145728 | tf_op jit(solution)/shard_map/all_to_all | solution.py:261
  229.2 43.6 %slice-start = ((f32[7680]{0:T(1024)}), f32[1536]{0:T(1024)S(1)}, s32[]{:S(2)}) async-start(f32[7680]{0:T(1024)} %param.6), calls=%async_computation.3 | async-start | bytes 16384 | tf_op jit(solution)/shard_map/slice | solution.py:263
  229.4 14.4 %collective-permute-start.4 = (f32[4,8,2,8,128]{4,3,2,1,0:T(8,128)S(1)}, f32[4,8,2,8,128]{4,3,2,1,0:T(8,128)S(1)}, u32[]{:S(2)}, u32[]{:S(2)}) collective-permute-start(f32[4,8,2,8,128]{4,3,2,1,0:T(8,128)S(1)} %get-tuple-element.16), channel_id=1, source_target_pairs={{0,192},{32,224},{64,0},{96,32},{128,64},{160,96},{192,128},{224,1... | collective-permute-start | bytes 786440 | tf_op jit(solution)/shard_map/ppermute | solution.py:237
  232.5 11.3 %collective-permute-start.3 = (f32[4,8,2,8,128]{4,3,2,1,0:T(8,128)S(1)}, f32[4,8,2,8,128]{4,3,2,1,0:T(8,128)S(1)}, u32[]{:S(2)}, u32[]{:S(2)}) collective-permute-start(f32[4,8,2,8,128]{4,3,2,1,0:T(8,128)S(1)} %get-tuple-element.17), channel_id=1, source_target_pairs={{0,128},{32,160},{64,192},{96,224},{128,0},{160,32},{192,64},{224,... | collective-permute-start | bytes 786440 | tf_op jit(solution)/shard_map/ppermute | solution.py:237
  233.1 14.4 %collective-permute-start.2 = (f32[4,8,2,8,128]{4,3,2,1,0:T(8,128)S(1)}, f32[4,8,2,8,128]{4,3,2,1,0:T(8,128)S(1)}, u32[]{:S(2)}, u32[]{:S(2)}) collective-permute-start(f32[4,8,2,8,128]{4,3,2,1,0:T(8,128)S(1)} %get-tuple-element.15), channel_id=1, source_target_pairs={{0,64},{32,96},{64,128},{96,160},{128,192},{160,224},{192,0},{224,... | collective-permute-start | bytes 786440 | tf_op jit(solution)/shard_map/ppermute | solution.py:237
  247.6 6.5 %collective-permute-start.7 = (f32[8,2,8,128]{3,2,1,0:T(8,128)S(1)}, f32[8,2,8,128]{3,2,1,0:T(8,128)S(1)}, u32[]{:S(2)}, u32[]{:S(2)}) collective-permute-start(f32[8,2,8,128]{3,2,1,0:T(8,128)S(1)} %get-tuple-element.19), channel_id=1, source_target_pairs={{0,24},{1,25},{2,26},{3,27},{4,28},{5,29},{6,30},{7,31},{8,0},{9,1... | collective-permute-start | bytes 196616 | tf_op jit(solution)/shard_map/ppermute | solution.py:237
  248.2 9.8 %collective-permute-start.6 = (f32[8,2,8,128]{3,2,1,0:T(8,128)S(1)}, f32[8,2,8,128]{3,2,1,0:T(8,128)S(1)}, u32[]{:S(2)}, u32[]{:S(2)}) collective-permute-start(f32[8,2,8,128]{3,2,1,0:T(8,128)S(1)} %get-tuple-element.20), channel_id=1, source_target_pairs={{0,16},{1,17},{2,18},{3,19},{4,20},{5,21},{6,22},{7,23},{8,24},{9,... | collective-permute-start | bytes 196616 | tf_op jit(solution)/shard_map/ppermute | solution.py:237
  250.6 7.4 %collective-permute-start.5 = (f32[8,2,8,128]{3,2,1,0:T(8,128)S(1)}, f32[8,2,8,128]{3,2,1,0:T(8,128)S(1)}, u32[]{:S(2)}, u32[]{:S(2)}) collective-permute-start(f32[8,2,8,128]{3,2,1,0:T(8,128)S(1)} %get-tuple-element.18), channel_id=1, source_target_pairs={{0,8},{1,9},{2,10},{3,11},{4,12},{5,13},{6,14},{7,15},{8,16},{9,17... | collective-permute-start | bytes 196616 | tf_op jit(solution)/shard_map/ppermute | solution.py:237
  258.1 10.4 %collective-permute-start.14 = (f32[2,8,128]{2,1,0:T(8,128)S(1)}, f32[2,8,128]{2,1,0:T(8,128)S(1)}, u32[]{:S(2)}, u32[]{:S(2)}) collective-permute-start(f32[2,8,128]{2,1,0:T(8,128)S(1)} %get-tuple-element.22), channel_id=1, source_target_pairs={{0,7},{1,0},{2,1},{3,2},{4,3},{5,4},{6,5},{7,6},{8,15},{9,8},{10,9... | collective-permute-start | bytes 24584 | tf_op jit(solution)/shard_map/ppermute | solution.py:237
  260.8 11.2 %collective-permute-start.13 = (f32[2,8,128]{2,1,0:T(8,128)S(1)}, f32[2,8,128]{2,1,0:T(8,128)S(1)}, u32[]{:S(2)}, u32[]{:S(2)}) collective-permute-start(f32[2,8,128]{2,1,0:T(8,128)S(1)} %get-tuple-element.23), channel_id=1, source_target_pairs={{0,6},{1,7},{2,0},{3,1},{4,2},{5,3},{6,4},{7,5},{8,14},{9,15},{10,... | collective-permute-start | bytes 24584 | tf_op jit(solution)/shard_map/ppermute | solution.py:237
  263.0 9.8 %collective-permute-start.12 = (f32[2,8,128]{2,1,0:T(8,128)S(1)}, f32[2,8,128]{2,1,0:T(8,128)S(1)}, u32[]{:S(2)}, u32[]{:S(2)}) collective-permute-start(f32[2,8,128]{2,1,0:T(8,128)S(1)} %get-tuple-element.24), channel_id=1, source_target_pairs={{0,5},{1,6},{2,7},{3,0},{4,1},{5,2},{6,3},{7,4},{8,13},{9,14},{10,... | collective-permute-start | bytes 24584 | tf_op jit(solution)/shard_map/ppermute | solution.py:237
  264.1 8.7 %collective-permute-start.11 = (f32[2,8,128]{2,1,0:T(8,128)S(1)}, f32[2,8,128]{2,1,0:T(8,128)S(1)}, u32[]{:S(2)}, u32[]{:S(2)}) collective-permute-start(f32[2,8,128]{2,1,0:T(8,128)S(1)} %get-tuple-element.25), channel_id=1, source_target_pairs={{0,4},{1,5},{2,6},{3,7},{4,0},{5,1},{6,2},{7,3},{8,12},{9,13},{10,... | collective-permute-start | bytes 24584 | tf_op jit(solution)/shard_map/ppermute | solution.py:237
  267.1 6.7 %collective-permute-start.10 = (f32[2,8,128]{2,1,0:T(8,128)S(1)}, f32[2,8,128]{2,1,0:T(8,128)S(1)}, u32[]{:S(2)}, u32[]{:S(2)}) collective-permute-start(f32[2,8,128]{2,1,0:T(8,128)S(1)} %get-tuple-element.26), channel_id=1, source_target_pairs={{0,3},{1,4},{2,5},{3,6},{4,7},{5,0},{6,1},{7,2},{8,11},{9,12},{10,... | collective-permute-start | bytes 24584 | tf_op jit(solution)/shard_map/ppermute | solution.py:237
  268.5 5.8 %collective-permute-start.9 = (f32[2,8,128]{2,1,0:T(8,128)S(1)}, f32[2,8,128]{2,1,0:T(8,128)S(1)}, u32[]{:S(2)}, u32[]{:S(2)}) collective-permute-start(f32[2,8,128]{2,1,0:T(8,128)S(1)} %get-tuple-element.27), channel_id=1, source_target_pairs={{0,2},{1,3},{2,4},{3,5},{4,6},{5,7},{6,0},{7,1},{8,10},{9,11},{10,... | collective-permute-start | bytes 24584 | tf_op jit(solution)/shard_map/ppermute | solution.py:237
  272.0 4.9 %collective-permute-start.8 = (f32[2,8,128]{2,1,0:T(8,128)S(1)}, f32[2,8,128]{2,1,0:T(8,128)S(1)}, u32[]{:S(2)}, u32[]{:S(2)}) collective-permute-start(f32[2,8,128]{2,1,0:T(8,128)S(1)} %get-tuple-element.21), channel_id=1, source_target_pairs={{0,1},{1,2},{2,3},{3,4},{4,5},{5,6},{6,7},{7,0},{8,9},{9,10},{10,1... | collective-permute-start | bytes 24584 | tf_op jit(solution)/shard_map/ppermute | solution.py:237
  276.9 12.4 %copy-start = (f32[2,8,128]{2,1,0:T(8,128)}, f32[2,8,128]{2,1,0:T(8,128)S(1)}, u32[]{:S(2)}) copy-start(f32[2,8,128]{2,1,0:T(8,128)S(1)} %fusion.19.b_ref) | copy-start | bytes 24580

commit v2 on v1

v2 whole, which is shorter than its diff:
```python
import jax
import jax.numpy as jnp
from jax import lax
from jax.experimental import pallas as pl
from jax.experimental.pallas import tpu as pltpu
from jax.sharding import PartitionSpec as P

NFFT = 256
NBINS = 64
HOP = NFFT // 2
BLOCKS = 64
LANES = 128
PTS_TM = 176
F32, BF16 = jnp.float32, jnp.bfloat16
VMEM_BYTES = 50 * 2**20


def split(a):
    hi = a.astype(BF16)
    return hi, (a - hi.astype(F32)).astype(BF16)


def dot3(a, b, dims):
    dg = lambda u, v: lax.dot_general(u, v, (dims, ((), ())), preferred_element_type=F32)
    return dg(a[0], b[0]) + dg(a[0], b[1]) + dg(a[1], b[0])


NN, NT = ((1,), (0,)), ((1,), (1,))


def table_rows(bin_index, length):
    sample = jnp.arange(length, dtype=jnp.int32)
    window = 0.5 - 0.5 * jnp.cos(2.0 * jnp.pi * sample.astype(F32) / length)
    turns = sample[None, :] * bin_index[:, None] % length
    angle = 2.0 * jnp.pi * turns.astype(F32) / length
    paired = jnp.stack([window * jnp.cos(angle), -window * jnp.sin(angle)], axis=1)
    return paired.reshape(2 * bin_index.shape[0], length)


def turn_kernel(x_ref, w_ref, o_ref):
    o_ref[...] = (x_ref[...] * w_ref[...]).T


def turned(x, roots, cols):
    rows, step = x.shape[0], 512
    return pl.pallas_call(
        turn_kernel,
        grid=(cols // step,),
        in_specs=[
            pl.BlockSpec((rows, step), lambda i: (0, i)),
            pl.BlockSpec((1, step), lambda i: (0, i)),
        ],
        out_specs=pl.BlockSpec((step, rows), lambda i: (i, 0)),
        out_shape=jax.ShapeDtypeStruct((cols, rows), F32),
        cost_estimate=pl.CostEstimate(flops=0, bytes_accessed=8 * rows * cols, transcendentals=0),
        compiler_params=pltpu.CompilerParams(vmem_limit_bytes=VMEM_BYTES),
        name="turn_samples",
    )(x, roots)


def lane_tile(a, n):
    return a[:, n * LANES : (n + 1) * LANES]


def coef_kernel(t_ref, w_ref, x_ref, odd_ref, o_ref, s_ref):
    table = split(t_ref[...])
    tiles = s_ref.shape[0]
    for e, part in enumerate((x_ref, odd_ref)):
        got = dot3(table, split(part[...] * w_ref[...]), NN)
        for n in range(tiles):
            s_ref.at[n][pl.ds(e, 2 * NBINS, stride=2), :] = lane_tile(got, n)
    for n in range(tiles):
        o_ref[:, n] = s_ref[n].reshape(-1, 8, LANES)


def coefs(table, roots, x, odd, first):
    rows, cols = x.shape[0], x.shape[1] - first
    step = 512
    return pl.pallas_call(
        coef_kernel,
        grid=(cols // step,),
        in_specs=[
            pl.BlockSpec((2 * NBINS, rows), lambda i: (0, 0)),
            pl.BlockSpec((1, step), lambda i: (0, first // step + i)),
            pl.BlockSpec((rows, step), lambda i: (0, first // step + i)),
            pl.BlockSpec((rows, step), lambda i: (0, i)),
        ],
        out_specs=pl.BlockSpec((NBINS // 2, step // LANES, 8, LANES), lambda i: (0, i, 0, 0)),
        out_shape=jax.ShapeDtypeStruct((NBINS // 2, cols // LANES, 8, LANES), F32),
        scratch_shapes=[pltpu.VMEM((step // LANES, 4 * NBINS, LANES), F32)],
        cost_estimate=pl.CostEstimate(
            flops=12 * 2 * NBINS * rows * cols, bytes_accessed=10 * rows * cols, transcendentals=0
        ),
        compiler_params=pltpu.CompilerParams(vmem_limit_bytes=VMEM_BYTES),
        name="coefs_by_bin",
    )(table, roots, x, odd)


def re_im(gram):
    half = gram.shape[0] // 2
    other = pltpu.roll(gram[half:], half, 1)
    lane = lax.broadcasted_iota(jnp.int32, other.shape, 1)
    return gram[:half] + jnp.where(lane < half, other, -other)


def diagonal(out):
    row = lax.broadcasted_iota(jnp.int32, out.shape, 0)
    lane = lax.broadcasted_iota(jnp.int32, out.shape, 1)
    return jnp.sum(jnp.where(row == lane, out, 0.0), axis=0, keepdims=True)


def two_traces(first, second):
    return diagonal(first) + pltpu.roll(diagonal(second), BLOCKS, 1)


def points_kernel(where_ref, t_ref, x_ref, c_ref, o_ref, s_ref):
    tm_count, pts = x_ref.shape[0], x_ref.shape[1]
    tiles = s_ref.shape[0]
    table = split(t_ref[...])
    blank = jnp.zeros((tiles * LANES - pts, NFFT), F32)

    def transform(j, samples):
        got = dot3(table, split(jnp.concatenate([samples, blank], axis=0)), NT)
        for n in range(tiles):
            s_ref.at[n][pl.ds(j, 2 * NBINS, stride=BLOCKS), :] = lane_tile(got, n)

    def both(t, following):
        x = x_ref[t]
        transform(2 * t, x)
        transform(2 * t + 1, jnp.concatenate([x[:, HOP:], following], axis=1))

    def four(i, carry):
        for n in range(4):
            both(4 * i + n, x_ref[4 * i + n + 1][:, :HOP])
        return carry

    lax.fori_loop(0, tm_count // 4 - 1, four, 0)
    for t in range(tm_count - 4, tm_count - 1):
        both(t, x_ref[t + 1][:, :HOP])
    both(tm_count - 1, c_ref[...])

    y, core, x_at, z_at = (where_ref[n] for n in range(4))

    def owner(t):
        xr = lax.rem(t // 8 - x_at + 4, 4)
        z = lax.rem(t, 8)
        zr = lax.rem(z - z_at + 8, 8)
        outs = []
        for b in range(2):
            mine = pl.ds(pl.multiple_of(2 * BLOCKS * (2 * t + b), 2 * BLOCKS), 2 * BLOCKS)
            rows = split(jnp.concatenate([s_ref[n, mine] for n in range(tiles)], axis=1))
            outs.append(re_im(dot3(rows, rows, NT)))
        traces = two_traces(*outs)
        for s in range(8):
            cr = lax.rem(s % 2 + core, 2)
            yr = lax.rem(s // 2 - y + 4, 4)
            for b in range(2):
                o_ref[cr, yr, xr, 2 * zr + b] = outs[b][8 * s : 8 * s + 8]
            o_ref[cr, yr, xr, 16, pl.ds(z, 1), :] = traces

    def four_owners(i, carry):
        for n in range(4):
            owner(4 * i + n)
        return carry

    lax.fori_loop(0, tm_count // 4, four_owners, 0)


def points_gram(where, table, samples, closing):
    wide = -(-samples.shape[1] // NFFT) * NFFT
    vmem = pl.BlockSpec(memory_space=pltpu.VMEM)
    return pl.pallas_call(
        points_kernel,
        in_specs=[pl.BlockSpec(memory_space=pltpu.SMEM), vmem, vmem, vmem],
        out_specs=vmem,
        out_shape=jax.ShapeDtypeStruct((2, 4, 4, 17, 8, LANES), F32),
        scratch_shapes=[pltpu.VMEM((wide // LANES, 2 * NBINS * BLOCKS, LANES), F32)],
        cost_estimate=pl.CostEstimate(
            flops=6 * 10**9, bytes_accessed=20 * 10**6, transcendentals=0
        ),
        compiler_params=pltpu.CompilerParams(vmem_limit_bytes=VMEM_BYTES),
        name="points_gram",
    )(where, table, samples, closing)


def bins_kernel(a_ref, o_ref, s_ref):
    tiles = s_ref.shape[0]
    tm_count = a_ref.shape[0] // (8 * tiles)
    for n in range(tiles):
        for c in range(4):
            for e in range(2):
                got = a_ref[pl.ds(8 * n + 2 * c + e, tm_count, stride=8 * tiles), :]
                if e == 1 and n >= tiles // 2:
                    got = pltpu.roll(got, tm_count - 1, 0)
                s_ref.at[n][pl.ds(c * BLOCKS + e, tm_count, stride=2), :] = got
    outs = []
    for b in range(2):
        mine = pl.ds(2 * BLOCKS * b, 2 * BLOCKS)
        rows = split(jnp.concatenate([s_ref[n, mine] for n in range(tiles)], axis=1))
        outs.append(re_im(dot3(rows, rows, NT)))
    traces = jnp.broadcast_to(two_traces(*outs), (8, LANES))
    for s in range(8):
        for b in range(2):
            o_ref[s, b] = outs[b][8 * s : 8 * s + 8]
        o_ref[s, 2] = traces


def bins_gram(coef):
    vmem = pl.BlockSpec(memory_space=pltpu.VMEM)
    tiles = coef.shape[1]
    return pl.pallas_call(
        bins_kernel,
        in_specs=[vmem],
        out_specs=vmem,
        out_shape=jax.ShapeDtypeStruct((8, 3, 8, LANES), F32),
        scratch_shapes=[pltpu.VMEM((tiles, 4 * BLOCKS, LANES), F32)],
        cost_estimate=pl.CostEstimate(
            flops=5 * 10**8, bytes_accessed=2 * 10**6, transcendentals=0
        ),
        compiler_params=pltpu.CompilerParams(vmem_limit_bytes=VMEM_BYTES),
        name="bins_gram",
    )(coef.reshape(-1, LANES))


def norm_kernel(where_ref, r_ref, *refs):
    o_ref = refs[-1]
    total = r_ref[0]
    for s in range(1, 8):
        total = total + r_ref[s]
    for ref in refs[:-1]:
        total = total + ref[...]
    row = lax.broadcasted_iota(jnp.int32, (8, LANES), 0)
    lane = lax.broadcasted_iota(jnp.int32, (8, LANES), 1)
    for b in range(2):
        mine = (row == where_ref[3]) & (lane // BLOCKS == b)
        energy = jnp.sum(jnp.where(mine, total[2], 0.0), keepdims=True)
        out = total[b] * (BLOCKS / energy)
        o_ref[b, 0] = out[:, :BLOCKS]
        o_ref[b, 1] = out[:, BLOCKS:]


def normalized(where, parts, others):
    vmem = pl.BlockSpec(memory_space=pltpu.VMEM)
    return pl.pallas_call(
        norm_kernel,
        in_specs=[pl.BlockSpec(memory_space=pltpu.SMEM)] + [vmem] * (1 + len(others)),
        out_specs=vmem,
        out_shape=jax.ShapeDtypeStruct((2, 2, 8, BLOCKS), F32),
        name="normalize",
    )(where, parts, *others)


def by_y(d):
    return [(2 * y + c, 2 * ((y + d) % 4) + c) for y in range(4) for c in range(2)]


def by_x(d):
    return [(8 * x + z, 8 * ((x + d) % 4) + z) for x in range(4) for z in range(8)]


def by_z(d):
    return [(8 * x + z, 8 * x + (z + d) % 8) for x in range(4) for z in range(8)]


def summed_up(held, axis, steps, pairs):
    return sum([lax.ppermute(held[d], axis, pairs(d)) for d in range(1, steps)], held[0])


def odd_blocks(snapshots, closing, tm, tm_count, first):
    middle = (first + snapshots.shape[1]) // 2
    down = lax.ppermute(
        snapshots[:HOP, first:middle], "tm", [(t, t - 1) for t in range(1, tm_count)]
    )
    up = lax.ppermute(
        snapshots[HOP:, middle:], "tm", [(t, (t + 1) % tm_count) for t in range(tm_count)]
    )

    def finish(down, up):
        after = jnp.where(tm == tm_count - 1, closing[:, first:middle], down)
        ending = jnp.where(tm == 0, closing[:, middle:], snapshots[:HOP, middle:])
        return jnp.concatenate(
            [
                jnp.concatenate([snapshots[HOP:, first:middle], after], axis=0),
                jnp.concatenate([up, ending], axis=0),
            ],
            axis=1,
        )

    return down, up, finish


def body(snapshots, closing, weights, bin_index):
    tm_count = lax.axis_size("tm")
    tm, space = lax.axis_index("tm"), lax.axis_index("space")
    where = jnp.stack([space // 2, space % 2, tm // 8, tm % 8]).astype(jnp.int32)
    first = tm_count * PTS_TM
    roots = jnp.sqrt(weights)[None, :]
    down, up, finish = odd_blocks(snapshots, closing, tm, tm_count, first)
    sent = turned(snapshots, roots, first).reshape(tm_count, PTS_TM, NFFT)
    sent, down, up = lax.optimization_barrier((sent, down, up))
    samples = lax.all_to_all(sent, "tm", 0, 0, tiled=True)
    table = table_rows(bin_index, NFFT)
    coef = coefs(table, roots, snapshots, finish(down, up), first)
    own_roots = lax.dynamic_slice(roots, (0, tm * PTS_TM), (1, PTS_TM))
    own_closing = lax.dynamic_slice(closing, (0, tm * PTS_TM), (HOP, PTS_TM)) * own_roots
    samples, coef, own_closing = lax.optimization_barrier((samples, coef, own_closing.T))
    by_bin = lax.all_to_all(coef, "tm", 0, 0, tiled=True)
    parts = points_gram(where, table, samples, own_closing)
    held = parts[0] + lax.ppermute(parts[1], "space", [(s, s ^ 1) for s in range(8)])
    held = summed_up(summed_up(held, "space", 4, by_y), "tm", 4, by_x)
    by_bin, held = lax.optimization_barrier((by_bin, held))
    others = [jnp.concatenate([held[2 * d : 2 * d + 2], held[16:]], axis=0) for d in range(8)]
    others[1:] = [lax.ppermute(others[d], "tm", by_z(d)) for d in range(1, 8)]
    parts = lax.all_to_all(bins_gram(by_bin), "space", 0, 0, tiled=True)
    return normalized(where, parts, others)


def solution(mesh):
    return jax.shard_map(
        body,
        mesh=mesh,
        in_specs=(P("tm", "space"), P(None, "space"), P("space"), P()),
        out_specs=P("tm", None, "space", None),
        check_vma=False,
    )
```

time: 295 us -> 248 us (0.84)
  waiting for transfers between devices: 169 us -> 145 us
  Pallas kernels: 55 us -> 38.2 us
  blocking collectives: 8.86 us -> 0 us
  other arithmetic: 1.95 us -> 5.92 us
    ppermute x15 -> x16, waiting for transfers between devices: 169 us -> 28.4 us  [the longest x6 17.6 us: summed_up(): lax.ppermute(held[d], axis, pairs(d))]
    all_to_all x1, waiting for transfers between devices: 0.01 us -> 116 us  [body(): samples = lax.all_to_all(sent, 'tm', 0, 0, tiled=True)]
    pallas_call x1, Pallas kernels: 37.3 us -> 19.5 us  [points_gram(): pl.pallas_call(points_kernel, in_specs=[pl.BlockSpec(memory_space=pltpu.S...]
    all_to_all x1 -> x0, blocking collectives: 8.86 us -> none  [body(): return normalized(lax.all_to_all(parts, 'space', 0, 0, tiled=True), others)]
    all_to_all x1, starting transfers between devices: 11.8 us -> 5.36 us  [body(): samples = lax.all_to_all(sent, 'tm', 0, 0, tiled=True)]
    ppermute x15 -> x16, starting transfers between devices: 28.8 us -> 33.3 us  [the longest x7 15.9 us: body(): others[1:] = [lax.ppermute(others[d], 'tm', by_z(d)) for d in range(1, 8)]]
    all_to_all x0 -> x1, starting transfers between devices: none -> 3.36 us  [body(): parts = lax.all_to_all(bins_gram(by_bin), 'space', 0, 0, tiled=True)]
  transfers between devices with their start and end apart: 17 -> 19, of which waited for: 8 -> 10; matrix products, arithmetic and copies ran while one was open for 2% -> 2% of each run, Pallas kernels for 1% -> 14%
where the time goes in v2:
time: 248 us; the launch traced here: 245 us
  waiting for transfers between devices  145 us (58%)
  starting transfers between devices  52 us (21%)
  Pallas kernels  38.2 us (15%)
  other arithmetic  5.92 us (2%)
  local copies, waits for them, and re-layouts  3.56 us (1%)
    all_to_all x1, waiting for transfers between devices, body(): samples = lax.all_to_all(sent, 'tm', 0, 0, tiled=True)  116 us
    pallas_call x1, Pallas kernels, points_gram(): pl.pallas_call(points_kernel, in_specs=[pl.BlockSpec(memory_space=pltpu.S...  19.5 us
    ppermute x6, waiting for transfers between devices, summed_up(): lax.ppermute(held[d], axis, pairs(d))  17.6 us
    ppermute x7, starting transfers between devices, body(): others[1:] = [lax.ppermute(others[d], 'tm', by_z(d)) for d in range(1, 8)]  15.9 us
    all_to_all x1, starting transfers between devices, body(): by_bin = lax.all_to_all(coef, 'tm', 0, 0, tiled=True)  9.95 us
    pallas_call x1, Pallas kernels, turned(): pl.pallas_call(turn_kernel, grid=(cols // step,), in_specs=[pl.BlockSpec(...  9.57 us
    ppermute x6, starting transfers between devices, summed_up(): lax.ppermute(held[d], axis, pairs(d))  9.51 us
    ppermute x1, starting transfers between devices, odd_blocks(): lax.ppermute(snapshots[:HOP, first:middle], 'tm', [(t, t - 1) for t in ra...  7.74 us
  transfers between devices with their start and end apart: 19, of which 10 were waited for; matrix products, arithmetic and copies ran while one was open for 2% of the time, Pallas kernels for 14%

profile of v2, /device:TPU:2, one launch (start us, length us, event | category | flops | bytes accessed | tf_op | source)
XLA Modules:
  0.0 244.9 jit_solution(14568795529607689686)
XLA Ops:
  0.0 1.9 fusion.14
  1.9 7.7 %collective-permute-start = (f32[128,1024]{1,0:T(8,128)S(1)}, f32[128,1024]{1,0:T(8,128)S(1)}, u32[]{:S(2)}, u32[]{:S(2)}) collective-permute-start(f32[128,1024]{1,0:T(8,128)S(1)} %get-tuple-element.23), channel_id=1, source_target_pairs={{1,0},{2,1},{3,2},{4,3},{5,4},{6,5},{7,6},{8,7},{9,8},{10,9},{11,1... | collective-permute-start | bytes 1572872 | tf_op jit(solution)/shard_map/ppermute | solution.py:271
  9.8 9.6 %turn_samples.1 = f32[5632,256]{1,0:T(8,128)} custom-call(f32[256,7680]{1,0:T(8,128)} %x_ref.3, f32[1,7680]{1,0:T(1,128)S(1)} %broadcast_in_dim.2.w_ref), custom_call_target="tpu_custom_call" | custom-call | bytes 11534336 | tf_op jit(solution)/shard_map/turn_samples/pallas_call | solution.py:46
  19.4 1.4 collective-permute-done
  20.8 4.4 %collective-permute-done.1 = f32[128,1024]{1,0:T(8,128)S(1)} collective-permute-done((f32[128,1024]{1,0:T(8,128)S(1)}, f32[128,1024]{1,0:T(8,128)S(1)}, u32[]{:S(2)}, u32[]{:S(2)}) %collective-permute-start.1) | collective-permute-done | bytes 524320 | tf_op jit(solution)/shard_map/ppermute | solution.py:274
  25.3 5.4 %all-to-all-start = ((f32[32,176,256]{2,1,0:T(8,128)}), f32[32,176,256]{2,1,0:T(8,128)}, u32[]{:S(2)}, u32[]{:S(2)}) async-start(f32[32,176,256]{2,1,0:T(8,128)} %bitcast.43), calls=%async_computation | async-start | bytes 11534336 | tf_op jit(solution)/shard_map/all_to_all | solution.py:301
  32.6 1.1 slice_select_fusion.1
  33.7 1.5 maximum_maximum_fusion.odd_ref
  35.2 4.1 %coefs_by_bin.1 = f32[32,16,8,128]{3,2,1,0:T(8,128)S(1)} custom-call(f32[128,256]{1,0:T(8,128)S(1)} %reshape.156.t_ref, f32[1,7680]{1,0:T(1,128)S(1)} %broadcast_in_dim.2.w_ref, f32[256,7680]{1,0:T(8,128)} %x_ref.3, f32[256,2048]{1,0:T(8,128)} %maximum_maximum_fusion.odd_ref), custom_call_target="tpu_custom_call" | custom-call | flops 805306368 | bytes 5242880 | tf_op jit(solution)/shard_map/coefs_by_bin/pallas_call | solution.py:79
  39.3 1.4 copy-done
  40.6 116.5 %all-to-all-done.x_ref = f32[32,176,256]{2,1,0:T(8,128)} async-done(((f32[32,176,256]{2,1,0:T(8,128)}), f32[32,176,256]{2,1,0:T(8,128)}, u32[]{:S(2)}, u32[]{:S(2)}) %all-to-all-start) | async-done | bytes 5767200 | tf_op jit(solution)/shard_map/all_to_all | solution.py:301
  157.1 10.0 %all-to-all-start.1 = ((f32[32,16,8,128]{3,2,1,0:T(8,128)}), f32[32,16,8,128]{3,2,1,0:T(8,128)S(1)}, u32[]{:S(2)}, u32[]{:S(2)}) async-start(f32[32,16,8,128]{3,2,1,0:T(8,128)} %copy-done), calls=%async_computation.1 | async-start | bytes 4194304 | tf_op jit(solution)/shard_map/all_to_all | solution.py:307
  167.2 19.5 %points_gram.1 = f32[2,4,4,17,8,128]{5,4,3,2,1,0:T(8,128)S(1)} custom-call(s32[4]{0:T(128)S(1)} %pad_add_fusion.where_ref, f32[128,256]{1,0:T(8,128)S(1)} %reshape.156.t_ref, f32[32,176,256]{2,1,0:T(8,128)} %all-to-all-done.x_ref, f32[176,128]{1,0:T(8,128)S(1)} %multiply_bitcast_fusion.c_ref), custom_call_target="tpu_custom_call" | custom-call | flops 6000000000 | bytes 20000000 | tf_op jit(solution)/shard_map/points_gram/pallas_call | solution.py:172
  186.9 2.7 %collective-permute-done.2 = f32[4,4,17,8,128]{4,3,2,1,0:T(8,128)S(1)} collective-permute-done((f32[4,4,17,8,128]{4,3,2,1,0:T(8,128)S(1)}, f32[4,4,17,8,128]{4,3,2,1,0:T(8,128)S(1)}, u32[]{:S(2)}, u32[]{:S(2)}) %collective-permute-start.2) | collective-permute-done | bytes 1114144 | tf_op jit(solution)/shard_map/ppermute | solution.py:309
  189.8 3.1 %collective-permute-start.5 = (f32[4,17,8,128]{3,2,1,0:T(8,128)S(1)}, f32[4,17,8,128]{3,2,1,0:T(8,128)S(1)}, u32[]{:S(2)}, u32[]{:S(2)}) collective-permute-start(f32[4,17,8,128]{3,2,1,0:T(8,128)S(1)} %get-tuple-element.26), channel_id=1, source_target_pairs={{0,192},{32,224},{64,0},{96,32},{128,64},{160,96},{192,128},{224,1... | collective-permute-start | bytes 835592 | tf_op jit(solution)/shard_map/ppermute | solution.py:266
  194.5 10.6 %collective-permute-done.5 = f32[4,17,8,128]{3,2,1,0:T(8,128)S(1)} collective-permute-done((f32[4,17,8,128]{3,2,1,0:T(8,128)S(1)}, f32[4,17,8,128]{3,2,1,0:T(8,128)S(1)}, u32[]{:S(2)}, u32[]{:S(2)}) %collective-permute-start.5) | collective-permute-done | bytes 278560 | tf_op jit(solution)/shard_map/ppermute | solution.py:266
  205.1 3.7 %collective-permute-done.3 = f32[4,17,8,128]{3,2,1,0:T(8,128)S(1)} collective-permute-done((f32[4,17,8,128]{3,2,1,0:T(8,128)S(1)}, f32[4,17,8,128]{3,2,1,0:T(8,128)S(1)}, u32[]{:S(2)}, u32[]{:S(2)}) %collective-permute-start.3) | collective-permute-done | bytes 278560 | tf_op jit(solution)/shard_map/ppermute | solution.py:266
  209.2 2.7 %collective-permute-start.7 = (f32[17,8,128]{2,1,0:T(8,128)S(1)}, f32[17,8,128]{2,1,0:T(8,128)S(1)}, u32[]{:S(2)}, u32[]{:S(2)}) collective-permute-start(f32[17,8,128]{2,1,0:T(8,128)S(1)} %get-tuple-element.30), channel_id=1, source_target_pairs={{0,16},{1,17},{2,18},{3,19},{4,20},{5,21},{6,22},{7,23},{8,24},{9,... | collective-permute-start | bytes 208904 | tf_op jit(solution)/shard_map/ppermute | solution.py:266
  211.9 1.8 collective-permute-start.6
  214.3 1.3 collective-permute-done.7
  215.6 1.5 collective-permute-done.6
  217.1 3.3 %bins_gram.1 = f32[8,3,8,128]{3,2,1,0:T(8,128)} custom-call(f32[4096,128]{1,0:T(8,128)S(1)} %bitcast.42), custom_call_target="tpu_custom_call" | custom-call | flops 500000000 | bytes 2000000 | tf_op jit(solution)/shard_map/bins_gram/pallas_call | solution.py:211
  220.4 3.4 %all-to-all-start.2 = ((f32[8,3,8,128]{3,2,1,0:T(8,128)}), f32[8,3,8,128]{3,2,1,0:T(8,128)S(1)}, u32[]{:S(2)}, u32[]{:S(2)}) async-start(f32[8,3,8,128]{3,2,1,0:T(8,128)} %bins_gram.1), calls=%async_computation.2 | async-start | bytes 196608 | tf_op jit(solution)/shard_map/all_to_all | solution.py:314
  224.4 2.0 collective-permute-start.9
  226.4 1.9 collective-permute-start.10
  228.3 2.1 collective-permute-start.11
  230.4 3.0 %collective-permute-start.12 = (f32[3,8,128]{2,1,0:T(8,128)S(1)}, f32[3,8,128]{2,1,0:T(8,128)S(1)}, u32[]{:S(2)}, u32[]{:S(2)}) collective-permute-start(f32[3,8,128]{2,1,0:T(8,128)S(1)} %get-tuple-element.42), channel_id=1, source_target_pairs={{0,4},{1,5},{2,6},{3,7},{4,0},{5,1},{6,2},{7,3},{8,12},{9,13},{10,... | collective-permute-start | bytes 36872 | tf_op jit(solution)/shard_map/ppermute | solution.py:313
  233.4 2.0 collective-permute-start.13
  235.4 3.4 %collective-permute-start.14 = (f32[3,8,128]{2,1,0:T(8,128)S(1)}, f32[3,8,128]{2,1,0:T(8,128)S(1)}, u32[]{:S(2)}, u32[]{:S(2)}) collective-permute-start(f32[3,8,128]{2,1,0:T(8,128)S(1)} %get-tuple-element.38), channel_id=1, source_target_pairs={{0,6},{1,7},{2,0},{3,1},{4,2},{5,3},{6,4},{7,5},{8,14},{9,15},{10,... | collective-permute-start | bytes 36872 | tf_op jit(solution)/shard_map/ppermute | solution.py:313
  238.8 1.5 collective-permute-start.15
  240.3 2.2 collective-permute-done.15.refs_7_
  243.1 1.8 normalize.1
  (60 shorter events, 6.2 us)
Async XLA Ops:
  0.0 9.8 %copy-start.3 = (f32[7680]{0:T(1024)S(1)}, f32[7680]{0:T(1024)}, u32[]{:S(2)}) copy-start(f32[7680]{0:T(1024)} %param.6) | copy-start | bytes 92164
  1.9 18.9 %collective-permute-start = (f32[128,1024]{1,0:T(8,128)S(1)}, f32[128,1024]{1,0:T(8,128)S(1)}, u32[]{:S(2)}, u32[]{:S(2)}) collective-permute-start(f32[128,1024]{1,0:T(8,128)S(1)} %get-tuple-element.23), channel_id=1, source_target_pairs={{1,0},{2,1},{3,2},{4,3},{5,4},{6,5},{7,6},{8,7},{9,8},{10,9},{11,1... | collective-permute-start | bytes 1572872 | tf_op jit(solution)/shard_map/ppermute | solution.py:271
  9.7 15.6 %collective-permute-start.1 = (f32[128,1024]{1,0:T(8,128)S(1)}, f32[128,1024]{1,0:T(8,128)S(1)}, u32[]{:S(2)}, u32[]{:S(2)}) collective-permute-start(f32[128,1024]{1,0:T(8,128)S(1)} %get-tuple-element.22), channel_id=1, source_target_pairs={{0,1},{1,2},{2,3},{3,4},{4,5},{5,6},{6,7},{7,8},{8,9},{9,10},{10,1... | collective-permute-start | bytes 1572872 | tf_op jit(solution)/shard_map/ppermute | solution.py:274
  25.3 5.4 %copy-start.11 = (s32[64]{0:T(128)S(1)}, s32[64]{0:T(128)}, u32[]{:S(2)}) copy-start(s32[64]{0:T(128)} %param.7) | copy-start | bytes 772
  25.3 131.9 %all-to-all-start = ((f32[32,176,256]{2,1,0:T(8,128)}), f32[32,176,256]{2,1,0:T(8,128)}, u32[]{:S(2)}, u32[]{:S(2)}) async-start(f32[32,176,256]{2,1,0:T(8,128)} %bitcast.43), calls=%async_computation | async-start | bytes 11534336 | tf_op jit(solution)/shard_map/all_to_all | solution.py:301
  39.3 1.4 copy-start
  157.1 60.0 %all-to-all-start.1 = ((f32[32,16,8,128]{3,2,1,0:T(8,128)}), f32[32,16,8,128]{3,2,1,0:T(8,128)S(1)}, u32[]{:S(2)}, u32[]{:S(2)}) async-start(f32[32,16,8,128]{3,2,1,0:T(8,128)} %copy-done), calls=%async_computation.1 | async-start | bytes 4194304 | tf_op jit(solution)/shard_map/all_to_all | solution.py:307
  167.2 19.5 %copy-start.1 = (s32[4]{0:T(128)}, s32[4]{0:T(128)S(1)}, u32[]{:S(2)}) copy-start(s32[4]{0:T(128)S(1)} %pad_add_fusion.where_ref) | copy-start | bytes 52
  186.8 2.8 %collective-permute-start.2 = (f32[4,4,17,8,128]{4,3,2,1,0:T(8,128)S(1)}, f32[4,4,17,8,128]{4,3,2,1,0:T(8,128)S(1)}, u32[]{:S(2)}, u32[]{:S(2)}) collective-permute-start(f32[4,4,17,8,128]{4,3,2,1,0:T(8,128)S(1)} %slice_bitcast_fusion), channel_id=1, source_target_pairs={{0,32},{32,0},{64,96},{96,64},{128,160},{160,128},{192,224},{224,1... | collective-permute-start | bytes 3342344 | tf_op jit(solution)/shard_map/ppermute | solution.py:309
  189.8 15.3 %collective-permute-start.5 = (f32[4,17,8,128]{3,2,1,0:T(8,128)S(1)}, f32[4,17,8,128]{3,2,1,0:T(8,128)S(1)}, u32[]{:S(2)}, u32[]{:S(2)}) collective-permute-start(f32[4,17,8,128]{3,2,1,0:T(8,128)S(1)} %get-tuple-element.26), channel_id=1, source_target_pairs={{0,192},{32,224},{64,0},{96,32},{128,64},{160,96},{192,128},{224,1... | collective-permute-start | bytes 835592 | tf_op jit(solution)/shard_map/ppermute | solution.py:266
  192.9 12.2 %collective-permute-start.4 = (f32[4,17,8,128]{3,2,1,0:T(8,128)S(1)}, f32[4,17,8,128]{3,2,1,0:T(8,128)S(1)}, u32[]{:S(2)}, u32[]{:S(2)}) collective-permute-start(f32[4,17,8,128]{3,2,1,0:T(8,128)S(1)} %get-tuple-element.27), channel_id=1, source_target_pairs={{0,128},{32,160},{64,192},{96,224},{128,0},{160,32},{192,64},{224,... | collective-permute-start | bytes 835592 | tf_op jit(solution)/shard_map/ppermute | solution.py:266
  193.5 15.3 %collective-permute-start.3 = (f32[4,17,8,128]{3,2,1,0:T(8,128)S(1)}, f32[4,17,8,128]{3,2,1,0:T(8,128)S(1)}, u32[]{:S(2)}, u32[]{:S(2)}) collective-permute-start(f32[4,17,8,128]{3,2,1,0:T(8,128)S(1)} %get-tuple-element.25), channel_id=1, source_target_pairs={{0,64},{32,96},{64,128},{96,160},{128,192},{160,224},{192,0},{224,... | collective-permute-start | bytes 835592 | tf_op jit(solution)/shard_map/ppermute | solution.py:266
  208.9 5.4 %collective-permute-start.8 = (f32[17,8,128]{2,1,0:T(8,128)S(1)}, f32[17,8,128]{2,1,0:T(8,128)S(1)}, u32[]{:S(2)}, u32[]{:S(2)}) collective-permute-start(f32[17,8,128]{2,1,0:T(8,128)S(1)} %get-tuple-element.29), channel_id=1, source_target_pairs={{0,24},{1,25},{2,26},{3,27},{4,28},{5,29},{6,30},{7,31},{8,0},{9,1... | collective-permute-start | bytes 208904 | tf_op jit(solution)/shard_map/ppermute | solution.py:266
  209.2 6.4 %collective-permute-start.7 = (f32[17,8,128]{2,1,0:T(8,128)S(1)}, f32[17,8,128]{2,1,0:T(8,128)S(1)}, u32[]{:S(2)}, u32[]{:S(2)}) collective-permute-start(f32[17,8,128]{2,1,0:T(8,128)S(1)} %get-tuple-element.30), channel_id=1, source_target_pairs={{0,16},{1,17},{2,18},{3,19},{4,20},{5,21},{6,22},{7,23},{8,24},{9,... | collective-permute-start | bytes 208904 | tf_op jit(solution)/shard_map/ppermute | solution.py:266
  211.9 5.2 %collective-permute-start.6 = (f32[17,8,128]{2,1,0:T(8,128)S(1)}, f32[17,8,128]{2,1,0:T(8,128)S(1)}, u32[]{:S(2)}, u32[]{:S(2)}) collective-permute-start(f32[17,8,128]{2,1,0:T(8,128)S(1)} %get-tuple-element.28), channel_id=1, source_target_pairs={{0,8},{1,9},{2,10},{3,11},{4,12},{5,13},{6,14},{7,15},{8,16},{9,17... | collective-permute-start | bytes 208904 | tf_op jit(solution)/shard_map/ppermute | solution.py:266
  220.4 22.1 %all-to-all-start.2 = ((f32[8,3,8,128]{3,2,1,0:T(8,128)}), f32[8,3,8,128]{3,2,1,0:T(8,128)S(1)}, u32[]{:S(2)}, u32[]{:S(2)}) async-start(f32[8,3,8,128]{3,2,1,0:T(8,128)} %bins_gram.1), calls=%async_computation.2 | async-start | bytes 196608 | tf_op jit(solution)/shard_map/all_to_all | solution.py:314
  224.4 11.0 %collective-permute-start.9 = (f32[3,8,128]{2,1,0:T(8,128)S(1)}, f32[3,8,128]{2,1,0:T(8,128)S(1)}, u32[]{:S(2)}, u32[]{:S(2)}) collective-permute-start(f32[3,8,128]{2,1,0:T(8,128)S(1)} %get-tuple-element.39), channel_id=1, source_target_pairs={{0,1},{1,2},{2,3},{3,4},{4,5},{5,6},{6,7},{7,0},{8,9},{9,10},{10,1... | collective-permute-start | bytes 36872 | tf_op jit(solution)/shard_map/ppermute | solution.py:313
  226.4 12.4 %collective-permute-start.10 = (f32[3,8,128]{2,1,0:T(8,128)S(1)}, f32[3,8,128]{2,1,0:T(8,128)S(1)}, u32[]{:S(2)}, u32[]{:S(2)}) collective-permute-start(f32[3,8,128]{2,1,0:T(8,128)S(1)} %get-tuple-element.40), channel_id=1, source_target_pairs={{0,2},{1,3},{2,4},{3,5},{4,6},{5,7},{6,0},{7,1},{8,10},{9,11},{10,... | collective-permute-start | bytes 36872 | tf_op jit(solution)/shard_map/ppermute | solution.py:313
  228.3 12.0 %collective-permute-start.11 = (f32[3,8,128]{2,1,0:T(8,128)S(1)}, f32[3,8,128]{2,1,0:T(8,128)S(1)}, u32[]{:S(2)}, u32[]{:S(2)}) collective-permute-start(f32[3,8,128]{2,1,0:T(8,128)S(1)} %get-tuple-element.41), channel_id=1, source_target_pairs={{0,3},{1,4},{2,5},{3,6},{4,7},{5,0},{6,1},{7,2},{8,11},{9,12},{10,... | collective-permute-start | bytes 36872 | tf_op jit(solution)/shard_map/ppermute | solution.py:313
  230.4 9.9 %collective-permute-start.12 = (f32[3,8,128]{2,1,0:T(8,128)S(1)}, f32[3,8,128]{2,1,0:T(8,128)S(1)}, u32[]{:S(2)}, u32[]{:S(2)}) collective-permute-start(f32[3,8,128]{2,1,0:T(8,128)S(1)} %get-tuple-element.42), channel_id=1, source_target_pairs={{0,4},{1,5},{2,6},{3,7},{4,0},{5,1},{6,2},{7,3},{8,12},{9,13},{10,... | collective-permute-start | bytes 36872 | tf_op jit(solution)/shard_map/ppermute | solution.py:313
  233.4 6.9 %collective-permute-start.13 = (f32[3,8,128]{2,1,0:T(8,128)S(1)}, f32[3,8,128]{2,1,0:T(8,128)S(1)}, u32[]{:S(2)}, u32[]{:S(2)}) collective-permute-start(f32[3,8,128]{2,1,0:T(8,128)S(1)} %get-tuple-element.43), channel_id=1, source_target_pairs={{0,5},{1,6},{2,7},{3,0},{4,1},{5,2},{6,3},{7,4},{8,13},{9,14},{10,... | collective-permute-start | bytes 36872 | tf_op jit(solution)/shard_map/ppermute | solution.py:313
  235.4 7.1 %copy-start.4 = (f32[3,8,128]{2,1,0:T(8,128)}, f32[3,8,128]{2,1,0:T(8,128)S(1)}, u32[]{:S(2)}) copy-start(f32[3,8,128]{2,1,0:T(8,128)S(1)} %collective-permute-done.9.refs_1_) | copy-start | bytes 36868
  235.4 4.9 %collective-permute-start.14 = (f32[3,8,128]{2,1,0:T(8,128)S(1)}, f32[3,8,128]{2,1,0:T(8,128)S(1)}, u32[]{:S(2)}, u32[]{:S(2)}) collective-permute-start(f32[3,8,128]{2,1,0:T(8,128)S(1)} %get-tuple-element.38), channel_id=1, source_target_pairs={{0,6},{1,7},{2,0},{3,1},{4,2},{5,3},{6,4},{7,5},{8,14},{9,15},{10,... | collective-permute-start | bytes 36872 | tf_op jit(solution)/shard_map/ppermute | solution.py:313
  238.8 3.7 %copy-start.5 = (f32[3,8,128]{2,1,0:T(8,128)}, f32[3,8,128]{2,1,0:T(8,128)S(1)}, u32[]{:S(2)}) copy-start(f32[3,8,128]{2,1,0:T(8,128)S(1)} %collective-permute-done.10.refs_2_) | copy-start | bytes 36868
  238.8 3.7 %collective-permute-start.15 = (f32[3,8,128]{2,1,0:T(8,128)S(1)}, f32[3,8,128]{2,1,0:T(8,128)S(1)}, u32[]{:S(2)}, u32[]{:S(2)}) collective-permute-start(f32[3,8,128]{2,1,0:T(8,128)S(1)} %concatenate.43), channel_id=1, source_target_pairs={{0,7},{1,0},{2,1},{3,2},{4,3},{5,4},{6,5},{7,6},{8,15},{9,8},{10,9... | collective-permute-start | bytes 36872 | tf_op jit(solution)/shard_map/ppermute | solution.py:313
  240.3 2.2 copy-start.6
  240.3 2.3 copy-start.7
  240.3 2.2 copy-start.8
  240.3 2.2 copy-start.9
  242.5 0.6 copy-start.10
  242.5 0.6 copy-start.2

commit v3 on v2

--- a/solution.py
+++ b/solution.py
@@ -103,14 +103,38 @@
     return gram[:half] + jnp.where(lane < half, other, -other)
 
 
-def diagonal(out):
-    row = lax.broadcasted_iota(jnp.int32, out.shape, 0)
-    lane = lax.broadcasted_iota(jnp.int32, out.shape, 1)
-    return jnp.sum(jnp.where(row == lane, out, 0.0), axis=0, keepdims=True)
-
-
-def two_traces(first, second):
-    return diagonal(first) + pltpu.roll(diagonal(second), BLOCKS, 1)
+def iotas(shape):
+    return (lax.broadcasted_iota(jnp.int32, shape, 0), lax.broadcasted_iota(jnp.int32, shape, 1))
+
+
+def swapped(out):
+    return pltpu.roll(out, BLOCKS, 1)
+
+
+def packed(first, second):
+    row, lane = iotas(first.shape)
+    lower = lane % BLOCKS < row
+    return jnp.where(
+        lane < BLOCKS,
+        jnp.where(lower, swapped(first), first),
+        jnp.where(lower, second, swapped(second)),
+    )
+
+
+def unpacked(squares):
+    row, lane = iotas((BLOCKS, LANES))
+    column = lane % BLOCKS
+    mirrored = squares.T
+    outs = []
+    for b in range(2):
+        mirror = mirrored[BLOCKS * b : BLOCKS * (b + 1)]
+        mirror = jnp.concatenate([mirror, mirror], axis=1)
+        square = squares[:, BLOCKS * b : BLOCKS * (b + 1)]
+        square = jnp.concatenate([square, square], axis=1)
+        real = jnp.where(column >= row, square, mirror)
+        imag = jnp.where(column < row, square, jnp.where(column > row, -mirror, 0.0))
+        outs.append(jnp.where(lane < BLOCKS, real, imag))
+    return outs
 
 
 def points_kernel(where_ref, t_ref, x_ref, c_ref, o_ref, s_ref):
@@ -139,24 +163,17 @@
         both(t, x_ref[t + 1][:, :HOP])
     both(tm_count - 1, c_ref[...])
 
-    y, core, x_at, z_at = (where_ref[n] for n in range(4))
+    x_at, z_at = where_ref[0], where_ref[1]
 
     def owner(t):
         xr = lax.rem(t // 8 - x_at + 4, 4)
-        z = lax.rem(t, 8)
-        zr = lax.rem(z - z_at + 8, 8)
+        zr = lax.rem(lax.rem(t, 8) - z_at + 8, 8)
         outs = []
         for b in range(2):
             mine = pl.ds(pl.multiple_of(2 * BLOCKS * (2 * t + b), 2 * BLOCKS), 2 * BLOCKS)
             rows = split(jnp.concatenate([s_ref[n, mine] for n in range(tiles)], axis=1))
             outs.append(re_im(dot3(rows, rows, NT)))
-        traces = two_traces(*outs)
-        for s in range(8):
-            cr = lax.rem(s % 2 + core, 2)
-            yr = lax.rem(s // 2 - y + 4, 4)
-            for b in range(2):
-                o_ref[cr, yr, xr, 2 * zr + b] = outs[b][8 * s : 8 * s + 8]
-            o_ref[cr, yr, xr, 16, pl.ds(z, 1), :] = traces
+        o_ref[xr, zr] = packed(*outs)
 
     def four_owners(i, carry):
         for n in range(4):
@@ -173,7 +190,7 @@
         points_kernel,
         in_specs=[pl.BlockSpec(memory_space=pltpu.SMEM), vmem, vmem, vmem],
         out_specs=vmem,
-        out_shape=jax.ShapeDtypeStruct((2, 4, 4, 17, 8, LANES), F32),
+        out_shape=jax.ShapeDtypeStruct((4, 8, BLOCKS, LANES), F32),
         scratch_shapes=[pltpu.VMEM((wide // LANES, 2 * NBINS * BLOCKS, LANES), F32)],
         cost_estimate=pl.CostEstimate(
             flops=6 * 10**9, bytes_accessed=20 * 10**6, transcendentals=0
@@ -183,7 +200,8 @@
     )(where, table, samples, closing)
 
 
-def bins_kernel(a_ref, o_ref, s_ref):
+def bins_kernel(a_ref, *refs):
+    o_ref, s_ref = refs[-2:]
     tiles = s_ref.shape[0]
     tm_count = a_ref.shape[0] // (8 * tiles)
     for n in range(tiles):
@@ -193,24 +211,26 @@
                 if e == 1 and n >= tiles // 2:
                     got = pltpu.roll(got, tm_count - 1, 0)
                 s_ref.at[n][pl.ds(c * BLOCKS + e, tm_count, stride=2), :] = got
-    outs = []
+    outs = unpacked(sum([ref[...] for ref in refs[1:-2]], refs[0][...]))
+    row, lane = iotas((BLOCKS, LANES))
     for b in range(2):
         mine = pl.ds(2 * BLOCKS * b, 2 * BLOCKS)
         rows = split(jnp.concatenate([s_ref[n, mine] for n in range(tiles)], axis=1))
-        outs.append(re_im(dot3(rows, rows, NT)))
-    traces = jnp.broadcast_to(two_traces(*outs), (8, LANES))
+        outs[b] = outs[b] + re_im(dot3(rows, rows, NT))
+    traces = [jnp.sum(jnp.where(row == lane, out, 0.0), keepdims=True) for out in outs]
+    traces = jnp.where(row[:8] == 0, traces[0], traces[1])
     for s in range(8):
         for b in range(2):
             o_ref[s, b] = outs[b][8 * s : 8 * s + 8]
         o_ref[s, 2] = traces
 
 
-def bins_gram(coef):
+def bins_gram(coef, others):
     vmem = pl.BlockSpec(memory_space=pltpu.VMEM)
     tiles = coef.shape[1]
     return pl.pallas_call(
         bins_kernel,
-        in_specs=[vmem],
+        in_specs=[vmem] * (1 + len(others)),
         out_specs=vmem,
         out_shape=jax.ShapeDtypeStruct((8, 3, 8, LANES), F32),
         scratch_shapes=[pltpu.VMEM((tiles, 4 * BLOCKS, LANES), F32)],
@@ -219,39 +239,28 @@
         ),
         compiler_params=pltpu.CompilerParams(vmem_limit_bytes=VMEM_BYTES),
         name="bins_gram",
-    )(coef.reshape(-1, LANES))
-
-
-def norm_kernel(where_ref, r_ref, *refs):
-    o_ref = refs[-1]
+    )(coef.reshape(-1, LANES), *others)
+
+
+def norm_kernel(r_ref, o_ref):
     total = r_ref[0]
     for s in range(1, 8):
         total = total + r_ref[s]
-    for ref in refs[:-1]:
-        total = total + ref[...]
-    row = lax.broadcasted_iota(jnp.int32, (8, LANES), 0)
-    lane = lax.broadcasted_iota(jnp.int32, (8, LANES), 1)
     for b in range(2):
-        mine = (row == where_ref[3]) & (lane // BLOCKS == b)
-        energy = jnp.sum(jnp.where(mine, total[2], 0.0), keepdims=True)
-        out = total[b] * (BLOCKS / energy)
+        out = total[b] * (BLOCKS / total[2, b : b + 1])
         o_ref[b, 0] = out[:, :BLOCKS]
         o_ref[b, 1] = out[:, BLOCKS:]
 
 
-def normalized(where, parts, others):
+def normalized(parts):
     vmem = pl.BlockSpec(memory_space=pltpu.VMEM)
     return pl.pallas_call(
         norm_kernel,
-        in_specs=[pl.BlockSpec(memory_space=pltpu.SMEM)] + [vmem] * (1 + len(others)),
+        in_specs=[vmem],
         out_specs=vmem,
         out_shape=jax.ShapeDtypeStruct((2, 2, 8, BLOCKS), F32),
         name="normalize",
-    )(where, parts, *others)
-
-
-def by_y(d):
-    return [(2 * y + c, 2 * ((y + d) % 4) + c) for y in range(4) for c in range(2)]
+    )(parts)
 
 
 def by_x(d):
@@ -262,8 +271,8 @@
     return [(8 * x + z, 8 * x + (z + d) % 8) for x in range(4) for z in range(8)]
 
 
-def summed_up(held, axis, steps, pairs):
-    return sum([lax.ppermute(held[d], axis, pairs(d)) for d in range(1, steps)], held[0])
+def sent_on(held, steps, pairs):
+    return [held[0]] + [lax.ppermute(held[d], "tm", pairs(d)) for d in range(1, steps)]
 
 
 def odd_blocks(snapshots, closing, tm, tm_count, first):
@@ -291,8 +300,8 @@
 
 def body(snapshots, closing, weights, bin_index):
     tm_count = lax.axis_size("tm")
-    tm, space = lax.axis_index("tm"), lax.axis_index("space")
-    where = jnp.stack([space // 2, space % 2, tm // 8, tm % 8]).astype(jnp.int32)
+    tm = lax.axis_index("tm")
+    where = jnp.stack([tm // 8, tm % 8]).astype(jnp.int32)
     first = tm_count * PTS_TM
     roots = jnp.sqrt(weights)[None, :]
     down, up, finish = odd_blocks(snapshots, closing, tm, tm_count, first)
@@ -306,13 +315,9 @@
     samples, coef, own_closing = lax.optimization_barrier((samples, coef, own_closing.T))
     by_bin = lax.all_to_all(coef, "tm", 0, 0, tiled=True)
     parts = points_gram(where, table, samples, own_closing)
-    held = parts[0] + lax.ppermute(parts[1], "space", [(s, s ^ 1) for s in range(8)])
-    held = summed_up(summed_up(held, "space", 4, by_y), "tm", 4, by_x)
-    by_bin, held = lax.optimization_barrier((by_bin, held))
-    others = [jnp.concatenate([held[2 * d : 2 * d + 2], held[16:]], axis=0) for d in range(8)]
-    others[1:] = [lax.ppermute(others[d], "tm", by_z(d)) for d in range(1, 8)]
-    parts = lax.all_to_all(bins_gram(by_bin), "space", 0, 0, tiled=True)
-    return normalized(where, parts, others)
+    others = sent_on(sum(sent_on(parts, 4, by_x)), 8, by_z)
+    parts = lax.all_to_all(bins_gram(by_bin, others), "space", 0, 0, tiled=True)
+    return normalized(parts)
 
 
 def solution(mesh):

time: 248 us -> 247 us (level)
  blocking collectives: 0 us -> 10.2 us
  starting transfers between devices: 52 us -> 46.4 us
    all_to_all x0 -> x1, blocking collectives: none -> 10.2 us  [body(): parts = lax.all_to_all(bins_gram(by_bin, others), 'space', 0, 0, tiled=True)]
    all_to_all x1 -> x0, starting transfers between devices: 3.36 us -> none  [body(): parts = lax.all_to_all(bins_gram(by_bin), 'space', 0, 0, tiled=True)]
    ppermute x14 -> x10, starting transfers between devices: 25.5 us -> 23.3 us  [sent_on(): lax.ppermute(held[d], 'tm', pairs(d))]
    ppermute x14 -> x10, waiting for transfers between devices: 22.5 us -> 21.5 us  [sent_on(): lax.ppermute(held[d], 'tm', pairs(d))]
  transfers between devices with their start and end apart: 19 -> 14, of which waited for: 10 -> 7; matrix products, arithmetic and copies ran while one was open for 2% -> 2% of each run, Pallas kernels for 14% -> 13%
where the time goes in v3:
time: 247 us; the launch traced here: 246 us
  waiting for transfers between devices  144 us (58%)
  starting transfers between devices  46.4 us (19%)
  Pallas kernels  37.3 us (15%)
  blocking collectives  10.2 us (4%)
  other arithmetic  5.22 us (2%)
  local copies, waits for them, and re-layouts  2.94 us (1%)
    all_to_all x1, waiting for transfers between devices, body(): samples = lax.all_to_all(sent, 'tm', 0, 0, tiled=True)  116 us
    ppermute x10, starting transfers between devices, sent_on(): lax.ppermute(held[d], 'tm', pairs(d))  23.3 us
    ppermute x10, waiting for transfers between devices, sent_on(): lax.ppermute(held[d], 'tm', pairs(d))  21.5 us
    pallas_call x1, Pallas kernels, points_gram(): pl.pallas_call(points_kernel, in_specs=[pl.BlockSpec(memory_space=pltpu.S...  19.4 us
    all_to_all x1, blocking collectives, body(): parts = lax.all_to_all(bins_gram(by_bin, others), 'space', 0, 0, tiled=True)  10.2 us
    all_to_all x1, starting transfers between devices, body(): by_bin = lax.all_to_all(coef, 'tm', 0, 0, tiled=True)  9.95 us
    pallas_call x1, Pallas kernels, turned(): pl.pallas_call(turn_kernel, grid=(cols // step,), in_specs=[pl.BlockSpec(...  9.56 us
    ppermute x1, starting transfers between devices, odd_blocks(): lax.ppermute(snapshots[:HOP, first:middle], 'tm', [(t, t - 1) for t in ra...  7.74 us
  transfers between devices with their start and end apart: 14, of which 7 were waited for; matrix products, arithmetic and copies ran while one was open for 2% of the time, Pallas kernels for 13%

profile of v3, /device:TPU:2, one launch (start us, length us, event | category | flops | bytes accessed | tf_op | source)
XLA Modules:
  0.0 246.0 jit_solution(9794845685246823797)
XLA Ops:
  0.0 1.9 fusion.10
  1.9 7.7 %collective-permute-start = (f32[128,1024]{1,0:T(8,128)S(1)}, f32[128,1024]{1,0:T(8,128)S(1)}, u32[]{:S(2)}, u32[]{:S(2)}) collective-permute-start(f32[128,1024]{1,0:T(8,128)S(1)} %get-tuple-element.19), channel_id=1, source_target_pairs={{1,0},{2,1},{3,2},{4,3},{5,4},{6,5},{7,6},{8,7},{9,8},{10,9},{11,1... | collective-permute-start | bytes 1572872 | tf_op jit(solution)/shard_map/ppermute | solution.py:280
  9.8 9.6 %turn_samples.1 = f32[5632,256]{1,0:T(8,128)} custom-call(f32[256,7680]{1,0:T(8,128)} %x_ref.3, f32[1,7680]{1,0:T(1,128)S(1)} %broadcast_in_dim.2.w_ref), custom_call_target="tpu_custom_call" | custom-call | bytes 11534336 | tf_op jit(solution)/shard_map/turn_samples/pallas_call | solution.py:46
  19.4 1.4 collective-permute-done
  20.8 4.4 %collective-permute-done.1 = f32[128,1024]{1,0:T(8,128)S(1)} collective-permute-done((f32[128,1024]{1,0:T(8,128)S(1)}, f32[128,1024]{1,0:T(8,128)S(1)}, u32[]{:S(2)}, u32[]{:S(2)}) %collective-permute-start.1) | collective-permute-done | bytes 524320 | tf_op jit(solution)/shard_map/ppermute | solution.py:283
  25.3 5.4 %all-to-all-start = ((f32[32,176,256]{2,1,0:T(8,128)}), f32[32,176,256]{2,1,0:T(8,128)}, u32[]{:S(2)}, u32[]{:S(2)}) async-start(f32[32,176,256]{2,1,0:T(8,128)} %bitcast.37), calls=%async_computation | async-start | bytes 11534336 | tf_op jit(solution)/shard_map/all_to_all | solution.py:310
  30.7 0.3 cosine_multiply_fusion
  31.0 0.1 copy.6
  31.3 1.0 constant_dynamic-slice_fusion
  32.6 1.1 slice_select_fusion.1
  33.7 1.6 maximum_maximum_fusion.odd_ref
  35.2 4.1 %coefs_by_bin.1 = f32[32,16,8,128]{3,2,1,0:T(8,128)S(1)} custom-call(f32[128,256]{1,0:T(8,128)S(1)} %reshape.156.t_ref, f32[1,7680]{1,0:T(1,128)S(1)} %broadcast_in_dim.2.w_ref, f32[256,7680]{1,0:T(8,128)} %x_ref.3, f32[256,2048]{1,0:T(8,128)} %maximum_maximum_fusion.odd_ref), custom_call_target="tpu_custom_call" | custom-call | flops 805306368 | bytes 5242880 | tf_op jit(solution)/shard_map/coefs_by_bin/pallas_call | solution.py:79
  39.3 1.4 copy-done
  40.8 116.4 %all-to-all-done.x_ref = f32[32,176,256]{2,1,0:T(8,128)} async-done(((f32[32,176,256]{2,1,0:T(8,128)}), f32[32,176,256]{2,1,0:T(8,128)}, u32[]{:S(2)}, u32[]{:S(2)}) %all-to-all-start) | async-done | bytes 5767200 | tf_op jit(solution)/shard_map/all_to_all | solution.py:310
  157.1 9.9 %all-to-all-start.1 = ((f32[32,16,8,128]{3,2,1,0:T(8,128)}), f32[32,16,8,128]{3,2,1,0:T(8,128)S(1)}, u32[]{:S(2)}, u32[]{:S(2)}) async-start(f32[32,16,8,128]{3,2,1,0:T(8,128)} %copy-done), calls=%async_computation.1 | async-start | bytes 4194304 | tf_op jit(solution)/shard_map/all_to_all | solution.py:316
  167.2 19.4 %points_gram.1 = f32[4,8,64,128]{3,2,1,0:T(8,128)S(1)} custom-call(s32[2]{0:T(128)S(1)} %pad_add_fusion.where_ref, f32[128,256]{1,0:T(8,128)S(1)} %reshape.156.t_ref, f32[32,176,256]{2,1,0:T(8,128)} %all-to-all-done.x_ref, f32[176,128]{1,0:T(8,128)S(1)} %multiply_bitcast_fusion.c_ref), custom_call_target="tpu_custom_call" | custom-call | flops 6000000000 | bytes 20000000 | tf_op jit(solution)/shard_map/points_gram/pallas_call | solution.py:189
  186.6 0.3 collective-permute-start.4
  186.9 2.7 %collective-permute-start.3 = (f32[8,64,128]{2,1,0:T(8,128)S(1)}, f32[8,64,128]{2,1,0:T(8,128)S(1)}, u32[]{:S(2)}, u32[]{:S(2)}) collective-permute-start(f32[8,64,128]{2,1,0:T(8,128)S(1)} %get-tuple-element.23), channel_id=1, source_target_pairs={{0,16},{1,17},{2,18},{3,19},{4,20},{5,21},{6,22},{7,23},{8,24},{9,... | collective-permute-start | bytes 786440 | tf_op jit(solution)/shard_map/ppermute | solution.py:275
  189.6 1.8 collective-permute-start.2
  191.4 9.4 %collective-permute-done.4 = f32[8,64,128]{2,1,0:T(8,128)S(1)} collective-permute-done((f32[8,64,128]{2,1,0:T(8,128)S(1)}, f32[8,64,128]{2,1,0:T(8,128)S(1)}, u32[]{:S(2)}, u32[]{:S(2)}) %collective-permute-start.4) | collective-permute-done | bytes 262176 | tf_op jit(solution)/shard_map/ppermute | solution.py:275
  200.9 8.0 %collective-permute-done.3 = f32[8,64,128]{2,1,0:T(8,128)S(1)} collective-permute-done((f32[8,64,128]{2,1,0:T(8,128)S(1)}, f32[8,64,128]{2,1,0:T(8,128)S(1)}, u32[]{:S(2)}, u32[]{:S(2)}) %collective-permute-start.3) | collective-permute-done | bytes 262176 | tf_op jit(solution)/shard_map/ppermute | solution.py:275
  208.9 2.1 collective-permute-done.2
  211.1 0.3 collective-permute-start.5
  211.4 3.5 %collective-permute-start.6 = (f32[64,128]{1,0:T(8,128)S(1)}, f32[64,128]{1,0:T(8,128)S(1)}, u32[]{:S(2)}, u32[]{:S(2)}) collective-permute-start(f32[64,128]{1,0:T(8,128)S(1)} %get-tuple-element.29), channel_id=1, source_target_pairs={{0,2},{1,3},{2,4},{3,5},{4,6},{5,7},{6,0},{7,1},{8,10},{9,11},{10,... | collective-permute-start | bytes 98312 | tf_op jit(solution)/shard_map/ppermute | solution.py:275
  214.8 4.1 %collective-permute-start.7 = (f32[64,128]{1,0:T(8,128)S(1)}, f32[64,128]{1,0:T(8,128)S(1)}, u32[]{:S(2)}, u32[]{:S(2)}) collective-permute-start(f32[64,128]{1,0:T(8,128)S(1)} %get-tuple-element.28), channel_id=1, source_target_pairs={{0,3},{1,4},{2,5},{3,6},{4,7},{5,0},{6,1},{7,2},{8,11},{9,12},{10,... | collective-permute-start | bytes 98312 | tf_op jit(solution)/shard_map/ppermute | solution.py:275
  219.0 5.0 %collective-permute-start.9 = (f32[64,128]{1,0:T(8,128)S(1)}, f32[64,128]{1,0:T(8,128)S(1)}, u32[]{:S(2)}, u32[]{:S(2)}) collective-permute-start(f32[64,128]{1,0:T(8,128)S(1)} %get-tuple-element.26), channel_id=1, source_target_pairs={{0,5},{1,6},{2,7},{3,0},{4,1},{5,2},{6,3},{7,4},{8,13},{9,14},{10,... | collective-permute-start | bytes 98312 | tf_op jit(solution)/shard_map/ppermute | solution.py:275
  224.0 3.7 %collective-permute-start.10 = (f32[64,128]{1,0:T(8,128)S(1)}, f32[64,128]{1,0:T(8,128)S(1)}, u32[]{:S(2)}, u32[]{:S(2)}) collective-permute-start(f32[64,128]{1,0:T(8,128)S(1)} %get-tuple-element.25), channel_id=1, source_target_pairs={{0,6},{1,7},{2,0},{3,1},{4,2},{5,3},{6,4},{7,5},{8,14},{9,15},{10,... | collective-permute-start | bytes 98312 | tf_op jit(solution)/shard_map/ppermute | solution.py:275
  227.7 1.9 collective-permute-start.11
  229.6 2.0 collective-permute-done.11.refs_7_
  231.6 2.7 %bins_gram.1 = f32[8,3,8,128]{3,2,1,0:T(8,128)S(1)} custom-call(f32[4096,128]{1,0:T(8,128)S(1)} %bitcast.36, f32[64,128]{1,0:T(8,128)S(1)} %get-tuple-element.31.refs_0_, f32[64,128]{1,0:T(8,128)S(1)} %collective-permute-done.5.refs_1_, f32[64,128]{1,0:T(8,128)S(1)} %collective-permute-done.6.refs_2_, f32[64,128]{1,0:T(8,128)S(1)} %collective-permute-done.7.refs_3_, ...), custom_call_target="tpu_custom_call" | custom-call | flops 500000000 | bytes 2000000 | tf_op jit(solution)/shard_map/bins_gram/pallas_call | solution.py:231
  234.3 10.2 %all_to_all.15.r_ref = f32[8,3,8,128]{3,2,1,0:T(8,128)} all-to-all(f32[8,3,8,128]{3,2,1,0:T(8,128)S(1)} %bins_gram.1), channel_id=1, replica_groups=mesh['space'=8,'tm'=32] {'space'}, dimensions={0} | all-to-all | bytes 196608 | tf_op jit(solution)/shard_map/all_to_all | solution.py:319
  244.5 1.6 normalize.1
  (26 shorter events, 0.8 us)
Async XLA Ops:
  0.0 9.8 %copy-start.1 = (f32[7680]{0:T(1024)S(1)}, f32[7680]{0:T(1024)}, u32[]{:S(2)}) copy-start(f32[7680]{0:T(1024)} %param.6) | copy-start | bytes 92164
  1.9 18.9 %collective-permute-start = (f32[128,1024]{1,0:T(8,128)S(1)}, f32[128,1024]{1,0:T(8,128)S(1)}, u32[]{:S(2)}, u32[]{:S(2)}) collective-permute-start(f32[128,1024]{1,0:T(8,128)S(1)} %get-tuple-element.19), channel_id=1, source_target_pairs={{1,0},{2,1},{3,2},{4,3},{5,4},{6,5},{7,6},{8,7},{9,8},{10,9},{11,1... | collective-permute-start | bytes 1572872 | tf_op jit(solution)/shard_map/ppermute | solution.py:280
  9.7 15.6 %collective-permute-start.1 = (f32[128,1024]{1,0:T(8,128)S(1)}, f32[128,1024]{1,0:T(8,128)S(1)}, u32[]{:S(2)}, u32[]{:S(2)}) collective-permute-start(f32[128,1024]{1,0:T(8,128)S(1)} %get-tuple-element.18), channel_id=1, source_target_pairs={{0,1},{1,2},{2,3},{3,4},{4,5},{5,6},{6,7},{7,8},{8,9},{9,10},{10,1... | collective-permute-start | bytes 1572872 | tf_op jit(solution)/shard_map/ppermute | solution.py:283
  25.3 5.4 %copy-start.2 = (s32[64]{0:T(128)S(1)}, s32[64]{0:T(128)}, u32[]{:S(2)}) copy-start(s32[64]{0:T(128)} %param.7) | copy-start | bytes 772
  25.3 131.9 %all-to-all-start = ((f32[32,176,256]{2,1,0:T(8,128)}), f32[32,176,256]{2,1,0:T(8,128)}, u32[]{:S(2)}, u32[]{:S(2)}) async-start(f32[32,176,256]{2,1,0:T(8,128)} %bitcast.37), calls=%async_computation | async-start | bytes 11534336 | tf_op jit(solution)/shard_map/all_to_all | solution.py:310
  39.3 1.4 copy-start
  157.1 74.5 %all-to-all-start.1 = ((f32[32,16,8,128]{3,2,1,0:T(8,128)}), f32[32,16,8,128]{3,2,1,0:T(8,128)S(1)}, u32[]{:S(2)}, u32[]{:S(2)}) async-start(f32[32,16,8,128]{3,2,1,0:T(8,128)} %copy-done), calls=%async_computation.1 | async-start | bytes 4194304 | tf_op jit(solution)/shard_map/all_to_all | solution.py:316
  186.6 14.2 %collective-permute-start.4 = (f32[8,64,128]{2,1,0:T(8,128)S(1)}, f32[8,64,128]{2,1,0:T(8,128)S(1)}, u32[]{:S(2)}, u32[]{:S(2)}) collective-permute-start(f32[8,64,128]{2,1,0:T(8,128)S(1)} %get-tuple-element.22), channel_id=1, source_target_pairs={{0,24},{1,25},{2,26},{3,27},{4,28},{5,29},{6,30},{7,31},{8,0},{9,1... | collective-permute-start | bytes 786440 | tf_op jit(solution)/shard_map/ppermute | solution.py:275
  186.9 22.0 %collective-permute-start.3 = (f32[8,64,128]{2,1,0:T(8,128)S(1)}, f32[8,64,128]{2,1,0:T(8,128)S(1)}, u32[]{:S(2)}, u32[]{:S(2)}) collective-permute-start(f32[8,64,128]{2,1,0:T(8,128)S(1)} %get-tuple-element.23), channel_id=1, source_target_pairs={{0,16},{1,17},{2,18},{3,19},{4,20},{5,21},{6,22},{7,23},{8,24},{9,... | collective-permute-start | bytes 786440 | tf_op jit(solution)/shard_map/ppermute | solution.py:275
  189.6 21.4 %collective-permute-start.2 = (f32[8,64,128]{2,1,0:T(8,128)S(1)}, f32[8,64,128]{2,1,0:T(8,128)S(1)}, u32[]{:S(2)}, u32[]{:S(2)}) collective-permute-start(f32[8,64,128]{2,1,0:T(8,128)S(1)} %get-tuple-element.21), channel_id=1, source_target_pairs={{0,8},{1,9},{2,10},{3,11},{4,12},{5,13},{6,14},{7,15},{8,16},{9,17... | collective-permute-start | bytes 786440 | tf_op jit(solution)/shard_map/ppermute | solution.py:275
  211.1 12.9 %collective-permute-start.5 = (f32[64,128]{1,0:T(8,128)S(1)}, f32[64,128]{1,0:T(8,128)S(1)}, u32[]{:S(2)}, u32[]{:S(2)}) collective-permute-start(f32[64,128]{1,0:T(8,128)S(1)} %get-tuple-element.30), channel_id=1, source_target_pairs={{0,1},{1,2},{2,3},{3,4},{4,5},{5,6},{6,7},{7,0},{8,9},{9,10},{10,1... | collective-permute-start | bytes 98312 | tf_op jit(solution)/shard_map/ppermute | solution.py:275
  211.4 16.3 %collective-permute-start.6 = (f32[64,128]{1,0:T(8,128)S(1)}, f32[64,128]{1,0:T(8,128)S(1)}, u32[]{:S(2)}, u32[]{:S(2)}) collective-permute-start(f32[64,128]{1,0:T(8,128)S(1)} %get-tuple-element.29), channel_id=1, source_target_pairs={{0,2},{1,3},{2,4},{3,5},{4,6},{5,7},{6,0},{7,1},{8,10},{9,11},{10,... | collective-permute-start | bytes 98312 | tf_op jit(solution)/shard_map/ppermute | solution.py:275
  214.8 14.7 %collective-permute-start.7 = (f32[64,128]{1,0:T(8,128)S(1)}, f32[64,128]{1,0:T(8,128)S(1)}, u32[]{:S(2)}, u32[]{:S(2)}) collective-permute-start(f32[64,128]{1,0:T(8,128)S(1)} %get-tuple-element.28), channel_id=1, source_target_pairs={{0,3},{1,4},{2,5},{3,6},{4,7},{5,0},{6,1},{7,2},{8,11},{9,12},{10,... | collective-permute-start | bytes 98312 | tf_op jit(solution)/shard_map/ppermute | solution.py:275
  218.9 10.6 %collective-permute-start.8 = (f32[64,128]{1,0:T(8,128)S(1)}, f32[64,128]{1,0:T(8,128)S(1)}, u32[]{:S(2)}, u32[]{:S(2)}) collective-permute-start(f32[64,128]{1,0:T(8,128)S(1)} %get-tuple-element.27), channel_id=1, source_target_pairs={{0,4},{1,5},{2,6},{3,7},{4,0},{5,1},{6,2},{7,3},{8,12},{9,13},{10,... | collective-permute-start | bytes 98312 | tf_op jit(solution)/shard_map/ppermute | solution.py:275
  219.0 10.6 %collective-permute-start.9 = (f32[64,128]{1,0:T(8,128)S(1)}, f32[64,128]{1,0:T(8,128)S(1)}, u32[]{:S(2)}, u32[]{:S(2)}) collective-permute-start(f32[64,128]{1,0:T(8,128)S(1)} %get-tuple-element.26), channel_id=1, source_target_pairs={{0,5},{1,6},{2,7},{3,0},{4,1},{5,2},{6,3},{7,4},{8,13},{9,14},{10,... | collective-permute-start | bytes 98312 | tf_op jit(solution)/shard_map/ppermute | solution.py:275
  224.0 5.6 %collective-permute-start.10 = (f32[64,128]{1,0:T(8,128)S(1)}, f32[64,128]{1,0:T(8,128)S(1)}, u32[]{:S(2)}, u32[]{:S(2)}) collective-permute-start(f32[64,128]{1,0:T(8,128)S(1)} %get-tuple-element.25), channel_id=1, source_target_pairs={{0,6},{1,7},{2,0},{3,1},{4,2},{5,3},{6,4},{7,5},{8,14},{9,15},{10,... | collective-permute-start | bytes 98312 | tf_op jit(solution)/shard_map/ppermute | solution.py:275
  227.7 3.9 %collective-permute-start.11 = (f32[64,128]{1,0:T(8,128)S(1)}, f32[64,128]{1,0:T(8,128)S(1)}, u32[]{:S(2)}, u32[]{:S(2)}) collective-permute-start(f32[64,128]{1,0:T(8,128)S(1)} %get-tuple-element.24), channel_id=1, source_target_pairs={{0,7},{1,0},{2,1},{3,2},{4,3},{5,4},{6,5},{7,6},{8,15},{9,8},{10,9... | collective-permute-start | bytes 98312 | tf_op jit(solution)/shard_map/ppermute | solution.py:275

commit v4 on v3

--- a/solution.py
+++ b/solution.py
@@ -1,3 +1,5 @@
+import math
+
 import jax
 import jax.numpy as jnp
 from jax import lax
@@ -10,7 +12,7 @@
 HOP = NFFT // 2
 BLOCKS = 64
 LANES = 128
-PTS_TM = 176
+PTS_TM = 152
 F32, BF16 = jnp.float32, jnp.bfloat16
 VMEM_BYTES = 50 * 2**20
 
@@ -37,12 +39,16 @@
     return paired.reshape(2 * bin_index.shape[0], length)
 
 
+def widest(cols):
+    return max(n * LANES for n in range(1, 7) if cols % (n * LANES) == 0)
+
+
 def turn_kernel(x_ref, w_ref, o_ref):
     o_ref[...] = (x_ref[...] * w_ref[...]).T
 
 
 def turned(x, roots, cols):
-    rows, step = x.shape[0], 512
+    rows, step = x.shape[0], widest(cols)
     return pl.pallas_call(
         turn_kernel,
         grid=(cols // step,),
@@ -75,7 +81,7 @@
 
 def coefs(table, roots, x, odd, first):
     rows, cols = x.shape[0], x.shape[1] - first
-    step = 512
+    step = widest(math.gcd(first, cols))
     return pl.pallas_call(
         coef_kernel,
         grid=(cols // step,),

time: 247 us -> 244 us (0.988)
  waiting for transfers between devices: 144 us -> 131 us
  Pallas kernels: 37.3 us -> 44.2 us
    all_to_all x1, waiting for transfers between devices: 116 us -> 93 us  [body(): samples = lax.all_to_all(sent, 'tm', 0, 0, tiled=True)]
    ppermute x10, waiting for transfers between devices: 21.5 us -> 30.7 us  [sent_on(): lax.ppermute(held[d], 'tm', pairs(d))]
    pallas_call x1, Pallas kernels: 4.07 us -> 8.43 us  [coefs(): pl.pallas_call(coef_kernel, grid=(cols // step,), in_specs=[pl.BlockSpec(...]
    pallas_call x1, Pallas kernels: 9.56 us -> 12.8 us  [turned(): pl.pallas_call(turn_kernel, grid=(cols // step,), in_specs=[pl.BlockSpec(...]
  transfers between devices with their start and end apart: 14 -> 14, of which waited for: 7 -> 9; matrix products, arithmetic and copies ran while one was open for 2% -> 3% of each run, Pallas kernels for 13% -> 16%
where the time goes in v4:
time: 244 us; the launch traced here: 242 us
  waiting for transfers between devices  131 us (54%)
  starting transfers between devices  46 us (19%)
  Pallas kernels  44.2 us (18%)
  blocking collectives  10.2 us (4%)
  other arithmetic  7.16 us (3%)
  local copies, waits for them, and re-layouts  4.01 us (2%)
    all_to_all x1, waiting for transfers between devices, body(): samples = lax.all_to_all(sent, 'tm', 0, 0, tiled=True)  93 us
    ppermute x10, waiting for transfers between devices, sent_on(): lax.ppermute(held[d], 'tm', pairs(d))  30.7 us
    ppermute x10, starting transfers between devices, sent_on(): lax.ppermute(held[d], 'tm', pairs(d))  23.3 us
    pallas_call x1, Pallas kernels, points_gram(): pl.pallas_call(points_kernel, in_specs=[pl.BlockSpec(memory_space=pltpu.S...  18.8 us
    pallas_call x1, Pallas kernels, turned(): pl.pallas_call(turn_kernel, grid=(cols // step,), in_specs=[pl.BlockSpec(...  12.8 us
    all_to_all x1, blocking collectives, body(): parts = lax.all_to_all(bins_gram(by_bin, others), 'space', 0, 0, tiled=True)  10.2 us
    all_to_all x1, starting transfers between devices, body(): by_bin = lax.all_to_all(coef, 'tm', 0, 0, tiled=True)  9.21 us
    pallas_call x1, Pallas kernels, coefs(): pl.pallas_call(coef_kernel, grid=(cols // step,), in_specs=[pl.BlockSpec(...  8.43 us
  transfers between devices with their start and end apart: 14, of which 9 were waited for; matrix products, arithmetic and copies ran while one was open for 3% of the time, Pallas kernels for 16%

profile of v4, /device:TPU:2, one launch (start us, length us, event | category | flops | bytes accessed | tf_op | source)
XLA Modules:
  0.0 242.4 jit_solution(6371934757579937413)
XLA Ops:
  0.0 2.2 fusion.10
  2.2 7.7 %collective-permute-start = (f32[128,1408]{1,0:T(8,128)S(1)}, f32[128,1408]{1,0:T(8,128)S(1)}, u32[]{:S(2)}, u32[]{:S(2)}) collective-permute-start(f32[128,1408]{1,0:T(8,128)S(1)} %get-tuple-element.19), channel_id=1, source_target_pairs={{1,0},{2,1},{3,2},{4,3},{5,4},{6,5},{7,6},{8,7},{9,8},{10,9},{11,1... | collective-permute-start | bytes 2162696 | tf_op jit(solution)/shard_map/ppermute | solution.py:286
  10.1 12.8 %turn_samples.1 = f32[4864,256]{1,0:T(8,128)} custom-call(f32[256,7680]{1,0:T(8,128)} %x_ref.3, f32[1,7680]{1,0:T(1,128)S(1)} %broadcast_in_dim.2.w_ref), custom_call_target="tpu_custom_call" | custom-call | bytes 9961472 | tf_op jit(solution)/shard_map/turn_samples/pallas_call | solution.py:52
  22.9 2.5 %collective-permute-done = f32[128,1408]{1,0:T(8,128)S(1)} collective-permute-done((f32[128,1408]{1,0:T(8,128)S(1)}, f32[128,1408]{1,0:T(8,128)S(1)}, u32[]{:S(2)}, u32[]{:S(2)}) %collective-permute-start) | collective-permute-done | bytes 720928 | tf_op jit(solution)/shard_map/ppermute | solution.py:286
  25.3 4.4 %collective-permute-done.1 = f32[128,1408]{1,0:T(8,128)S(1)} collective-permute-done((f32[128,1408]{1,0:T(8,128)S(1)}, f32[128,1408]{1,0:T(8,128)S(1)}, u32[]{:S(2)}, u32[]{:S(2)}) %collective-permute-start.1) | collective-permute-done | bytes 720928 | tf_op jit(solution)/shard_map/ppermute | solution.py:289
  29.8 0.9 copy-done.2
  30.6 5.7 %all-to-all-start = ((f32[32,152,256]{2,1,0:T(8,128)}), f32[32,152,256]{2,1,0:T(8,128)}, u32[]{:S(2)}, u32[]{:S(2)}) async-start(f32[32,152,256]{2,1,0:T(8,128)} %bitcast.37), calls=%async_computation | async-start | bytes 9961472 | tf_op jit(solution)/shard_map/all_to_all | solution.py:316
  37.1 1.0 constant_dynamic-slice_fusion
  38.3 1.4 slice_select_fusion.1
  39.7 2.9 %maximum_maximum_fusion.odd_ref = f32[256,2816]{1,0:T(8,128)} fusion(f32[128,1408]{1,0:T(8,128)S(1)} %get-tuple-element.20, f32[128,1408]{1,0:T(8,128)} %copy-done.2, f32[128,1408]{1,0:T(8,128)S(1)} %slice_select_fusion.1, f32[128,1408]{1,0:T(8,128)S(1)} %get-tuple-element.17), kind=kLoop, calls=%fused_computation | loop fusion | flops 2162688 | bytes 5767168 | tf_op jit(solution)/shard_map/concatenate | solution.py:296
  42.6 8.4 %coefs_by_bin.1 = f32[32,22,8,128]{3,2,1,0:T(8,128)S(1)} custom-call(f32[128,256]{1,0:T(8,128)S(1)} %reshape.156.t_ref, f32[1,7680]{1,0:T(1,128)S(1)} %broadcast_in_dim.2.w_ref, f32[256,7680]{1,0:T(8,128)} %x_ref.3, f32[256,2816]{1,0:T(8,128)} %maximum_maximum_fusion.odd_ref), custom_call_target="tpu_custom_call" | custom-call | flops 1107296256 | bytes 7208960 | tf_op jit(solution)/shard_map/coefs_by_bin/pallas_call | solution.py:85
  51.1 1.6 copy-done
  52.7 93.0 %all-to-all-done.x_ref = f32[32,152,256]{2,1,0:T(8,128)} async-done(((f32[32,152,256]{2,1,0:T(8,128)}), f32[32,152,256]{2,1,0:T(8,128)}, u32[]{:S(2)}, u32[]{:S(2)}) %all-to-all-start) | async-done | bytes 4980768 | tf_op jit(solution)/shard_map/all_to_all | solution.py:316
  145.7 9.2 %all-to-all-start.1 = ((f32[32,22,8,128]{3,2,1,0:T(8,128)}), f32[32,22,8,128]{3,2,1,0:T(8,128)S(1)}, u32[]{:S(2)}, u32[]{:S(2)}) async-start(f32[32,22,8,128]{3,2,1,0:T(8,128)} %copy-done), calls=%async_computation.1 | async-start | bytes 5767168 | tf_op jit(solution)/shard_map/all_to_all | solution.py:322
  155.0 18.8 %points_gram.1 = f32[4,8,64,128]{3,2,1,0:T(8,128)S(1)} custom-call(s32[2]{0:T(128)S(1)} %pad_add_fusion.where_ref, f32[128,256]{1,0:T(8,128)S(1)} %reshape.156.t_ref, f32[32,152,256]{2,1,0:T(8,128)} %all-to-all-done.x_ref, f32[152,128]{1,0:T(8,128)S(1)} %multiply_bitcast_fusion.c_ref), custom_call_target="tpu_custom_call" | custom-call | flops 6000000000 | bytes 20000000 | tf_op jit(solution)/shard_map/points_gram/pallas_call | solution.py:195
  174.2 2.7 %collective-permute-start.3 = (f32[8,64,128]{2,1,0:T(8,128)S(1)}, f32[8,64,128]{2,1,0:T(8,128)S(1)}, u32[]{:S(2)}, u32[]{:S(2)}) collective-permute-start(f32[8,64,128]{2,1,0:T(8,128)S(1)} %get-tuple-element.23), channel_id=1, source_target_pairs={{0,16},{1,17},{2,18},{3,19},{4,20},{5,21},{6,22},{7,23},{8,24},{9,... | collective-permute-start | bytes 786440 | tf_op jit(solution)/shard_map/ppermute | solution.py:281
  176.9 1.8 collective-permute-start.2
  178.7 7.2 %collective-permute-done.4 = f32[8,64,128]{2,1,0:T(8,128)S(1)} collective-permute-done((f32[8,64,128]{2,1,0:T(8,128)S(1)}, f32[8,64,128]{2,1,0:T(8,128)S(1)}, u32[]{:S(2)}, u32[]{:S(2)}) %collective-permute-start.4) | collective-permute-done | bytes 262176 | tf_op jit(solution)/shard_map/ppermute | solution.py:281
  185.9 12.8 %collective-permute-done.3 = f32[8,64,128]{2,1,0:T(8,128)S(1)} collective-permute-done((f32[8,64,128]{2,1,0:T(8,128)S(1)}, f32[8,64,128]{2,1,0:T(8,128)S(1)}, u32[]{:S(2)}, u32[]{:S(2)}) %collective-permute-start.3) | collective-permute-done | bytes 262176 | tf_op jit(solution)/shard_map/ppermute | solution.py:281
  198.8 5.7 %collective-permute-start.5 = (f32[64,128]{1,0:T(8,128)S(1)}, f32[64,128]{1,0:T(8,128)S(1)}, u32[]{:S(2)}, u32[]{:S(2)}) collective-permute-start(f32[64,128]{1,0:T(8,128)S(1)} %get-tuple-element.30), channel_id=1, source_target_pairs={{0,1},{1,2},{2,3},{3,4},{4,5},{5,6},{6,7},{7,0},{8,9},{9,10},{10,1... | collective-permute-start | bytes 98312 | tf_op jit(solution)/shard_map/ppermute | solution.py:281
  204.5 0.6 collective-permute-start.6
  205.1 3.1 %collective-permute-start.7 = (f32[64,128]{1,0:T(8,128)S(1)}, f32[64,128]{1,0:T(8,128)S(1)}, u32[]{:S(2)}, u32[]{:S(2)}) collective-permute-start(f32[64,128]{1,0:T(8,128)S(1)} %get-tuple-element.28), channel_id=1, source_target_pairs={{0,3},{1,4},{2,5},{3,6},{4,7},{5,0},{6,1},{7,2},{8,11},{9,12},{10,... | collective-permute-start | bytes 98312 | tf_op jit(solution)/shard_map/ppermute | solution.py:281
  208.1 2.4 collective-permute-start.8
  210.5 3.6 %collective-permute-start.9 = (f32[64,128]{1,0:T(8,128)S(1)}, f32[64,128]{1,0:T(8,128)S(1)}, u32[]{:S(2)}, u32[]{:S(2)}) collective-permute-start(f32[64,128]{1,0:T(8,128)S(1)} %get-tuple-element.26), channel_id=1, source_target_pairs={{0,5},{1,6},{2,7},{3,0},{4,1},{5,2},{6,3},{7,4},{8,13},{9,14},{10,... | collective-permute-start | bytes 98312 | tf_op jit(solution)/shard_map/ppermute | solution.py:281
  214.1 7.3 %collective-permute-done.5.refs_1_ = f32[64,128]{1,0:T(8,128)S(1)} collective-permute-done((f32[64,128]{1,0:T(8,128)S(1)}, f32[64,128]{1,0:T(8,128)S(1)}, u32[]{:S(2)}, u32[]{:S(2)}) %collective-permute-start.5) | collective-permute-done | bytes 32800 | tf_op jit(solution)/shard_map/ppermute | solution.py:281
  221.3 2.3 collective-permute-start.10
  224.0 0.9 collective-permute-start.11
  225.0 1.6 collective-permute-done.8.refs_4_
  226.6 1.4 collective-permute-done.11.refs_7_
  227.9 2.7 %bins_gram.1 = f32[8,3,8,128]{3,2,1,0:T(8,128)S(1)} custom-call(f32[5632,128]{1,0:T(8,128)S(1)} %bitcast.36, f32[64,128]{1,0:T(8,128)S(1)} %get-tuple-element.31.refs_0_, f32[64,128]{1,0:T(8,128)S(1)} %collective-permute-done.5.refs_1_, f32[64,128]{1,0:T(8,128)S(1)} %collective-permute-done.6.refs_2_, f32[64,128]{1,0:T(8,128)S(1)} %collective-permute-done.7.refs_3_, ...), custom_call_target="tpu_custom_call" | custom-call | flops 500000000 | bytes 2000000 | tf_op jit(solution)/shard_map/bins_gram/pallas_call | solution.py:237
  230.6 10.2 %all_to_all.15.r_ref = f32[8,3,8,128]{3,2,1,0:T(8,128)} all-to-all(f32[8,3,8,128]{3,2,1,0:T(8,128)S(1)} %bins_gram.1), channel_id=1, replica_groups=mesh['space'=8,'tm'=32] {'space'}, dimensions={0} | all-to-all | bytes 196608 | tf_op jit(solution)/shard_map/all_to_all | solution.py:325
  240.8 1.6 normalize.1
  (30 shorter events, 1.9 us)
Async XLA Ops:
  0.0 10.1 %copy-start.3 = (f32[7680]{0:T(1024)S(1)}, f32[7680]{0:T(1024)}, u32[]{:S(2)}) copy-start(f32[7680]{0:T(1024)} %param.6) | copy-start | bytes 92164
  2.2 23.1 %collective-permute-start = (f32[128,1408]{1,0:T(8,128)S(1)}, f32[128,1408]{1,0:T(8,128)S(1)}, u32[]{:S(2)}, u32[]{:S(2)}) collective-permute-start(f32[128,1408]{1,0:T(8,128)S(1)} %get-tuple-element.19), channel_id=1, source_target_pairs={{1,0},{2,1},{3,2},{4,3},{5,4},{6,5},{7,6},{8,7},{9,8},{10,9},{11,1... | collective-permute-start | bytes 2162696 | tf_op jit(solution)/shard_map/ppermute | solution.py:286
  10.0 19.8 %collective-permute-start.1 = (f32[128,1408]{1,0:T(8,128)S(1)}, f32[128,1408]{1,0:T(8,128)S(1)}, u32[]{:S(2)}, u32[]{:S(2)}) collective-permute-start(f32[128,1408]{1,0:T(8,128)S(1)} %get-tuple-element.18), channel_id=1, source_target_pairs={{0,1},{1,2},{2,3},{3,4},{4,5},{5,6},{6,7},{7,8},{8,9},{9,10},{10,1... | collective-permute-start | bytes 2162696 | tf_op jit(solution)/shard_map/ppermute | solution.py:289
  25.3 4.4 %copy-start.1 = (f32[128,1408]{1,0:T(8,128)}, f32[128,1408]{1,0:T(8,128)S(1)}, u32[]{:S(2)}) copy-start(f32[128,1408]{1,0:T(8,128)S(1)} %collective-permute-done) | copy-start | bytes 2162692
  29.8 0.9 copy-start.2
  30.6 5.8 %copy-start.4 = (s32[64]{0:T(128)S(1)}, s32[64]{0:T(128)}, u32[]{:S(2)}) copy-start(s32[64]{0:T(128)} %param.7) | copy-start | bytes 772
  30.6 115.1 %all-to-all-start = ((f32[32,152,256]{2,1,0:T(8,128)}), f32[32,152,256]{2,1,0:T(8,128)}, u32[]{:S(2)}, u32[]{:S(2)}) async-start(f32[32,152,256]{2,1,0:T(8,128)} %bitcast.37), calls=%async_computation | async-start | bytes 9961472 | tf_op jit(solution)/shard_map/all_to_all | solution.py:316
  51.1 1.6 copy-start
  145.7 82.2 %all-to-all-start.1 = ((f32[32,22,8,128]{3,2,1,0:T(8,128)}), f32[32,22,8,128]{3,2,1,0:T(8,128)S(1)}, u32[]{:S(2)}, u32[]{:S(2)}) async-start(f32[32,22,8,128]{3,2,1,0:T(8,128)} %copy-done), calls=%async_computation.1 | async-start | bytes 5767168 | tf_op jit(solution)/shard_map/all_to_all | solution.py:322
  173.9 12.0 %collective-permute-start.4 = (f32[8,64,128]{2,1,0:T(8,128)S(1)}, f32[8,64,128]{2,1,0:T(8,128)S(1)}, u32[]{:S(2)}, u32[]{:S(2)}) collective-permute-start(f32[8,64,128]{2,1,0:T(8,128)S(1)} %get-tuple-element.22), channel_id=1, source_target_pairs={{0,24},{1,25},{2,26},{3,27},{4,28},{5,29},{6,30},{7,31},{8,0},{9,1... | collective-permute-start | bytes 786440 | tf_op jit(solution)/shard_map/ppermute | solution.py:281
  174.2 24.5 %collective-permute-start.3 = (f32[8,64,128]{2,1,0:T(8,128)S(1)}, f32[8,64,128]{2,1,0:T(8,128)S(1)}, u32[]{:S(2)}, u32[]{:S(2)}) collective-permute-start(f32[8,64,128]{2,1,0:T(8,128)S(1)} %get-tuple-element.23), channel_id=1, source_target_pairs={{0,16},{1,17},{2,18},{3,19},{4,20},{5,21},{6,22},{7,23},{8,24},{9,... | collective-permute-start | bytes 786440 | tf_op jit(solution)/shard_map/ppermute | solution.py:281
  176.9 21.8 %collective-permute-start.2 = (f32[8,64,128]{2,1,0:T(8,128)S(1)}, f32[8,64,128]{2,1,0:T(8,128)S(1)}, u32[]{:S(2)}, u32[]{:S(2)}) collective-permute-start(f32[8,64,128]{2,1,0:T(8,128)S(1)} %get-tuple-element.21), channel_id=1, source_target_pairs={{0,8},{1,9},{2,10},{3,11},{4,12},{5,13},{6,14},{7,15},{8,16},{9,17... | collective-permute-start | bytes 786440 | tf_op jit(solution)/shard_map/ppermute | solution.py:281
  198.8 22.5 %collective-permute-start.5 = (f32[64,128]{1,0:T(8,128)S(1)}, f32[64,128]{1,0:T(8,128)S(1)}, u32[]{:S(2)}, u32[]{:S(2)}) collective-permute-start(f32[64,128]{1,0:T(8,128)S(1)} %get-tuple-element.30), channel_id=1, source_target_pairs={{0,1},{1,2},{2,3},{3,4},{4,5},{5,6},{6,7},{7,0},{8,9},{9,10},{10,1... | collective-permute-start | bytes 98312 | tf_op jit(solution)/shard_map/ppermute | solution.py:281
  204.5 19.5 %collective-permute-start.6 = (f32[64,128]{1,0:T(8,128)S(1)}, f32[64,128]{1,0:T(8,128)S(1)}, u32[]{:S(2)}, u32[]{:S(2)}) collective-permute-start(f32[64,128]{1,0:T(8,128)S(1)} %get-tuple-element.29), channel_id=1, source_target_pairs={{0,2},{1,3},{2,4},{3,5},{4,6},{5,7},{6,0},{7,1},{8,10},{9,11},{10,... | collective-permute-start | bytes 98312 | tf_op jit(solution)/shard_map/ppermute | solution.py:281
  205.1 19.9 %collective-permute-start.7 = (f32[64,128]{1,0:T(8,128)S(1)}, f32[64,128]{1,0:T(8,128)S(1)}, u32[]{:S(2)}, u32[]{:S(2)}) collective-permute-start(f32[64,128]{1,0:T(8,128)S(1)} %get-tuple-element.28), channel_id=1, source_target_pairs={{0,3},{1,4},{2,5},{3,6},{4,7},{5,0},{6,1},{7,2},{8,11},{9,12},{10,... | collective-permute-start | bytes 98312 | tf_op jit(solution)/shard_map/ppermute | solution.py:281
  208.1 18.4 %collective-permute-start.8 = (f32[64,128]{1,0:T(8,128)S(1)}, f32[64,128]{1,0:T(8,128)S(1)}, u32[]{:S(2)}, u32[]{:S(2)}) collective-permute-start(f32[64,128]{1,0:T(8,128)S(1)} %get-tuple-element.27), channel_id=1, source_target_pairs={{0,4},{1,5},{2,6},{3,7},{4,0},{5,1},{6,2},{7,3},{8,12},{9,13},{10,... | collective-permute-start | bytes 98312 | tf_op jit(solution)/shard_map/ppermute | solution.py:281
  210.5 16.1 %collective-permute-start.9 = (f32[64,128]{1,0:T(8,128)S(1)}, f32[64,128]{1,0:T(8,128)S(1)}, u32[]{:S(2)}, u32[]{:S(2)}) collective-permute-start(f32[64,128]{1,0:T(8,128)S(1)} %get-tuple-element.26), channel_id=1, source_target_pairs={{0,5},{1,6},{2,7},{3,0},{4,1},{5,2},{6,3},{7,4},{8,13},{9,14},{10,... | collective-permute-start | bytes 98312 | tf_op jit(solution)/shard_map/ppermute | solution.py:281
  221.3 5.2 %collective-permute-start.10 = (f32[64,128]{1,0:T(8,128)S(1)}, f32[64,128]{1,0:T(8,128)S(1)}, u32[]{:S(2)}, u32[]{:S(2)}) collective-permute-start(f32[64,128]{1,0:T(8,128)S(1)} %get-tuple-element.25), channel_id=1, source_target_pairs={{0,6},{1,7},{2,0},{3,1},{4,2},{5,3},{6,4},{7,5},{8,14},{9,15},{10,... | collective-permute-start | bytes 98312 | tf_op jit(solution)/shard_map/ppermute | solution.py:281
  224.0 3.9 %collective-permute-start.11 = (f32[64,128]{1,0:T(8,128)S(1)}, f32[64,128]{1,0:T(8,128)S(1)}, u32[]{:S(2)}, u32[]{:S(2)}) collective-permute-start(f32[64,128]{1,0:T(8,128)S(1)} %get-tuple-element.24), channel_id=1, source_target_pairs={{0,7},{1,0},{2,1},{3,2},{4,3},{5,4},{6,5},{7,6},{8,15},{9,8},{10,9... | collective-permute-start | bytes 98312 | tf_op jit(solution)/shard_map/ppermute | solution.py:281

commit v5 on v2

--- a/solution.py
+++ b/solution.py
@@ -1,3 +1,5 @@
+import math
+
 import jax
 import jax.numpy as jnp
 from jax import lax
@@ -10,7 +12,7 @@
 HOP = NFFT // 2
 BLOCKS = 64
 LANES = 128
-PTS_TM = 176
+PTS_TM = 168
 F32, BF16 = jnp.float32, jnp.bfloat16
 VMEM_BYTES = 50 * 2**20
 
@@ -37,12 +39,16 @@
     return paired.reshape(2 * bin_index.shape[0], length)
 
 
+def widest(cols):
+    return max(n * LANES for n in range(1, 7) if cols % (n * LANES) == 0)
+
+
 def turn_kernel(x_ref, w_ref, o_ref):
     o_ref[...] = (x_ref[...] * w_ref[...]).T
 
 
 def turned(x, roots, cols):
-    rows, step = x.shape[0], 512
+    rows, step = x.shape[0], widest(cols)
     return pl.pallas_call(
         turn_kernel,
         grid=(cols // step,),
@@ -75,7 +81,7 @@
 
 def coefs(table, roots, x, odd, first):
     rows, cols = x.shape[0], x.shape[1] - first
-    step = 512
+    step = widest(math.gcd(first, cols))
     return pl.pallas_call(
         coef_kernel,
         grid=(cols // step,),
@@ -113,7 +119,13 @@
     return diagonal(first) + pltpu.roll(diagonal(second), BLOCKS, 1)
 
 
-def points_kernel(where_ref, t_ref, x_ref, c_ref, o_ref, s_ref):
+def by_core(rows, core):
+    for y in range(4):
+        even, odd = rows[16 * y : 16 * y + 8], rows[16 * y + 8 : 16 * y + 16]
+        yield y, jnp.where(core == 0, even, odd), jnp.where(core == 0, odd, even)
+
+
+def points_kernel(where_ref, t_ref, x_ref, c_ref, near_ref, far_ref, s_ref):
     tm_count, pts = x_ref.shape[0], x_ref.shape[1]
     tiles = s_ref.shape[0]
     table = split(t_ref[...])
@@ -139,24 +151,25 @@
         both(t, x_ref[t + 1][:, :HOP])
     both(tm_count - 1, c_ref[...])
 
-    y, core, x_at, z_at = (where_ref[n] for n in range(4))
+    y_at, core, x_at = (where_ref[n] for n in range(3))
 
     def owner(t):
         xr = lax.rem(t // 8 - x_at + 4, 4)
         z = lax.rem(t, 8)
-        zr = lax.rem(z - z_at + 8, 8)
         outs = []
         for b in range(2):
             mine = pl.ds(pl.multiple_of(2 * BLOCKS * (2 * t + b), 2 * BLOCKS), 2 * BLOCKS)
             rows = split(jnp.concatenate([s_ref[n, mine] for n in range(tiles)], axis=1))
             outs.append(re_im(dot3(rows, rows, NT)))
+        for b in range(2):
+            for y, near, far in by_core(outs[b], core):
+                yr = lax.rem(y - y_at + 4, 4)
+                near_ref[yr, xr, 2 * z + b] = near
+                far_ref[yr, xr, 2 * z + b] = far
         traces = two_traces(*outs)
-        for s in range(8):
-            cr = lax.rem(s % 2 + core, 2)
-            yr = lax.rem(s // 2 - y + 4, 4)
-            for b in range(2):
-                o_ref[cr, yr, xr, 2 * zr + b] = outs[b][8 * s : 8 * s + 8]
-            o_ref[cr, yr, xr, 16, pl.ds(z, 1), :] = traces
+        for y in range(4):
+            near_ref[y, xr, 16, pl.ds(z, 1), :] = traces
+            far_ref[y, xr, 16, pl.ds(z, 1), :] = traces
 
     def four_owners(i, carry):
         for n in range(4):
@@ -172,8 +185,8 @@
     return pl.pallas_call(
         points_kernel,
         in_specs=[pl.BlockSpec(memory_space=pltpu.SMEM), vmem, vmem, vmem],
-        out_specs=vmem,
-        out_shape=jax.ShapeDtypeStruct((2, 4, 4, 17, 8, LANES), F32),
+        out_specs=(vmem, vmem),
+        out_shape=(jax.ShapeDtypeStruct((4, 4, 17, 8, LANES), F32),) * 2,
         scratch_shapes=[pltpu.VMEM((wide // LANES, 2 * NBINS * BLOCKS, LANES), F32)],
         cost_estimate=pl.CostEstimate(
             flops=6 * 10**9, bytes_accessed=20 * 10**6, transcendentals=0
@@ -183,7 +196,7 @@
     )(where, table, samples, closing)
 
 
-def bins_kernel(a_ref, o_ref, s_ref):
+def bins_kernel(where_ref, a_ref, near_ref, far_ref, s_ref):
     tiles = s_ref.shape[0]
     tm_count = a_ref.shape[0] // (8 * tiles)
     for n in range(tiles):
@@ -198,35 +211,40 @@
         mine = pl.ds(2 * BLOCKS * b, 2 * BLOCKS)
         rows = split(jnp.concatenate([s_ref[n, mine] for n in range(tiles)], axis=1))
         outs.append(re_im(dot3(rows, rows, NT)))
+    y_at, core = where_ref[0], where_ref[1]
+    for b in range(2):
+        for y, near, far in by_core(outs[b], core):
+            yr = lax.rem(y - y_at + 4, 4)
+            near_ref[yr, b] = near
+            far_ref[yr, b] = far
     traces = jnp.broadcast_to(two_traces(*outs), (8, LANES))
-    for s in range(8):
-        for b in range(2):
-            o_ref[s, b] = outs[b][8 * s : 8 * s + 8]
-        o_ref[s, 2] = traces
-
-
-def bins_gram(coef):
+    for y in range(4):
+        near_ref[y, 2] = traces
+        far_ref[y, 2] = traces
+
+
+def bins_gram(where, coef):
     vmem = pl.BlockSpec(memory_space=pltpu.VMEM)
     tiles = coef.shape[1]
     return pl.pallas_call(
         bins_kernel,
-        in_specs=[vmem],
-        out_specs=vmem,
-        out_shape=jax.ShapeDtypeStruct((8, 3, 8, LANES), F32),
+        in_specs=[pl.BlockSpec(memory_space=pltpu.SMEM), vmem],
+        out_specs=(vmem, vmem),
+        out_shape=(jax.ShapeDtypeStruct((4, 3, 8, LANES), F32),) * 2,
         scratch_shapes=[pltpu.VMEM((tiles, 4 * BLOCKS, LANES), F32)],
         cost_estimate=pl.CostEstimate(
             flops=5 * 10**8, bytes_accessed=2 * 10**6, transcendentals=0
         ),
         compiler_params=pltpu.CompilerParams(vmem_limit_bytes=VMEM_BYTES),
         name="bins_gram",
-    )(coef.reshape(-1, LANES))
+    )(where, coef.reshape(-1, LANES))
 
 
 def norm_kernel(where_ref, r_ref, *refs):
     o_ref = refs[-1]
     total = r_ref[0]
-    for s in range(1, 8):
-        total = total + r_ref[s]
+    for z in range(1, 8):
+        total = total + r_ref[z]
     for ref in refs[:-1]:
         total = total + ref[...]
     row = lax.broadcasted_iota(jnp.int32, (8, LANES), 0)
@@ -246,6 +264,7 @@
         in_specs=[pl.BlockSpec(memory_space=pltpu.SMEM)] + [vmem] * (1 + len(others)),
         out_specs=vmem,
         out_shape=jax.ShapeDtypeStruct((2, 2, 8, BLOCKS), F32),
+        compiler_params=pltpu.CompilerParams(vmem_limit_bytes=VMEM_BYTES),
         name="normalize",
     )(where, parts, *others)
 
@@ -258,12 +277,13 @@
     return [(8 * x + z, 8 * ((x + d) % 4) + z) for x in range(4) for z in range(8)]
 
 
-def by_z(d):
-    return [(8 * x + z, 8 * x + (z + d) % 8) for x in range(4) for z in range(8)]
-
-
-def summed_up(held, axis, steps, pairs):
-    return sum([lax.ppermute(held[d], axis, pairs(d)) for d in range(1, steps)], held[0])
+def sent_on(near, axis, pairs):
+    return [near(0)] + [lax.ppermute(near(d), axis, pairs(d)) for d in range(1, 4)]
+
+
+def over_space(near, far):
+    far = lax.ppermute(far, "space", [(s, s ^ 1) for s in range(8)])
+    return sent_on(lambda d: near[d] + far[d], "space", by_y)
 
 
 def odd_blocks(snapshots, closing, tm, tm_count, first):
@@ -305,14 +325,14 @@
     own_closing = lax.dynamic_slice(closing, (0, tm * PTS_TM), (HOP, PTS_TM)) * own_roots
     samples, coef, own_closing = lax.optimization_barrier((samples, coef, own_closing.T))
     by_bin = lax.all_to_all(coef, "tm", 0, 0, tiled=True)
-    parts = points_gram(where, table, samples, own_closing)
-    held = parts[0] + lax.ppermute(parts[1], "space", [(s, s ^ 1) for s in range(8)])
-    held = summed_up(summed_up(held, "space", 4, by_y), "tm", 4, by_x)
+    held = sum(over_space(*points_gram(where, table, samples, own_closing)))
+    held = sum(sent_on(lambda d: held[d], "tm", by_x))
     by_bin, held = lax.optimization_barrier((by_bin, held))
-    others = [jnp.concatenate([held[2 * d : 2 * d + 2], held[16:]], axis=0) for d in range(8)]
-    others[1:] = [lax.ppermute(others[d], "tm", by_z(d)) for d in range(1, 8)]
-    parts = lax.all_to_all(bins_gram(by_bin), "space", 0, 0, tiled=True)
-    return normalized(where, parts, others)
+    traces = jnp.broadcast_to(held[16:], (8, 1, 8, LANES))
+    held = jnp.concatenate([held[:16].reshape(8, 2, 8, LANES), traces], axis=1)
+    columns = [[8 * x + z for z in range(8)] for x in range(4)]
+    others = lax.all_to_all(held, "tm", 0, 0, tiled=True, axis_index_groups=columns)
+    return normalized(where, others, over_space(*bins_gram(where, by_bin)))
 
 
 def solution(mesh):

time: 248 us -> 237 us (0.956)
  starting transfers between devices: 52 us -> 43.4 us
    ppermute x14 -> x11, starting transfers between devices: 25.5 us -> 14.4 us  [the longest x9 14.3 us: sent_on(): lax.ppermute(near(d), axis, pairs(d))]
    all_to_all x1, waiting for transfers between devices: 116 us -> 110 us  [body(): samples = lax.all_to_all(sent, 'tm', 0, 0, tiled=True)]
    ppermute x14 -> x11, waiting for transfers between devices: 22.5 us -> 25.7 us  [the longest x9 23 us: sent_on(): lax.ppermute(near(d), axis, pairs(d))]
    all_to_all x1, starting transfers between devices: 3.36 us -> 6.27 us  [body(): lax.all_to_all(held, 'tm', 0, 0, tiled=True, axis_index_groups=columns)]
    ppermute x1, waiting for transfers between devices: 1.44 us -> 4.12 us  [odd_blocks(): lax.ppermute(snapshots[:HOP, first:middle], 'tm', [(t, t - 1) for t in ra...]
  transfers between devices with their start and end apart: 19 -> 16, of which waited for: 10 -> 13; matrix products, arithmetic and copies ran while one was open for 2% -> 2% of each run, Pallas kernels for 14% -> 14%
where the time goes in v5:
time: 237 us; the launch traced here: 236 us
  waiting for transfers between devices  147 us (62%)
  starting transfers between devices  43.4 us (18%)
  Pallas kernels  36.4 us (15%)
  other arithmetic  6.18 us (3%)
  local copies, waits for them, and re-layouts  2.97 us (1%)
    all_to_all x1, waiting for transfers between devices, body(): samples = lax.all_to_all(sent, 'tm', 0, 0, tiled=True)  110 us
    ppermute x9, waiting for transfers between devices, sent_on(): lax.ppermute(near(d), axis, pairs(d))  23 us
    pallas_call x1, Pallas kernels, points_gram(): pl.pallas_call(points_kernel, in_specs=[pl.BlockSpec(memory_space=pltpu.S...  19.8 us
    ppermute x9, starting transfers between devices, sent_on(): lax.ppermute(near(d), axis, pairs(d))  14.3 us
    all_to_all x1, starting transfers between devices, body(): by_bin = lax.all_to_all(coef, 'tm', 0, 0, tiled=True)  9.53 us
    pallas_call x1, Pallas kernels, turned(): pl.pallas_call(turn_kernel, grid=(cols // step,), in_specs=[pl.BlockSpec(...  8.29 us
    ppermute x1, starting transfers between devices, odd_blocks(): lax.ppermute(snapshots[:HOP, first:middle], 'tm', [(t, t - 1) for t in ra...  7.74 us
    all_to_all x1, starting transfers between devices, body(): lax.all_to_all(held, 'tm', 0, 0, tiled=True, axis_index_groups=columns)  6.27 us
  transfers between devices with their start and end apart: 16, of which 13 were waited for; matrix products, arithmetic and copies ran while one was open for 2% of the time, Pallas kernels for 14%

profile of v5, /device:TPU:2, one launch (start us, length us, event | category | flops | bytes accessed | tf_op | source)
XLA Modules:
  0.0 236.4 jit_solution(6474189940908245785)
XLA Ops:
  0.0 2.0 fusion.21
  2.0 7.7 %collective-permute-start = (f32[128,1152]{1,0:T(8,128)S(1)}, f32[128,1152]{1,0:T(8,128)S(1)}, u32[]{:S(2)}, u32[]{:S(2)}) collective-permute-start(f32[128,1152]{1,0:T(8,128)S(1)} %get-tuple-element.31), channel_id=1, source_target_pairs={{1,0},{2,1},{3,2},{4,3},{5,4},{6,5},{7,6},{8,7},{9,8},{10,9},{11,1... | collective-permute-start | bytes 1769480 | tf_op jit(solution)/shard_map/ppermute | solution.py:291
  9.9 8.3 %turn_samples.1 = f32[5376,256]{1,0:T(8,128)} custom-call(f32[256,7680]{1,0:T(8,128)} %x_ref.3, f32[1,7680]{1,0:T(1,128)S(1)} %broadcast_in_dim.4.w_ref), custom_call_target="tpu_custom_call" | custom-call | bytes 11010048 | tf_op jit(solution)/shard_map/turn_samples/pallas_call | solution.py:52
  18.2 4.1 %collective-permute-done = f32[128,1152]{1,0:T(8,128)S(1)} collective-permute-done((f32[128,1152]{1,0:T(8,128)S(1)}, f32[128,1152]{1,0:T(8,128)S(1)}, u32[]{:S(2)}, u32[]{:S(2)}) %collective-permute-start) | collective-permute-done | bytes 589856 | tf_op jit(solution)/shard_map/ppermute | solution.py:291
  22.3 4.4 %collective-permute-done.1 = f32[128,1152]{1,0:T(8,128)S(1)} collective-permute-done((f32[128,1152]{1,0:T(8,128)S(1)}, f32[128,1152]{1,0:T(8,128)S(1)}, u32[]{:S(2)}, u32[]{:S(2)}) %collective-permute-start.1) | collective-permute-done | bytes 589856 | tf_op jit(solution)/shard_map/ppermute | solution.py:294
  26.7 5.4 %all-to-all-start = ((f32[32,168,256]{2,1,0:T(8,128)}), f32[32,168,256]{2,1,0:T(8,128)}, u32[]{:S(2)}, u32[]{:S(2)}) async-start(f32[32,168,256]{2,1,0:T(8,128)} %bitcast.48), calls=%async_computation | async-start | bytes 11010048 | tf_op jit(solution)/shard_map/all_to_all | solution.py:321
  32.8 1.0 constant_dynamic-slice_fusion
  34.0 1.1 slice_select_fusion.1
  35.2 1.7 maximum_maximum_fusion.odd_ref
  36.8 4.2 %coefs_by_bin.1 = f32[32,18,8,128]{3,2,1,0:T(8,128)S(1)} custom-call(f32[128,256]{1,0:T(8,128)S(1)} %reshape.168.t_ref, f32[1,7680]{1,0:T(1,128)S(1)} %broadcast_in_dim.4.w_ref, f32[256,7680]{1,0:T(8,128)} %x_ref.3, f32[256,2304]{1,0:T(8,128)} %maximum_maximum_fusion.odd_ref), custom_call_target="tpu_custom_call" | custom-call | flops 905969664 | bytes 5898240 | tf_op jit(solution)/shard_map/coefs_by_bin/pallas_call | solution.py:85
  41.1 1.5 copy-done
  42.6 110.2 %all-to-all-done.x_ref = f32[32,168,256]{2,1,0:T(8,128)} async-done(((f32[32,168,256]{2,1,0:T(8,128)}), f32[32,168,256]{2,1,0:T(8,128)}, u32[]{:S(2)}, u32[]{:S(2)}) %all-to-all-start) | async-done | bytes 5505056 | tf_op jit(solution)/shard_map/all_to_all | solution.py:321
  152.8 9.5 %all-to-all-start.1 = ((f32[32,18,8,128]{3,2,1,0:T(8,128)}), f32[32,18,8,128]{3,2,1,0:T(8,128)S(1)}, u32[]{:S(2)}, u32[]{:S(2)}) async-start(f32[32,18,8,128]{3,2,1,0:T(8,128)} %copy-done), calls=%async_computation.1 | async-start | bytes 4718592 | tf_op jit(solution)/shard_map/all_to_all | solution.py:327
  162.4 19.8 %points_gram.1 = (f32[4,4,17,8,128]{4,3,2,1,0:T(8,128)S(1)}, f32[4,4,17,8,128]{4,3,2,1,0:T(8,128)S(1)}) custom-call(s32[4]{0:T(128)S(1)} %pad_add_fusion.where_ref, f32[128,256]{1,0:T(8,128)S(1)} %reshape.168.t_ref, f32[32,168,256]{2,1,0:T(8,128)} %all-to-all-done.x_ref, f32[168,128]{1,0:T(8,128)S(1)} %multiply_bitcast_fusion.c_ref), custom_call_target="tpu_custom_call" | custom-call | flops 6000000000 | bytes 20000000 | tf_op jit(solution)/shard_map/points_gram/pallas_call | solution.py:185
  182.3 2.7 %collective-permute-done.2 = f32[4,4,17,8,128]{4,3,2,1,0:T(8,128)S(1)} collective-permute-done((f32[4,4,17,8,128]{4,3,2,1,0:T(8,128)S(1)}, f32[4,4,17,8,128]{4,3,2,1,0:T(8,128)S(1)}, u32[]{:S(2)}, u32[]{:S(2)}) %collective-permute-start.2) | collective-permute-done | bytes 1114144 | tf_op jit(solution)/shard_map/ppermute | solution.py:285
  185.1 3.1 %collective-permute-start.5 = (f32[4,17,8,128]{3,2,1,0:T(8,128)S(1)}, f32[4,17,8,128]{3,2,1,0:T(8,128)S(1)}, u32[]{:S(2)}, u32[]{:S(2)}) collective-permute-start(f32[4,17,8,128]{3,2,1,0:T(8,128)S(1)} %get-tuple-element.34), channel_id=1, source_target_pairs={{0,192},{32,224},{64,0},{96,32},{128,64},{160,96},{192,128},{224,1... | collective-permute-start | bytes 835592 | tf_op jit(solution)/shard_map/ppermute | solution.py:281
  188.9 1.0 collective-permute-start.3
  189.8 10.6 %collective-permute-done.5 = f32[4,17,8,128]{3,2,1,0:T(8,128)S(1)} collective-permute-done((f32[4,17,8,128]{3,2,1,0:T(8,128)S(1)}, f32[4,17,8,128]{3,2,1,0:T(8,128)S(1)}, u32[]{:S(2)}, u32[]{:S(2)}) %collective-permute-start.5) | collective-permute-done | bytes 278560 | tf_op jit(solution)/shard_map/ppermute | solution.py:281
  200.4 3.7 %collective-permute-done.3 = f32[4,17,8,128]{3,2,1,0:T(8,128)S(1)} collective-permute-done((f32[4,17,8,128]{3,2,1,0:T(8,128)S(1)}, f32[4,17,8,128]{3,2,1,0:T(8,128)S(1)}, u32[]{:S(2)}, u32[]{:S(2)}) %collective-permute-start.3) | collective-permute-done | bytes 278560 | tf_op jit(solution)/shard_map/ppermute | solution.py:281
  204.5 2.7 %collective-permute-start.7 = (f32[17,8,128]{2,1,0:T(8,128)S(1)}, f32[17,8,128]{2,1,0:T(8,128)S(1)}, u32[]{:S(2)}, u32[]{:S(2)}) collective-permute-start(f32[17,8,128]{2,1,0:T(8,128)S(1)} %get-tuple-element.38), channel_id=1, source_target_pairs={{0,16},{1,17},{2,18},{3,19},{4,20},{5,21},{6,22},{7,23},{8,24},{9,... | collective-permute-start | bytes 208904 | tf_op jit(solution)/shard_map/ppermute | solution.py:281
  207.2 1.8 collective-permute-start.6
  209.0 4.5 %collective-permute-done.8 = f32[17,8,128]{2,1,0:T(8,128)S(1)} collective-permute-done((f32[17,8,128]{2,1,0:T(8,128)S(1)}, f32[17,8,128]{2,1,0:T(8,128)S(1)}, u32[]{:S(2)}, u32[]{:S(2)}) %collective-permute-start.8) | collective-permute-done | bytes 69664 | tf_op jit(solution)/shard_map/ppermute | solution.py:281
  213.6 1.7 collective-permute-done.7
  215.4 1.0 all-to-all-done.1
  216.3 2.7 %bins_gram.1 = (f32[4,3,8,128]{3,2,1,0:T(8,128)S(1)}, f32[4,3,8,128]{3,2,1,0:T(8,128)S(1)}) custom-call(s32[4]{0:T(128)S(1)} %pad_add_fusion.where_ref, f32[4608,128]{1,0:T(8,128)S(1)} %bitcast.47), custom_call_target="tpu_custom_call" | custom-call | flops 500000000 | bytes 2000000 | tf_op jit(solution)/shard_map/bins_gram/pallas_call | solution.py:229
  219.7 6.3 %all-to-all-start.2 = ((f32[8,3,8,128]{3,2,1,0:T(8,128)}), f32[8,3,8,128]{3,2,1,0:T(8,128)S(1)}, u32[]{:S(2)}, u32[]{:S(2)}) async-start(f32[8,3,8,128]{3,2,1,0:T(8,128)} %pad_maximum_fusion.1), calls=%async_computation.2 | async-start | bytes 196608 | tf_op jit(solution)/shard_map/all_to_all | solution.py:334
  226.6 2.9 %collective-permute-start.11 = (f32[3,8,128]{2,1,0:T(8,128)S(1)}, f32[3,8,128]{2,1,0:T(8,128)S(1)}, u32[]{:S(2)}, u32[]{:S(2)}) collective-permute-start(f32[3,8,128]{2,1,0:T(8,128)S(1)} %get-tuple-element.40), channel_id=1, source_target_pairs={{0,128},{32,160},{64,192},{96,224},{128,0},{160,32},{192,64},{224,... | collective-permute-start | bytes 36872 | tf_op jit(solution)/shard_map/ppermute | solution.py:281
  229.5 1.3 collective-permute-start.12
  231.0 0.7 collective-permute-done.11.refs_2_
  231.8 1.4 collective-permute-done.12.refs_3_
  233.2 1.9 all-to-all-done.2.r_ref
  235.0 1.4 normalize.1
  (35 shorter events, 3.8 us)
Async XLA Ops:
  0.0 9.8 %copy-start.1 = (f32[7680]{0:T(1024)S(1)}, f32[7680]{0:T(1024)}, u32[]{:S(2)}) copy-start(f32[7680]{0:T(1024)} %param.6) | copy-start | bytes 92164
  2.0 20.3 %collective-permute-start = (f32[128,1152]{1,0:T(8,128)S(1)}, f32[128,1152]{1,0:T(8,128)S(1)}, u32[]{:S(2)}, u32[]{:S(2)}) collective-permute-start(f32[128,1152]{1,0:T(8,128)S(1)} %get-tuple-element.31), channel_id=1, source_target_pairs={{1,0},{2,1},{3,2},{4,3},{5,4},{6,5},{7,6},{8,7},{9,8},{10,9},{11,1... | collective-permute-start | bytes 1769480 | tf_op jit(solution)/shard_map/ppermute | solution.py:291
  9.7 17.0 %collective-permute-start.1 = (f32[128,1152]{1,0:T(8,128)S(1)}, f32[128,1152]{1,0:T(8,128)S(1)}, u32[]{:S(2)}, u32[]{:S(2)}) collective-permute-start(f32[128,1152]{1,0:T(8,128)S(1)} %get-tuple-element.30), channel_id=1, source_target_pairs={{0,1},{1,2},{2,3},{3,4},{4,5},{5,6},{6,7},{7,8},{8,9},{9,10},{10,1... | collective-permute-start | bytes 1769480 | tf_op jit(solution)/shard_map/ppermute | solution.py:294
  26.7 5.4 %copy-start.2 = (s32[64]{0:T(128)S(1)}, s32[64]{0:T(128)}, u32[]{:S(2)}) copy-start(s32[64]{0:T(128)} %param.7) | copy-start | bytes 772
  26.7 126.1 %all-to-all-start = ((f32[32,168,256]{2,1,0:T(8,128)}), f32[32,168,256]{2,1,0:T(8,128)}, u32[]{:S(2)}, u32[]{:S(2)}) async-start(f32[32,168,256]{2,1,0:T(8,128)} %bitcast.48), calls=%async_computation | async-start | bytes 11010048 | tf_op jit(solution)/shard_map/all_to_all | solution.py:321
  41.1 1.5 copy-start
  152.8 63.6 %all-to-all-start.1 = ((f32[32,18,8,128]{3,2,1,0:T(8,128)}), f32[32,18,8,128]{3,2,1,0:T(8,128)S(1)}, u32[]{:S(2)}, u32[]{:S(2)}) async-start(f32[32,18,8,128]{3,2,1,0:T(8,128)} %copy-done), calls=%async_computation.1 | async-start | bytes 4718592 | tf_op jit(solution)/shard_map/all_to_all | solution.py:327
  182.2 2.8 %collective-permute-start.2 = (f32[4,4,17,8,128]{4,3,2,1,0:T(8,128)S(1)}, f32[4,4,17,8,128]{4,3,2,1,0:T(8,128)S(1)}, u32[]{:S(2)}, u32[]{:S(2)}) collective-permute-start(f32[4,4,17,8,128]{4,3,2,1,0:T(8,128)S(1)} %get-tuple-element.24), channel_id=1, source_target_pairs={{0,32},{32,0},{64,96},{96,64},{128,160},{160,128},{192,224},{224,1... | collective-permute-start | bytes 3342344 | tf_op jit(solution)/shard_map/ppermute | solution.py:285
  185.1 15.3 %collective-permute-start.5 = (f32[4,17,8,128]{3,2,1,0:T(8,128)S(1)}, f32[4,17,8,128]{3,2,1,0:T(8,128)S(1)}, u32[]{:S(2)}, u32[]{:S(2)}) collective-permute-start(f32[4,17,8,128]{3,2,1,0:T(8,128)S(1)} %get-tuple-element.34), channel_id=1, source_target_pairs={{0,192},{32,224},{64,0},{96,32},{128,64},{160,96},{192,128},{224,1... | collective-permute-start | bytes 835592 | tf_op jit(solution)/shard_map/ppermute | solution.py:281
  188.2 12.2 %collective-permute-start.4 = (f32[4,17,8,128]{3,2,1,0:T(8,128)S(1)}, f32[4,17,8,128]{3,2,1,0:T(8,128)S(1)}, u32[]{:S(2)}, u32[]{:S(2)}) collective-permute-start(f32[4,17,8,128]{3,2,1,0:T(8,128)S(1)} %get-tuple-element.35), channel_id=1, source_target_pairs={{0,128},{32,160},{64,192},{96,224},{128,0},{160,32},{192,64},{224,... | collective-permute-start | bytes 835592 | tf_op jit(solution)/shard_map/ppermute | solution.py:281
  188.9 15.3 %collective-permute-start.3 = (f32[4,17,8,128]{3,2,1,0:T(8,128)S(1)}, f32[4,17,8,128]{3,2,1,0:T(8,128)S(1)}, u32[]{:S(2)}, u32[]{:S(2)}) collective-permute-start(f32[4,17,8,128]{3,2,1,0:T(8,128)S(1)} %get-tuple-element.33), channel_id=1, source_target_pairs={{0,64},{32,96},{64,128},{96,160},{128,192},{160,224},{192,0},{224,... | collective-permute-start | bytes 835592 | tf_op jit(solution)/shard_map/ppermute | solution.py:281
  204.2 9.4 %collective-permute-start.8 = (f32[17,8,128]{2,1,0:T(8,128)S(1)}, f32[17,8,128]{2,1,0:T(8,128)S(1)}, u32[]{:S(2)}, u32[]{:S(2)}) collective-permute-start(f32[17,8,128]{2,1,0:T(8,128)S(1)} %get-tuple-element.37), channel_id=1, source_target_pairs={{0,24},{1,25},{2,26},{3,27},{4,28},{5,29},{6,30},{7,31},{8,0},{9,1... | collective-permute-start | bytes 208904 | tf_op jit(solution)/shard_map/ppermute | solution.py:281
  204.5 10.8 %collective-permute-start.7 = (f32[17,8,128]{2,1,0:T(8,128)S(1)}, f32[17,8,128]{2,1,0:T(8,128)S(1)}, u32[]{:S(2)}, u32[]{:S(2)}) collective-permute-start(f32[17,8,128]{2,1,0:T(8,128)S(1)} %get-tuple-element.38), channel_id=1, source_target_pairs={{0,16},{1,17},{2,18},{3,19},{4,20},{5,21},{6,22},{7,23},{8,24},{9,... | collective-permute-start | bytes 208904 | tf_op jit(solution)/shard_map/ppermute | solution.py:281
  207.2 8.1 %collective-permute-start.6 = (f32[17,8,128]{2,1,0:T(8,128)S(1)}, f32[17,8,128]{2,1,0:T(8,128)S(1)}, u32[]{:S(2)}, u32[]{:S(2)}) collective-permute-start(f32[17,8,128]{2,1,0:T(8,128)S(1)} %get-tuple-element.36), channel_id=1, source_target_pairs={{0,8},{1,9},{2,10},{3,11},{4,12},{5,13},{6,14},{7,15},{8,16},{9,17... | collective-permute-start | bytes 208904 | tf_op jit(solution)/shard_map/ppermute | solution.py:281
  219.1 7.0 %collective-permute-start.9 = (f32[4,3,8,128]{3,2,1,0:T(8,128)S(1)}, f32[4,3,8,128]{3,2,1,0:T(8,128)S(1)}, u32[]{:S(2)}, u32[]{:S(2)}) collective-permute-start(f32[4,3,8,128]{3,2,1,0:T(8,128)S(1)} %get-tuple-element.28), channel_id=1, source_target_pairs={{0,32},{32,0},{64,96},{96,64},{128,160},{160,128},{192,224},{224,1... | collective-permute-start | bytes 147464 | tf_op jit(solution)/shard_map/ppermute | solution.py:285
  219.7 15.3 %all-to-all-start.2 = ((f32[8,3,8,128]{3,2,1,0:T(8,128)}), f32[8,3,8,128]{3,2,1,0:T(8,128)S(1)}, u32[]{:S(2)}, u32[]{:S(2)}) async-start(f32[8,3,8,128]{3,2,1,0:T(8,128)} %pad_maximum_fusion.1), calls=%async_computation.2 | async-start | bytes 196608 | tf_op jit(solution)/shard_map/all_to_all | solution.py:334
  226.0 5.0 %collective-permute-start.10 = (f32[3,8,128]{2,1,0:T(8,128)S(1)}, f32[3,8,128]{2,1,0:T(8,128)S(1)}, u32[]{:S(2)}, u32[]{:S(2)}) collective-permute-start(f32[3,8,128]{2,1,0:T(8,128)S(1)} %get-tuple-element.41), channel_id=1, source_target_pairs={{0,64},{32,96},{64,128},{96,160},{128,192},{160,224},{192,0},{224,... | collective-permute-start | bytes 36872 | tf_op jit(solution)/shard_map/ppermute | solution.py:281
  226.6 5.2 %collective-permute-start.11 = (f32[3,8,128]{2,1,0:T(8,128)S(1)}, f32[3,8,128]{2,1,0:T(8,128)S(1)}, u32[]{:S(2)}, u32[]{:S(2)}) collective-permute-start(f32[3,8,128]{2,1,0:T(8,128)S(1)} %get-tuple-element.40), channel_id=1, source_target_pairs={{0,128},{32,160},{64,192},{96,224},{128,0},{160,32},{192,64},{224,... | collective-permute-start | bytes 36872 | tf_op jit(solution)/shard_map/ppermute | solution.py:281
  229.5 3.7 %collective-permute-start.12 = (f32[3,8,128]{2,1,0:T(8,128)S(1)}, f32[3,8,128]{2,1,0:T(8,128)S(1)}, u32[]{:S(2)}, u32[]{:S(2)}) collective-permute-start(f32[3,8,128]{2,1,0:T(8,128)S(1)} %get-tuple-element.39), channel_id=1, source_target_pairs={{0,192},{32,224},{64,0},{96,32},{128,64},{160,96},{192,128},{224,1... | collective-permute-start | bytes 36872 | tf_op jit(solution)/shard_map/ppermute | solution.py:281

commit v6 on v5

--- a/solution.py
+++ b/solution.py
@@ -15,6 +15,7 @@
 PTS_TM = 168
 F32, BF16 = jnp.float32, jnp.bfloat16
 VMEM_BYTES = 50 * 2**20
+LONG = 4 * 10**11
 
 
 def split(a):
@@ -95,7 +96,7 @@
         out_shape=jax.ShapeDtypeStruct((NBINS // 2, cols // LANES, 8, LANES), F32),
         scratch_shapes=[pltpu.VMEM((step // LANES, 4 * NBINS, LANES), F32)],
         cost_estimate=pl.CostEstimate(
-            flops=12 * 2 * NBINS * rows * cols, bytes_accessed=10 * rows * cols, transcendentals=0
+            flops=LONG, bytes_accessed=10 * rows * cols, transcendentals=0
         ),
         compiler_params=pltpu.CompilerParams(vmem_limit_bytes=VMEM_BYTES),
         name="coefs_by_bin",
@@ -316,14 +317,16 @@
     first = tm_count * PTS_TM
     roots = jnp.sqrt(weights)[None, :]
     down, up, finish = odd_blocks(snapshots, closing, tm, tm_count, first)
+    table = table_rows(bin_index, NFFT)
+    own_roots = lax.dynamic_slice(roots, (0, tm * PTS_TM), (1, PTS_TM))
+    own_closing = (lax.dynamic_slice(closing, (0, tm * PTS_TM), (HOP, PTS_TM)) * own_roots).T
+    roots, table, own_closing, where = lax.optimization_barrier(
+        (roots, table, own_closing, where)
+    )
     sent = turned(snapshots, roots, first).reshape(tm_count, PTS_TM, NFFT)
-    sent, down, up = lax.optimization_barrier((sent, down, up))
     samples = lax.all_to_all(sent, "tm", 0, 0, tiled=True)
-    table = table_rows(bin_index, NFFT)
     coef = coefs(table, roots, snapshots, finish(down, up), first)
-    own_roots = lax.dynamic_slice(roots, (0, tm * PTS_TM), (1, PTS_TM))
-    own_closing = lax.dynamic_slice(closing, (0, tm * PTS_TM), (HOP, PTS_TM)) * own_roots
-    samples, coef, own_closing = lax.optimization_barrier((samples, coef, own_closing.T))
+    samples, coef = lax.optimization_barrier((samples, coef))
     by_bin = lax.all_to_all(coef, "tm", 0, 0, tiled=True)
     held = sum(over_space(*points_gram(where, table, samples, own_closing)))
     held = sum(sent_on(lambda d: held[d], "tm", by_x))

time: 237 us -> 235 us (level)
  waiting for transfers between devices: 147 us -> 140 us
  starting transfers between devices: 43.4 us -> 48.1 us
    ppermute x1, waiting for transfers between devices: 4.41 us -> 0.01 us  [odd_blocks(): lax.ppermute(snapshots[HOP:, middle:], 'tm', [(t, (t + 1) % tm_count) for...]
    ppermute x1, waiting for transfers between devices: 4.12 us -> 0.01 us  [odd_blocks(): lax.ppermute(snapshots[:HOP, first:middle], 'tm', [(t, t - 1) for t in ra...]
    all_to_all x1, starting transfers between devices: 5.36 us -> 9.07 us  [body(): samples = lax.all_to_all(sent, 'tm', 0, 0, tiled=True)]
  transfers between devices with their start and end apart: 16 -> 16, of which waited for: 13 -> 11; matrix products, arithmetic and copies ran while one was open for 2% -> 2% of each run, Pallas kernels for 14% -> 14%
where the time goes in v6:
time: 235 us
  waiting for transfers between devices  140 us (60%)
  starting transfers between devices  48.1 us (20%)
  Pallas kernels  36.4 us (15%)
  other arithmetic  7.16 us (3%)
  local copies, waits for them, and re-layouts  2.97 us (1%)
    all_to_all x1, waiting for transfers between devices, body(): samples = lax.all_to_all(sent, 'tm', 0, 0, tiled=True)  111 us
    ppermute x9, waiting for transfers between devices, sent_on(): lax.ppermute(near(d), axis, pairs(d))  22.8 us
    pallas_call x1, Pallas kernels, points_gram(): pl.pallas_call(points_kernel, in_specs=[pl.BlockSpec(memory_space=pltpu.S...  19.8 us
    ppermute x9, starting transfers between devices, sent_on(): lax.ppermute(near(d), axis, pairs(d))  14.3 us
    all_to_all x1, starting transfers between devices, body(): by_bin = lax.all_to_all(coef, 'tm', 0, 0, tiled=True)  10.7 us
    all_to_all x1, starting transfers between devices, body(): samples = lax.all_to_all(sent, 'tm', 0, 0, tiled=True)  9.07 us
    pallas_call x1, Pallas kernels, turned(): pl.pallas_call(turn_kernel, grid=(cols // step,), in_specs=[pl.BlockSpec(...  8.28 us
    all_to_all x1, starting transfers between devices, body(): lax.all_to_all(held, 'tm', 0, 0, tiled=True, axis_index_groups=columns)  6.17 us
  transfers between devices with their start and end apart: 16, of which 11 were waited for; matrix products, arithmetic and copies ran while one was open for 2% of the time, Pallas kernels for 14%

profile of v6, /device:TPU:2, one launch (start us, length us, event | category | flops | bytes accessed | tf_op | source)
XLA Modules:
  0.0 234.7 jit_solution(3508846234902214000)
XLA Ops:
  0.0 2.8 %fusion.21 = (f32[128,1152]{1,0:T(8,128)S(1)}, f32[128,1152]{1,0:T(8,128)}, f32[128,1152]{1,0:T(8,128)S(1)}, f32[128,1152]{1,0:T(8,128)S(1)}) fusion(f32[256,7680]{1,0:T(8,128)} %x_ref.3, f32[128,7680]{1,0:T(8,128)} %param.5, pred[]{:T(512)S(6)} %eq.12), kind=kLoop, calls=%fused_computation.48 | loop fusion | flops 147456 | bytes 5308417 | tf_op jit(solution)/shard_map/slice | solution.py:304
  2.8 1.9 collective-permute-start.1
  4.7 5.8 %collective-permute-start = (f32[128,1152]{1,0:T(8,128)S(1)}, f32[128,1152]{1,0:T(8,128)}, u32[]{:S(2)}, u32[]{:S(2)}) collective-permute-start(f32[128,1152]{1,0:T(8,128)S(1)} %get-tuple-element.31), channel_id=1, source_target_pairs={{1,0},{2,1},{3,2},{4,3},{5,4},{6,5},{7,6},{8,7},{9,8},{10,9},{11,1... | collective-permute-start | bytes 1769480 | tf_op jit(solution)/shard_map/ppermute | solution.py:292
  11.3 1.0 constant_dynamic-slice_fusion
  12.7 8.3 %turn_samples.1 = f32[5376,256]{1,0:T(8,128)} custom-call(f32[256,7680]{1,0:T(8,128)} %x_ref.3, f32[1,7680]{1,0:T(1,128)S(1)} %broadcast_in_dim.4.w_ref), custom_call_target="tpu_custom_call" | custom-call | bytes 11010048 | tf_op jit(solution)/shard_map/turn_samples/pallas_call | solution.py:53
  20.9 9.1 %all-to-all-start = ((f32[32,168,256]{2,1,0:T(8,128)}), f32[32,168,256]{2,1,0:T(8,128)}, u32[]{:S(2)}, u32[]{:S(2)}) async-start(f32[32,168,256]{2,1,0:T(8,128)} %bitcast.48), calls=%async_computation | async-start | bytes 11010048 | tf_op jit(solution)/shard_map/all_to_all | solution.py:327
  30.0 1.3 slice_select_fusion.1
  31.4 1.7 maximum_maximum_fusion.odd_ref
  33.0 4.2 %coefs_by_bin.1 = f32[32,18,8,128]{3,2,1,0:T(8,128)S(1)} custom-call(f32[128,256]{1,0:T(8,128)S(1)} %reshape.167.t_ref, f32[1,7680]{1,0:T(1,128)S(1)} %broadcast_in_dim.4.w_ref, f32[256,7680]{1,0:T(8,128)} %x_ref.3, f32[256,2304]{1,0:T(8,128)} %maximum_maximum_fusion.odd_ref), custom_call_target="tpu_custom_call" | custom-call | flops 399999991808 | bytes 5898240 | tf_op jit(solution)/shard_map/coefs_by_bin/pallas_call | solution.py:86
  37.3 1.5 copy-done
  38.8 111.3 %all-to-all-done.x_ref = f32[32,168,256]{2,1,0:T(8,128)} async-done(((f32[32,168,256]{2,1,0:T(8,128)}), f32[32,168,256]{2,1,0:T(8,128)}, u32[]{:S(2)}, u32[]{:S(2)}) %all-to-all-start) | async-done | bytes 5505056 | tf_op jit(solution)/shard_map/all_to_all | solution.py:327
  150.1 10.7 %all-to-all-start.1 = ((f32[32,18,8,128]{3,2,1,0:T(8,128)}), f32[32,18,8,128]{3,2,1,0:T(8,128)S(1)}, u32[]{:S(2)}, u32[]{:S(2)}) async-start(f32[32,18,8,128]{3,2,1,0:T(8,128)} %copy-done), calls=%async_computation.1 | async-start | bytes 4718592 | tf_op jit(solution)/shard_map/all_to_all | solution.py:330
  160.8 19.8 %points_gram.1 = (f32[4,4,17,8,128]{4,3,2,1,0:T(8,128)S(1)}, f32[4,4,17,8,128]{4,3,2,1,0:T(8,128)S(1)}) custom-call(s32[4]{0:T(128)S(1)} %pad_add_fusion.where_ref, f32[128,256]{1,0:T(8,128)S(1)} %reshape.167.t_ref, f32[32,168,256]{2,1,0:T(8,128)} %all-to-all-done.x_ref, f32[168,128]{1,0:T(8,128)S(1)} %multiply_bitcast_fusion.c_ref), custom_call_target="tpu_custom_call" | custom-call | flops 6000000000 | bytes 20000000 | tf_op jit(solution)/shard_map/points_gram/pallas_call | solution.py:186
  180.7 2.7 %collective-permute-done.2 = f32[4,4,17,8,128]{4,3,2,1,0:T(8,128)S(1)} collective-permute-done((f32[4,4,17,8,128]{4,3,2,1,0:T(8,128)S(1)}, f32[4,4,17,8,128]{4,3,2,1,0:T(8,128)S(1)}, u32[]{:S(2)}, u32[]{:S(2)}) %collective-permute-start.2) | collective-permute-done | bytes 1114144 | tf_op jit(solution)/shard_map/ppermute | solution.py:286
  183.5 3.1 %collective-permute-start.5 = (f32[4,17,8,128]{3,2,1,0:T(8,128)S(1)}, f32[4,17,8,128]{3,2,1,0:T(8,128)S(1)}, u32[]{:S(2)}, u32[]{:S(2)}) collective-permute-start(f32[4,17,8,128]{3,2,1,0:T(8,128)S(1)} %get-tuple-element.34), channel_id=1, source_target_pairs={{0,192},{32,224},{64,0},{96,32},{128,64},{160,96},{192,128},{224,1... | collective-permute-start | bytes 835592 | tf_op jit(solution)/shard_map/ppermute | solution.py:282
  187.2 1.0 collective-permute-start.3
  188.2 10.6 %collective-permute-done.5 = f32[4,17,8,128]{3,2,1,0:T(8,128)S(1)} collective-permute-done((f32[4,17,8,128]{3,2,1,0:T(8,128)S(1)}, f32[4,17,8,128]{3,2,1,0:T(8,128)S(1)}, u32[]{:S(2)}, u32[]{:S(2)}) %collective-permute-start.5) | collective-permute-done | bytes 278560 | tf_op jit(solution)/shard_map/ppermute | solution.py:282
  198.8 3.7 %collective-permute-done.3 = f32[4,17,8,128]{3,2,1,0:T(8,128)S(1)} collective-permute-done((f32[4,17,8,128]{3,2,1,0:T(8,128)S(1)}, f32[4,17,8,128]{3,2,1,0:T(8,128)S(1)}, u32[]{:S(2)}, u32[]{:S(2)}) %collective-permute-start.3) | collective-permute-done | bytes 278560 | tf_op jit(solution)/shard_map/ppermute | solution.py:282
  202.9 2.7 %collective-permute-start.7 = (f32[17,8,128]{2,1,0:T(8,128)S(1)}, f32[17,8,128]{2,1,0:T(8,128)S(1)}, u32[]{:S(2)}, u32[]{:S(2)}) collective-permute-start(f32[17,8,128]{2,1,0:T(8,128)S(1)} %get-tuple-element.38), channel_id=1, source_target_pairs={{0,16},{1,17},{2,18},{3,19},{4,20},{5,21},{6,22},{7,23},{8,24},{9,... | collective-permute-start | bytes 208904 | tf_op jit(solution)/shard_map/ppermute | solution.py:282
  205.6 1.8 collective-permute-start.6
  207.4 4.5 %collective-permute-done.8 = f32[17,8,128]{2,1,0:T(8,128)S(1)} collective-permute-done((f32[17,8,128]{2,1,0:T(8,128)S(1)}, f32[17,8,128]{2,1,0:T(8,128)S(1)}, u32[]{:S(2)}, u32[]{:S(2)}) %collective-permute-start.8) | collective-permute-done | bytes 69664 | tf_op jit(solution)/shard_map/ppermute | solution.py:282
  211.9 1.7 collective-permute-done.7
  213.6 1.1 all-to-all-done.1
  214.7 2.7 %bins_gram.1 = (f32[4,3,8,128]{3,2,1,0:T(8,128)S(1)}, f32[4,3,8,128]{3,2,1,0:T(8,128)S(1)}) custom-call(s32[4]{0:T(128)S(1)} %pad_add_fusion.where_ref, f32[4608,128]{1,0:T(8,128)S(1)} %bitcast.47), custom_call_target="tpu_custom_call" | custom-call | flops 500000000 | bytes 2000000 | tf_op jit(solution)/shard_map/bins_gram/pallas_call | solution.py:230
  217.5 0.6 pad_maximum_fusion.1
  218.1 6.2 %all-to-all-start.2 = ((f32[8,3,8,128]{3,2,1,0:T(8,128)}), f32[8,3,8,128]{3,2,1,0:T(8,128)S(1)}, u32[]{:S(2)}, u32[]{:S(2)}) async-start(f32[8,3,8,128]{3,2,1,0:T(8,128)} %pad_maximum_fusion.1), calls=%async_computation.2 | async-start | bytes 196608 | tf_op jit(solution)/shard_map/all_to_all | solution.py:337
  224.9 2.9 %collective-permute-start.11 = (f32[3,8,128]{2,1,0:T(8,128)S(1)}, f32[3,8,128]{2,1,0:T(8,128)S(1)}, u32[]{:S(2)}, u32[]{:S(2)}) collective-permute-start(f32[3,8,128]{2,1,0:T(8,128)S(1)} %get-tuple-element.40), channel_id=1, source_target_pairs={{0,128},{32,160},{64,192},{96,224},{128,0},{160,32},{192,64},{224,... | collective-permute-start | bytes 36872 | tf_op jit(solution)/shard_map/ppermute | solution.py:282
  227.9 1.3 collective-permute-start.12
  229.3 0.8 collective-permute-done.11.refs_2_
  230.1 1.4 collective-permute-done.12.refs_3_
  231.5 1.8 all-to-all-done.2.r_ref
  233.3 1.4 normalize.1
  (35 shorter events, 3.0 us)
Async XLA Ops:
  0.0 10.6 %copy-start.2 = (s32[64]{0:T(128)S(1)}, s32[64]{0:T(128)}, u32[]{:S(2)}) copy-start(s32[64]{0:T(128)} %param.7) | copy-start | bytes 772
  0.0 10.9 %copy-start.1 = (f32[7680]{0:T(1024)S(1)}, f32[7680]{0:T(1024)}, u32[]{:S(2)}) copy-start(f32[7680]{0:T(1024)} %param.6) | copy-start | bytes 92164
  2.8 28.6 %collective-permute-start.1 = (f32[128,1152]{1,0:T(8,128)}, f32[128,1152]{1,0:T(8,128)S(1)}, u32[]{:S(2)}, u32[]{:S(2)}) collective-permute-start(f32[128,1152]{1,0:T(8,128)} %get-tuple-element.30), channel_id=1, source_target_pairs={{0,1},{1,2},{2,3},{3,4},{4,5},{5,6},{6,7},{7,8},{8,9},{9,10},{10,1... | collective-permute-start | bytes 1769480 | tf_op jit(solution)/shard_map/ppermute | solution.py:295
  4.7 25.3 %collective-permute-start = (f32[128,1152]{1,0:T(8,128)S(1)}, f32[128,1152]{1,0:T(8,128)}, u32[]{:S(2)}, u32[]{:S(2)}) collective-permute-start(f32[128,1152]{1,0:T(8,128)S(1)} %get-tuple-element.31), channel_id=1, source_target_pairs={{1,0},{2,1},{3,2},{4,3},{5,4},{6,5},{7,6},{8,7},{9,8},{10,9},{11,1... | collective-permute-start | bytes 1769480 | tf_op jit(solution)/shard_map/ppermute | solution.py:292
  20.9 129.1 %all-to-all-start = ((f32[32,168,256]{2,1,0:T(8,128)}), f32[32,168,256]{2,1,0:T(8,128)}, u32[]{:S(2)}, u32[]{:S(2)}) async-start(f32[32,168,256]{2,1,0:T(8,128)} %bitcast.48), calls=%async_computation | async-start | bytes 11010048 | tf_op jit(solution)/shard_map/all_to_all | solution.py:327
  37.3 1.5 copy-start
  150.1 64.6 %all-to-all-start.1 = ((f32[32,18,8,128]{3,2,1,0:T(8,128)}), f32[32,18,8,128]{3,2,1,0:T(8,128)S(1)}, u32[]{:S(2)}, u32[]{:S(2)}) async-start(f32[32,18,8,128]{3,2,1,0:T(8,128)} %copy-done), calls=%async_computation.1 | async-start | bytes 4718592 | tf_op jit(solution)/shard_map/all_to_all | solution.py:330
  180.6 2.8 %collective-permute-start.2 = (f32[4,4,17,8,128]{4,3,2,1,0:T(8,128)S(1)}, f32[4,4,17,8,128]{4,3,2,1,0:T(8,128)S(1)}, u32[]{:S(2)}, u32[]{:S(2)}) collective-permute-start(f32[4,4,17,8,128]{4,3,2,1,0:T(8,128)S(1)} %get-tuple-element.24), channel_id=1, source_target_pairs={{0,32},{32,0},{64,96},{96,64},{128,160},{160,128},{192,224},{224,1... | collective-permute-start | bytes 3342344 | tf_op jit(solution)/shard_map/ppermute | solution.py:286
  183.5 15.3 %collective-permute-start.5 = (f32[4,17,8,128]{3,2,1,0:T(8,128)S(1)}, f32[4,17,8,128]{3,2,1,0:T(8,128)S(1)}, u32[]{:S(2)}, u32[]{:S(2)}) collective-permute-start(f32[4,17,8,128]{3,2,1,0:T(8,128)S(1)} %get-tuple-element.34), channel_id=1, source_target_pairs={{0,192},{32,224},{64,0},{96,32},{128,64},{160,96},{192,128},{224,1... | collective-permute-start | bytes 835592 | tf_op jit(solution)/shard_map/ppermute | solution.py:282
  186.6 12.2 %collective-permute-start.4 = (f32[4,17,8,128]{3,2,1,0:T(8,128)S(1)}, f32[4,17,8,128]{3,2,1,0:T(8,128)S(1)}, u32[]{:S(2)}, u32[]{:S(2)}) collective-permute-start(f32[4,17,8,128]{3,2,1,0:T(8,128)S(1)} %get-tuple-element.35), channel_id=1, source_target_pairs={{0,128},{32,160},{64,192},{96,224},{128,0},{160,32},{192,64},{224,... | collective-permute-start | bytes 835592 | tf_op jit(solution)/shard_map/ppermute | solution.py:282
  187.2 15.3 %collective-permute-start.3 = (f32[4,17,8,128]{3,2,1,0:T(8,128)S(1)}, f32[4,17,8,128]{3,2,1,0:T(8,128)S(1)}, u32[]{:S(2)}, u32[]{:S(2)}) collective-permute-start(f32[4,17,8,128]{3,2,1,0:T(8,128)S(1)} %get-tuple-element.33), channel_id=1, source_target_pairs={{0,64},{32,96},{64,128},{96,160},{128,192},{160,224},{192,0},{224,... | collective-permute-start | bytes 835592 | tf_op jit(solution)/shard_map/ppermute | solution.py:282
  202.6 9.3 %collective-permute-start.8 = (f32[17,8,128]{2,1,0:T(8,128)S(1)}, f32[17,8,128]{2,1,0:T(8,128)S(1)}, u32[]{:S(2)}, u32[]{:S(2)}) collective-permute-start(f32[17,8,128]{2,1,0:T(8,128)S(1)} %get-tuple-element.37), channel_id=1, source_target_pairs={{0,24},{1,25},{2,26},{3,27},{4,28},{5,29},{6,30},{7,31},{8,0},{9,1... | collective-permute-start | bytes 208904 | tf_op jit(solution)/shard_map/ppermute | solution.py:282
  202.9 10.7 %collective-permute-start.7 = (f32[17,8,128]{2,1,0:T(8,128)S(1)}, f32[17,8,128]{2,1,0:T(8,128)S(1)}, u32[]{:S(2)}, u32[]{:S(2)}) collective-permute-start(f32[17,8,128]{2,1,0:T(8,128)S(1)} %get-tuple-element.38), channel_id=1, source_target_pairs={{0,16},{1,17},{2,18},{3,19},{4,20},{5,21},{6,22},{7,23},{8,24},{9,... | collective-permute-start | bytes 208904 | tf_op jit(solution)/shard_map/ppermute | solution.py:282
  205.6 8.0 %collective-permute-start.6 = (f32[17,8,128]{2,1,0:T(8,128)S(1)}, f32[17,8,128]{2,1,0:T(8,128)S(1)}, u32[]{:S(2)}, u32[]{:S(2)}) collective-permute-start(f32[17,8,128]{2,1,0:T(8,128)S(1)} %get-tuple-element.36), channel_id=1, source_target_pairs={{0,8},{1,9},{2,10},{3,11},{4,12},{5,13},{6,14},{7,15},{8,16},{9,17... | collective-permute-start | bytes 208904 | tf_op jit(solution)/shard_map/ppermute | solution.py:282
  217.5 6.9 %collective-permute-start.9 = (f32[4,3,8,128]{3,2,1,0:T(8,128)S(1)}, f32[4,3,8,128]{3,2,1,0:T(8,128)S(1)}, u32[]{:S(2)}, u32[]{:S(2)}) collective-permute-start(f32[4,3,8,128]{3,2,1,0:T(8,128)S(1)} %get-tuple-element.28), channel_id=1, source_target_pairs={{0,32},{32,0},{64,96},{96,64},{128,160},{160,128},{192,224},{224,1... | collective-permute-start | bytes 147464 | tf_op jit(solution)/shard_map/ppermute | solution.py:286
  218.1 15.2 %all-to-all-start.2 = ((f32[8,3,8,128]{3,2,1,0:T(8,128)}), f32[8,3,8,128]{3,2,1,0:T(8,128)S(1)}, u32[]{:S(2)}, u32[]{:S(2)}) async-start(f32[8,3,8,128]{3,2,1,0:T(8,128)} %pad_maximum_fusion.1), calls=%async_computation.2 | async-start | bytes 196608 | tf_op jit(solution)/shard_map/all_to_all | solution.py:337
  224.3 5.0 %collective-permute-start.10 = (f32[3,8,128]{2,1,0:T(8,128)S(1)}, f32[3,8,128]{2,1,0:T(8,128)S(1)}, u32[]{:S(2)}, u32[]{:S(2)}) collective-permute-start(f32[3,8,128]{2,1,0:T(8,128)S(1)} %get-tuple-element.41), channel_id=1, source_target_pairs={{0,64},{32,96},{64,128},{96,160},{128,192},{160,224},{192,0},{224,... | collective-permute-start | bytes 36872 | tf_op jit(solution)/shard_map/ppermute | solution.py:282
  224.9 5.2 %collective-permute-start.11 = (f32[3,8,128]{2,1,0:T(8,128)S(1)}, f32[3,8,128]{2,1,0:T(8,128)S(1)}, u32[]{:S(2)}, u32[]{:S(2)}) collective-permute-start(f32[3,8,128]{2,1,0:T(8,128)S(1)} %get-tuple-element.40), channel_id=1, source_target_pairs={{0,128},{32,160},{64,192},{96,224},{128,0},{160,32},{192,64},{224,... | collective-permute-start | bytes 36872 | tf_op jit(solution)/shard_map/ppermute | solution.py:282
  227.9 3.7 %collective-permute-start.12 = (f32[3,8,128]{2,1,0:T(8,128)S(1)}, f32[3,8,128]{2,1,0:T(8,128)S(1)}, u32[]{:S(2)}, u32[]{:S(2)}) collective-permute-start(f32[3,8,128]{2,1,0:T(8,128)S(1)} %get-tuple-element.39), channel_id=1, source_target_pairs={{0,192},{32,224},{64,0},{96,32},{128,64},{160,96},{192,128},{224,1... | collective-permute-start | bytes 36872 | tf_op jit(solution)/shard_map/ppermute | solution.py:282

commit v7 on v5

--- a/solution.py
+++ b/solution.py
@@ -15,6 +15,7 @@
 PTS_TM = 168
 F32, BF16 = jnp.float32, jnp.bfloat16
 VMEM_BYTES = 50 * 2**20
+LONG = 4 * 10**11
 
 
 def split(a):
@@ -39,8 +40,8 @@
     return paired.reshape(2 * bin_index.shape[0], length)
 
 
-def widest(cols):
-    return max(n * LANES for n in range(1, 7) if cols % (n * LANES) == 0)
+def widest(cols, most):
+    return max(n * LANES for n in range(1, most + 1) if cols % (n * LANES) == 0)
 
 
 def turn_kernel(x_ref, w_ref, o_ref):
@@ -48,7 +49,7 @@
 
 
 def turned(x, roots, cols):
-    rows, step = x.shape[0], widest(cols)
+    rows, step = x.shape[0], widest(cols, 24)
     return pl.pallas_call(
         turn_kernel,
         grid=(cols // step,),
@@ -81,7 +82,7 @@
 
 def coefs(table, roots, x, odd, first):
     rows, cols = x.shape[0], x.shape[1] - first
-    step = widest(math.gcd(first, cols))
+    step = widest(math.gcd(first, cols), 6)
     return pl.pallas_call(
         coef_kernel,
         grid=(cols // step,),
@@ -95,7 +96,7 @@
         out_shape=jax.ShapeDtypeStruct((NBINS // 2, cols // LANES, 8, LANES), F32),
         scratch_shapes=[pltpu.VMEM((step // LANES, 4 * NBINS, LANES), F32)],
         cost_estimate=pl.CostEstimate(
-            flops=12 * 2 * NBINS * rows * cols, bytes_accessed=10 * rows * cols, transcendentals=0
+            flops=LONG, bytes_accessed=10 * rows * cols, transcendentals=0
         ),
         compiler_params=pltpu.CompilerParams(vmem_limit_bytes=VMEM_BYTES),
         name="coefs_by_bin",
@@ -317,19 +318,19 @@
     roots = jnp.sqrt(weights)[None, :]
     down, up, finish = odd_blocks(snapshots, closing, tm, tm_count, first)
     sent = turned(snapshots, roots, first).reshape(tm_count, PTS_TM, NFFT)
-    sent, down, up = lax.optimization_barrier((sent, down, up))
     samples = lax.all_to_all(sent, "tm", 0, 0, tiled=True)
+    down, up, bin_index, closing = lax.optimization_barrier((down, up, bin_index, closing))
     table = table_rows(bin_index, NFFT)
-    coef = coefs(table, roots, snapshots, finish(down, up), first)
     own_roots = lax.dynamic_slice(roots, (0, tm * PTS_TM), (1, PTS_TM))
     own_closing = lax.dynamic_slice(closing, (0, tm * PTS_TM), (HOP, PTS_TM)) * own_roots
+    coef = coefs(table, roots, snapshots, finish(down, up), first)
     samples, coef, own_closing = lax.optimization_barrier((samples, coef, own_closing.T))
     by_bin = lax.all_to_all(coef, "tm", 0, 0, tiled=True)
     held = sum(over_space(*points_gram(where, table, samples, own_closing)))
     held = sum(sent_on(lambda d: held[d], "tm", by_x))
-    by_bin, held = lax.optimization_barrier((by_bin, held))
     traces = jnp.broadcast_to(held[16:], (8, 1, 8, LANES))
     held = jnp.concatenate([held[:16].reshape(8, 2, 8, LANES), traces], axis=1)
+    by_bin, held = lax.optimization_barrier((by_bin, held))
     columns = [[8 * x + z for z in range(8)] for x in range(4)]
     others = lax.all_to_all(held, "tm", 0, 0, tiled=True, axis_index_groups=columns)
     return normalized(where, others, over_space(*bins_gram(where, by_bin)))

time: 237 us -> 230 us (0.970)
  waiting for transfers between devices: 147 us -> 133 us
  starting transfers between devices: 43.4 us -> 47.9 us
  local copies, waits for them, and re-layouts: 2.97 us -> 7.21 us
  Pallas kernels: 36.4 us -> 33.1 us
    all_to_all x1, waiting for transfers between devices: 110 us -> 97.1 us  [body(): samples = lax.all_to_all(sent, 'tm', 0, 0, tiled=True)]
    optimization_barrier x0 -> x1, local copies, waits for them, and re-layouts: none -> 6.29 us  [body(): lax.optimization_barrier((down, up, bin_index, closing))]
    ppermute x1, waiting for transfers between devices: 4.12 us -> 0.01 us  [odd_blocks(): lax.ppermute(snapshots[:HOP, first:middle], 'tm', [(t, t - 1) for t in ra...]
    ppermute x1, waiting for transfers between devices: 4.41 us -> 7.8 us  [odd_blocks(): lax.ppermute(snapshots[HOP:, middle:], 'tm', [(t, (t + 1) % tm_count) for...]
    all_to_all x1, starting transfers between devices: 5.36 us -> 8.75 us  [body(): samples = lax.all_to_all(sent, 'tm', 0, 0, tiled=True)]
    pallas_call x1, Pallas kernels: 8.29 us -> 5.05 us  [turned(): pl.pallas_call(turn_kernel, grid=(cols // step,), in_specs=[pl.BlockSpec(...]
  transfers between devices with their start and end apart: 16 -> 16, of which waited for: 13 -> 12; matrix products, arithmetic and copies ran while one was open for 2% -> 5% of each run, Pallas kernels for 14% -> 13%
where the time goes in v7:
time: 230 us; the launch traced here: 229 us
  waiting for transfers between devices  133 us (58%)
  starting transfers between devices  47.9 us (21%)
  Pallas kernels  33.1 us (14%)
  other arithmetic  7.88 us (3%)
  local copies, waits for them, and re-layouts  7.21 us (3%)
    all_to_all x1, waiting for transfers between devices, body(): samples = lax.all_to_all(sent, 'tm', 0, 0, tiled=True)  97.1 us
    ppermute x9, waiting for transfers between devices, sent_on(): lax.ppermute(near(d), axis, pairs(d))  22.4 us
    pallas_call x1, Pallas kernels, points_gram(): pl.pallas_call(points_kernel, in_specs=[pl.BlockSpec(memory_space=pltpu.S...  19.8 us
    ppermute x9, starting transfers between devices, sent_on(): lax.ppermute(near(d), axis, pairs(d))  14.2 us
    all_to_all x1, starting transfers between devices, body(): by_bin = lax.all_to_all(coef, 'tm', 0, 0, tiled=True)  10 us
    all_to_all x1, starting transfers between devices, body(): samples = lax.all_to_all(sent, 'tm', 0, 0, tiled=True)  8.75 us
    ppermute x1, waiting for transfers between devices, odd_blocks(): lax.ppermute(snapshots[HOP:, middle:], 'tm', [(t, (t + 1) % tm_count) for...  7.8 us
    ppermute x1, starting transfers between devices, odd_blocks(): lax.ppermute(snapshots[:HOP, first:middle], 'tm', [(t, t - 1) for t in ra...  7.72 us
  transfers between devices with their start and end apart: 16, of which 12 were waited for; matrix products, arithmetic and copies ran while one was open for 5% of the time, Pallas kernels for 13%

profile of v7, /device:TPU:2, one launch (start us, length us, event | category | flops | bytes accessed | tf_op | source)
XLA Modules:
  0.0 229.2 jit_solution(2381012803174025555)
XLA Ops:
  0.0 2.8 %fusion.21 = (f32[128,1152]{1,0:T(8,128)S(1)}, f32[128,1152]{1,0:T(8,128)S(1)}, f32[128,1152]{1,0:T(8,128)}, f32[128,1152]{1,0:T(8,128)S(1)}) fusion(f32[256,7680]{1,0:T(8,128)} %x_ref.3, f32[128,7680]{1,0:T(8,128)} %param.5, pred[]{:T(512)S(6)} %eq.12), kind=kLoop, calls=%fused_computation.47 | loop fusion | flops 147456 | bytes 5308417 | tf_op jit(solution)/shard_map/slice | solution.py:304
  2.8 7.7 %collective-permute-start = (f32[128,1152]{1,0:T(8,128)}, f32[128,1152]{1,0:T(8,128)S(1)}, u32[]{:S(2)}, u32[]{:S(2)}) collective-permute-start(f32[128,1152]{1,0:T(8,128)} %get-tuple-element.33), channel_id=1, source_target_pairs={{1,0},{2,1},{3,2},{4,3},{5,4},{6,5},{7,6},{8,7},{9,8},{10,9},{11,1... | collective-permute-start | bytes 1769480 | tf_op jit(solution)/shard_map/ppermute | solution.py:292
  10.7 5.1 %turn_samples.1 = f32[5376,256]{1,0:T(8,128)} custom-call(f32[256,7680]{1,0:T(8,128)} %x_ref.3, f32[1,7680]{1,0:T(1,128)S(1)} %broadcast_in_dim.4.w_ref), custom_call_target="tpu_custom_call" | custom-call | bytes 11010048 | tf_op jit(solution)/shard_map/turn_samples/pallas_call | solution.py:53
  15.7 8.7 %all-to-all-start = ((f32[32,168,256]{2,1,0:T(8,128)}), f32[32,168,256]{2,1,0:T(8,128)}, u32[]{:S(2)}, u32[]{:S(2)}) async-start(f32[32,168,256]{2,1,0:T(8,128)} %bitcast.48), calls=%async_computation | async-start | bytes 11010048 | tf_op jit(solution)/shard_map/all_to_all | solution.py:321
  24.5 0.6 dynamic-slice.3
  25.2 7.8 %collective-permute-done.1 = f32[128,1152]{1,0:T(8,128)S(1)} collective-permute-done((f32[128,1152]{1,0:T(8,128)S(1)}, f32[128,1152]{1,0:T(8,128)S(1)}, u32[]{:S(2)}, u32[]{:S(2)}) %collective-permute-start.1) | collective-permute-done | bytes 589856 | tf_op jit(solution)/shard_map/ppermute | solution.py:295
  33.6 1.1 slice_select_fusion.1
  34.7 1.7 maximum_maximum_fusion.odd_ref
  36.4 4.2 %coefs_by_bin.1 = f32[32,18,8,128]{3,2,1,0:T(8,128)S(1)} custom-call(f32[128,256]{1,0:T(8,128)S(1)} %reshape.168.t_ref, f32[1,7680]{1,0:T(1,128)S(1)} %broadcast_in_dim.4.w_ref, f32[256,7680]{1,0:T(8,128)} %x_ref.3, f32[256,2304]{1,0:T(8,128)} %maximum_maximum_fusion.odd_ref), custom_call_target="tpu_custom_call" | custom-call | flops 399999991808 | bytes 5898240 | tf_op jit(solution)/shard_map/coefs_by_bin/pallas_call | solution.py:86
  40.6 6.3 %copy.7 = f32[128,7680]{0,1:T(8,128)} copy(f32[128,7680]{1,0:T(8,128)} %param.5) | data formatting | bytes 7864320 | tf_op jit(solution)/shard_map/optimization_barrier | solution.py:322
  46.9 1.0 multiply_bitcast_fusion.c_ref
  47.9 97.1 %all-to-all-done.x_ref = f32[32,168,256]{2,1,0:T(8,128)} async-done(((f32[32,168,256]{2,1,0:T(8,128)}), f32[32,168,256]{2,1,0:T(8,128)}, u32[]{:S(2)}, u32[]{:S(2)}) %all-to-all-start) | async-done | bytes 5505056 | tf_op jit(solution)/shard_map/all_to_all | solution.py:321
  145.1 10.0 %all-to-all-start.1 = ((f32[32,18,8,128]{3,2,1,0:T(8,128)}), f32[32,18,8,128]{3,2,1,0:T(8,128)S(1)}, u32[]{:S(2)}, u32[]{:S(2)}) async-start(f32[32,18,8,128]{3,2,1,0:T(8,128)} %copy-done), calls=%async_computation.1 | async-start | bytes 4718592 | tf_op jit(solution)/shard_map/all_to_all | solution.py:328
  155.2 19.8 %points_gram.1 = (f32[4,4,17,8,128]{4,3,2,1,0:T(8,128)S(1)}, f32[4,4,17,8,128]{4,3,2,1,0:T(8,128)S(1)}) custom-call(s32[4]{0:T(128)S(1)} %pad_add_fusion.where_ref, f32[128,256]{1,0:T(8,128)S(1)} %reshape.168.t_ref, f32[32,168,256]{2,1,0:T(8,128)} %all-to-all-done.x_ref, f32[168,128]{1,0:T(8,128)S(1)} %multiply_bitcast_fusion.c_ref), custom_call_target="tpu_custom_call" | custom-call | flops 6000000000 | bytes 20000000 | tf_op jit(solution)/shard_map/points_gram/pallas_call | solution.py:186
  175.1 2.7 %collective-permute-done.2 = f32[4,4,17,8,128]{4,3,2,1,0:T(8,128)S(1)} collective-permute-done((f32[4,4,17,8,128]{4,3,2,1,0:T(8,128)S(1)}, f32[4,4,17,8,128]{4,3,2,1,0:T(8,128)S(1)}, u32[]{:S(2)}, u32[]{:S(2)}) %collective-permute-start.2) | collective-permute-done | bytes 1114144 | tf_op jit(solution)/shard_map/ppermute | solution.py:286
  177.9 3.1 %collective-permute-start.5 = (f32[4,17,8,128]{3,2,1,0:T(8,128)S(1)}, f32[4,17,8,128]{3,2,1,0:T(8,128)S(1)}, u32[]{:S(2)}, u32[]{:S(2)}) collective-permute-start(f32[4,17,8,128]{3,2,1,0:T(8,128)S(1)} %get-tuple-element.36), channel_id=1, source_target_pairs={{0,192},{32,224},{64,0},{96,32},{128,64},{160,96},{192,128},{224,1... | collective-permute-start | bytes 835592 | tf_op jit(solution)/shard_map/ppermute | solution.py:282
  181.0 0.6 collective-permute-start.4
  181.6 1.0 collective-permute-start.3
  182.6 10.6 %collective-permute-done.5 = f32[4,17,8,128]{3,2,1,0:T(8,128)S(1)} collective-permute-done((f32[4,17,8,128]{3,2,1,0:T(8,128)S(1)}, f32[4,17,8,128]{3,2,1,0:T(8,128)S(1)}, u32[]{:S(2)}, u32[]{:S(2)}) %collective-permute-start.5) | collective-permute-done | bytes 278560 | tf_op jit(solution)/shard_map/ppermute | solution.py:282
  193.2 3.7 %collective-permute-done.3 = f32[4,17,8,128]{3,2,1,0:T(8,128)S(1)} collective-permute-done((f32[4,17,8,128]{3,2,1,0:T(8,128)S(1)}, f32[4,17,8,128]{3,2,1,0:T(8,128)S(1)}, u32[]{:S(2)}, u32[]{:S(2)}) %collective-permute-start.3) | collective-permute-done | bytes 278560 | tf_op jit(solution)/shard_map/ppermute | solution.py:282
  197.3 2.7 %collective-permute-start.7 = (f32[17,8,128]{2,1,0:T(8,128)S(1)}, f32[17,8,128]{2,1,0:T(8,128)S(1)}, u32[]{:S(2)}, u32[]{:S(2)}) collective-permute-start(f32[17,8,128]{2,1,0:T(8,128)S(1)} %get-tuple-element.40), channel_id=1, source_target_pairs={{0,16},{1,17},{2,18},{3,19},{4,20},{5,21},{6,22},{7,23},{8,24},{9,... | collective-permute-start | bytes 208904 | tf_op jit(solution)/shard_map/ppermute | solution.py:282
  200.0 1.8 collective-permute-start.6
  201.8 4.5 %collective-permute-done.8 = f32[17,8,128]{2,1,0:T(8,128)S(1)} collective-permute-done((f32[17,8,128]{2,1,0:T(8,128)S(1)}, f32[17,8,128]{2,1,0:T(8,128)S(1)}, u32[]{:S(2)}, u32[]{:S(2)}) %collective-permute-start.8) | collective-permute-done | bytes 69664 | tf_op jit(solution)/shard_map/ppermute | solution.py:282
  206.4 1.8 collective-permute-done.7
  208.2 0.7 pad_maximum_fusion.1
  209.1 2.7 %bins_gram.1 = (f32[4,3,8,128]{3,2,1,0:T(8,128)S(1)}, f32[4,3,8,128]{3,2,1,0:T(8,128)S(1)}) custom-call(s32[4]{0:T(128)S(1)} %pad_add_fusion.where_ref, f32[4608,128]{1,0:T(8,128)S(1)} %bitcast.47), custom_call_target="tpu_custom_call" | custom-call | flops 500000000 | bytes 2000000 | tf_op jit(solution)/shard_map/bins_gram/pallas_call | solution.py:230
  211.9 6.9 %all-to-all-start.2 = ((f32[8,3,8,128]{3,2,1,0:T(8,128)}), f32[8,3,8,128]{3,2,1,0:T(8,128)S(1)}, u32[]{:S(2)}, u32[]{:S(2)}) async-start(f32[8,3,8,128]{3,2,1,0:T(8,128)} %pad_maximum_fusion.1), calls=%async_computation.2 | async-start | bytes 196608 | tf_op jit(solution)/shard_map/all_to_all | solution.py:335
  218.9 2.7 %collective-permute-start.11 = (f32[3,8,128]{2,1,0:T(8,128)S(1)}, f32[3,8,128]{2,1,0:T(8,128)S(1)}, u32[]{:S(2)}, u32[]{:S(2)}) collective-permute-start(f32[3,8,128]{2,1,0:T(8,128)S(1)} %get-tuple-element.42), channel_id=1, source_target_pairs={{0,128},{32,160},{64,192},{96,224},{128,0},{160,32},{192,64},{224,... | collective-permute-start | bytes 36872 | tf_op jit(solution)/shard_map/ppermute | solution.py:282
  221.7 1.9 collective-permute-start.12
  224.2 1.2 collective-permute-done.12.refs_3_
  225.4 2.5 %all-to-all-done.2.r_ref = f32[8,3,8,128]{3,2,1,0:T(8,128)S(1)} async-done(((f32[8,3,8,128]{3,2,1,0:T(8,128)}), f32[8,3,8,128]{3,2,1,0:T(8,128)S(1)}, u32[]{:S(2)}, u32[]{:S(2)}) %all-to-all-start.2) | async-done | bytes 98336 | tf_op jit(solution)/shard_map/all_to_all | solution.py:335
  227.8 1.4 normalize.1
  (36 shorter events, 2.5 us)
Async XLA Ops:
  0.0 10.6 %copy-start.1 = (f32[7680]{0:T(1024)S(1)}, f32[7680]{0:T(1024)}, u32[]{:S(2)}) copy-start(f32[7680]{0:T(1024)} %param.6) | copy-start | bytes 92164
  2.8 22.4 %collective-permute-start = (f32[128,1152]{1,0:T(8,128)}, f32[128,1152]{1,0:T(8,128)S(1)}, u32[]{:S(2)}, u32[]{:S(2)}) collective-permute-start(f32[128,1152]{1,0:T(8,128)} %get-tuple-element.33), channel_id=1, source_target_pairs={{1,0},{2,1},{3,2},{4,3},{5,4},{6,5},{7,6},{8,7},{9,8},{10,9},{11,1... | collective-permute-start | bytes 1769480 | tf_op jit(solution)/shard_map/ppermute | solution.py:292
  10.5 22.5 %collective-permute-start.1 = (f32[128,1152]{1,0:T(8,128)S(1)}, f32[128,1152]{1,0:T(8,128)S(1)}, u32[]{:S(2)}, u32[]{:S(2)}) collective-permute-start(f32[128,1152]{1,0:T(8,128)S(1)} %get-tuple-element.32), channel_id=1, source_target_pairs={{0,1},{1,2},{2,3},{3,4},{4,5},{5,6},{6,7},{7,8},{8,9},{9,10},{10,1... | collective-permute-start | bytes 1769480 | tf_op jit(solution)/shard_map/ppermute | solution.py:295
  15.7 17.3 %copy-start.3 = (s32[64]{0:T(128)S(1)}, s32[64]{0:T(128)}, u32[]{:S(2)}) copy-start(s32[64]{0:T(128)} %param.7) | copy-start | bytes 772
  15.7 129.3 %all-to-all-start = ((f32[32,168,256]{2,1,0:T(8,128)}), f32[32,168,256]{2,1,0:T(8,128)}, u32[]{:S(2)}, u32[]{:S(2)}) async-start(f32[32,168,256]{2,1,0:T(8,128)} %bitcast.48), calls=%async_computation | async-start | bytes 11010048 | tf_op jit(solution)/shard_map/all_to_all | solution.py:321
  40.6 6.3 %copy-start = (f32[32,18,8,128]{3,2,1,0:T(8,128)}, f32[32,18,8,128]{3,2,1,0:T(8,128)S(1)}, u32[]{:S(2)}) copy-start(f32[32,18,8,128]{3,2,1,0:T(8,128)S(1)} %coefs_by_bin.1) | copy-start | bytes 7077892
  40.6 6.3 %copy-start.2 = (f32[168]{0:T(256)S(1)}, f32[168]{0:T(256)}, u32[]{:S(2)}) copy-start(f32[168]{0:T(256)} %dynamic-slice.3) | copy-start | bytes 2020
  145.1 64.1 %all-to-all-start.1 = ((f32[32,18,8,128]{3,2,1,0:T(8,128)}), f32[32,18,8,128]{3,2,1,0:T(8,128)S(1)}, u32[]{:S(2)}, u32[]{:S(2)}) async-start(f32[32,18,8,128]{3,2,1,0:T(8,128)} %copy-done), calls=%async_computation.1 | async-start | bytes 4718592 | tf_op jit(solution)/shard_map/all_to_all | solution.py:328
  175.0 2.8 %collective-permute-start.2 = (f32[4,4,17,8,128]{4,3,2,1,0:T(8,128)S(1)}, f32[4,4,17,8,128]{4,3,2,1,0:T(8,128)S(1)}, u32[]{:S(2)}, u32[]{:S(2)}) collective-permute-start(f32[4,4,17,8,128]{4,3,2,1,0:T(8,128)S(1)} %get-tuple-element.26), channel_id=1, source_target_pairs={{0,32},{32,0},{64,96},{96,64},{128,160},{160,128},{192,224},{224,1... | collective-permute-start | bytes 3342344 | tf_op jit(solution)/shard_map/ppermute | solution.py:286
  177.9 15.3 %collective-permute-start.5 = (f32[4,17,8,128]{3,2,1,0:T(8,128)S(1)}, f32[4,17,8,128]{3,2,1,0:T(8,128)S(1)}, u32[]{:S(2)}, u32[]{:S(2)}) collective-permute-start(f32[4,17,8,128]{3,2,1,0:T(8,128)S(1)} %get-tuple-element.36), channel_id=1, source_target_pairs={{0,192},{32,224},{64,0},{96,32},{128,64},{160,96},{192,128},{224,1... | collective-permute-start | bytes 835592 | tf_op jit(solution)/shard_map/ppermute | solution.py:282
  181.0 12.2 %collective-permute-start.4 = (f32[4,17,8,128]{3,2,1,0:T(8,128)S(1)}, f32[4,17,8,128]{3,2,1,0:T(8,128)S(1)}, u32[]{:S(2)}, u32[]{:S(2)}) collective-permute-start(f32[4,17,8,128]{3,2,1,0:T(8,128)S(1)} %get-tuple-element.37), channel_id=1, source_target_pairs={{0,128},{32,160},{64,192},{96,224},{128,0},{160,32},{192,64},{224,... | collective-permute-start | bytes 835592 | tf_op jit(solution)/shard_map/ppermute | solution.py:282
  181.6 15.3 %collective-permute-start.3 = (f32[4,17,8,128]{3,2,1,0:T(8,128)S(1)}, f32[4,17,8,128]{3,2,1,0:T(8,128)S(1)}, u32[]{:S(2)}, u32[]{:S(2)}) collective-permute-start(f32[4,17,8,128]{3,2,1,0:T(8,128)S(1)} %get-tuple-element.35), channel_id=1, source_target_pairs={{0,64},{32,96},{64,128},{96,160},{128,192},{160,224},{192,0},{224,... | collective-permute-start | bytes 835592 | tf_op jit(solution)/shard_map/ppermute | solution.py:282
  197.0 9.4 %collective-permute-start.8 = (f32[17,8,128]{2,1,0:T(8,128)S(1)}, f32[17,8,128]{2,1,0:T(8,128)S(1)}, u32[]{:S(2)}, u32[]{:S(2)}) collective-permute-start(f32[17,8,128]{2,1,0:T(8,128)S(1)} %get-tuple-element.39), channel_id=1, source_target_pairs={{0,24},{1,25},{2,26},{3,27},{4,28},{5,29},{6,30},{7,31},{8,0},{9,1... | collective-permute-start | bytes 208904 | tf_op jit(solution)/shard_map/ppermute | solution.py:282
  197.3 10.8 %collective-permute-start.7 = (f32[17,8,128]{2,1,0:T(8,128)S(1)}, f32[17,8,128]{2,1,0:T(8,128)S(1)}, u32[]{:S(2)}, u32[]{:S(2)}) collective-permute-start(f32[17,8,128]{2,1,0:T(8,128)S(1)} %get-tuple-element.40), channel_id=1, source_target_pairs={{0,16},{1,17},{2,18},{3,19},{4,20},{5,21},{6,22},{7,23},{8,24},{9,... | collective-permute-start | bytes 208904 | tf_op jit(solution)/shard_map/ppermute | solution.py:282
  200.0 8.1 %collective-permute-start.6 = (f32[17,8,128]{2,1,0:T(8,128)S(1)}, f32[17,8,128]{2,1,0:T(8,128)S(1)}, u32[]{:S(2)}, u32[]{:S(2)}) collective-permute-start(f32[17,8,128]{2,1,0:T(8,128)S(1)} %get-tuple-element.38), channel_id=1, source_target_pairs={{0,8},{1,9},{2,10},{3,11},{4,12},{5,13},{6,14},{7,15},{8,16},{9,17... | collective-permute-start | bytes 208904 | tf_op jit(solution)/shard_map/ppermute | solution.py:282
  211.9 7.0 %collective-permute-start.9 = (f32[4,3,8,128]{3,2,1,0:T(8,128)S(1)}, f32[4,3,8,128]{3,2,1,0:T(8,128)S(1)}, u32[]{:S(2)}, u32[]{:S(2)}) collective-permute-start(f32[4,3,8,128]{3,2,1,0:T(8,128)S(1)} %get-tuple-element.30), channel_id=1, source_target_pairs={{0,32},{32,0},{64,96},{96,64},{128,160},{160,128},{192,224},{224,1... | collective-permute-start | bytes 147464 | tf_op jit(solution)/shard_map/ppermute | solution.py:286
  211.9 15.9 %all-to-all-start.2 = ((f32[8,3,8,128]{3,2,1,0:T(8,128)}), f32[8,3,8,128]{3,2,1,0:T(8,128)S(1)}, u32[]{:S(2)}, u32[]{:S(2)}) async-start(f32[8,3,8,128]{3,2,1,0:T(8,128)} %pad_maximum_fusion.1), calls=%async_computation.2 | async-start | bytes 196608 | tf_op jit(solution)/shard_map/all_to_all | solution.py:335
  218.8 5.0 %collective-permute-start.10 = (f32[3,8,128]{2,1,0:T(8,128)S(1)}, f32[3,8,128]{2,1,0:T(8,128)S(1)}, u32[]{:S(2)}, u32[]{:S(2)}) collective-permute-start(f32[3,8,128]{2,1,0:T(8,128)S(1)} %get-tuple-element.43), channel_id=1, source_target_pairs={{0,64},{32,96},{64,128},{96,160},{128,192},{160,224},{192,0},{224,... | collective-permute-start | bytes 36872 | tf_op jit(solution)/shard_map/ppermute | solution.py:282
  218.9 5.3 %collective-permute-start.11 = (f32[3,8,128]{2,1,0:T(8,128)S(1)}, f32[3,8,128]{2,1,0:T(8,128)S(1)}, u32[]{:S(2)}, u32[]{:S(2)}) collective-permute-start(f32[3,8,128]{2,1,0:T(8,128)S(1)} %get-tuple-element.42), channel_id=1, source_target_pairs={{0,128},{32,160},{64,192},{96,224},{128,0},{160,32},{192,64},{224,... | collective-permute-start | bytes 36872 | tf_op jit(solution)/shard_map/ppermute | solution.py:282
  221.7 3.7 %collective-permute-start.12 = (f32[3,8,128]{2,1,0:T(8,128)S(1)}, f32[3,8,128]{2,1,0:T(8,128)S(1)}, u32[]{:S(2)}, u32[]{:S(2)}) collective-permute-start(f32[3,8,128]{2,1,0:T(8,128)S(1)} %get-tuple-element.41), channel_id=1, source_target_pairs={{0,192},{32,224},{64,0},{96,32},{128,64},{160,96},{192,128},{224,1... | collective-permute-start | bytes 36872 | tf_op jit(solution)/shard_map/ppermute | solution.py:282

commit v8 on v7

--- a/solution.py
+++ b/solution.py
@@ -1,3 +1,4 @@
+import functools
 import math
 
 import jax
@@ -63,6 +64,34 @@
         compiler_params=pltpu.CompilerParams(vmem_limit_bytes=VMEM_BYTES),
         name="turn_samples",
     )(x, roots)
+
+
+def halves_kernel(first, middle, x_ref, low_ref, high_ref, sems):
+    low = pltpu.make_async_copy(
+        x_ref.at[pl.ds(0, HOP), pl.ds(first, middle - first)], low_ref, sems.at[0]
+    )
+    high = pltpu.make_async_copy(
+        x_ref.at[pl.ds(HOP, HOP), pl.ds(middle, x_ref.shape[1] - middle)], high_ref, sems.at[1]
+    )
+    low.start()
+    high.start()
+    low.wait()
+    high.wait()
+
+
+def halves(x, first, middle):
+    return pl.pallas_call(
+        functools.partial(halves_kernel, first, middle),
+        in_specs=[pl.BlockSpec(memory_space=pl.ANY)],
+        out_specs=(pl.BlockSpec(memory_space=pltpu.VMEM),) * 2,
+        out_shape=(
+            jax.ShapeDtypeStruct((HOP, middle - first), F32),
+            jax.ShapeDtypeStruct((HOP, x.shape[1] - middle), F32),
+        ),
+        scratch_shapes=[pltpu.SemaphoreType.DMA((2,))],
+        compiler_params=pltpu.CompilerParams(vmem_limit_bytes=VMEM_BYTES),
+        name="halo_halves",
+    )(x)
 
 
 def lane_tile(a, n):
@@ -289,12 +318,9 @@
 
 def odd_blocks(snapshots, closing, tm, tm_count, first):
     middle = (first + snapshots.shape[1]) // 2
-    down = lax.ppermute(
-        snapshots[:HOP, first:middle], "tm", [(t, t - 1) for t in range(1, tm_count)]
-    )
-    up = lax.ppermute(
-        snapshots[HOP:, middle:], "tm", [(t, (t + 1) % tm_count) for t in range(tm_count)]
-    )
+    low, high = halves(snapshots, first, middle)
+    down = lax.ppermute(low, "tm", [(t, t - 1) for t in range(1, tm_count)])
+    up = lax.ppermute(high, "tm", [(t, (t + 1) % tm_count) for t in range(tm_count)])
 
     def finish(down, up):
         after = jnp.where(tm == tm_count - 1, closing[:, first:middle], down)

time: 230 us -> 228 us (level)
  no operation moved by 1% of the time
where the time goes in v8:
time: 228 us
  waiting for transfers between devices  131 us (57%)
  starting transfers between devices  47.8 us (21%)
  Pallas kernels  34.4 us (15%)
  local copies, waits for them, and re-layouts  8.08 us (4%)
  other arithmetic  5.77 us (3%)
    all_to_all x1, waiting for transfers between devices, body(): samples = lax.all_to_all(sent, 'tm', 0, 0, tiled=True)  95.6 us
    ppermute x9, waiting for transfers between devices, sent_on(): lax.ppermute(near(d), axis, pairs(d))  22.4 us
    pallas_call x1, Pallas kernels, points_gram(): pl.pallas_call(points_kernel, in_specs=[pl.BlockSpec(memory_space=pltpu.S...  19.8 us
    ppermute x9, starting transfers between devices, sent_on(): lax.ppermute(near(d), axis, pairs(d))  14.2 us
    all_to_all x1, starting transfers between devices, body(): by_bin = lax.all_to_all(coef, 'tm', 0, 0, tiled=True)  10 us
    all_to_all x1, starting transfers between devices, body(): samples = lax.all_to_all(sent, 'tm', 0, 0, tiled=True)  8.74 us
    ppermute x1, waiting for transfers between devices, odd_blocks(): lax.ppermute(high, 'tm', [(t, (t + 1) % tm_count) for t in range(tm_count)])  7.79 us
    ppermute x1, starting transfers between devices, odd_blocks(): down = lax.ppermute(low, 'tm', [(t, t - 1) for t in range(1, tm_count)])  7.74 us
  transfers between devices with their start and end apart: 16, of which 12 were waited for; matrix products, arithmetic and copies ran while one was open for 5% of the time, Pallas kernels for 13%

profile of v8, /device:TPU:2, one launch (start us, length us, event | category | flops | bytes accessed | tf_op | source)
XLA Modules:
  0.0 227.7 jit_solution(548730123640391791)
XLA Ops:
  0.0 1.3 halo_halves.1
  1.3 7.7 %collective-permute-start = (f32[128,1152]{1,0:T(8,128)S(1)}, f32[128,1152]{1,0:T(8,128)S(1)}, u32[]{:S(2)}, u32[]{:S(2)}) collective-permute-start(f32[128,1152]{1,0:T(8,128)S(1)} %get-tuple-element.20), channel_id=1, source_target_pairs={{1,0},{2,1},{3,2},{4,3},{5,4},{6,5},{7,6},{8,7},{9,8},{10,9},{11,1... | collective-permute-start | bytes 1769480 | tf_op jit(solution)/shard_map/ppermute | solution.py:322
  9.2 5.1 %turn_samples.1 = f32[5376,256]{1,0:T(8,128)} custom-call(f32[256,7680]{1,0:T(8,128)} %x_ref.5, f32[1,7680]{1,0:T(1,128)S(1)} %broadcast_in_dim.4.w_ref), custom_call_target="tpu_custom_call" | custom-call | bytes 11010048 | tf_op jit(solution)/shard_map/turn_samples/pallas_call | solution.py:54
  14.2 8.7 %all-to-all-start = ((f32[32,168,256]{2,1,0:T(8,128)}), f32[32,168,256]{2,1,0:T(8,128)}, u32[]{:S(2)}, u32[]{:S(2)}) async-start(f32[32,168,256]{2,1,0:T(8,128)} %bitcast.48), calls=%async_computation | async-start | bytes 11010048 | tf_op jit(solution)/shard_map/all_to_all | solution.py:347
  23.0 0.6 dynamic-slice.3
  23.7 7.8 %collective-permute-done.1 = f32[128,1152]{1,0:T(8,128)S(1)} collective-permute-done((f32[128,1152]{1,0:T(8,128)S(1)}, f32[128,1152]{1,0:T(8,128)S(1)}, u32[]{:S(2)}, u32[]{:S(2)}) %collective-permute-start.1) | collective-permute-done | bytes 589856 | tf_op jit(solution)/shard_map/ppermute | solution.py:323
  32.4 1.8 fusion.21
  34.2 1.7 maximum_maximum_fusion.odd_ref
  35.9 4.2 %coefs_by_bin.1 = f32[32,18,8,128]{3,2,1,0:T(8,128)S(1)} custom-call(f32[128,256]{1,0:T(8,128)S(1)} %reshape.168.t_ref, f32[1,7680]{1,0:T(1,128)S(1)} %broadcast_in_dim.4.w_ref, f32[256,7680]{1,0:T(8,128)} %x_ref.5, f32[256,2304]{1,0:T(8,128)} %maximum_maximum_fusion.odd_ref), custom_call_target="tpu_custom_call" | custom-call | flops 399999991808 | bytes 5898240 | tf_op jit(solution)/shard_map/coefs_by_bin/pallas_call | solution.py:115
  40.1 1.4 copy-done
  41.5 5.5 %copy.7 = f32[128,7680]{0,1:T(8,128)} copy(f32[128,7680]{1,0:T(8,128)} %param.5) | data formatting | bytes 7864320 | tf_op jit(solution)/shard_map/optimization_barrier | solution.py:348
  47.0 1.0 multiply_bitcast_fusion.c_ref
  48.0 95.6 %all-to-all-done.x_ref = f32[32,168,256]{2,1,0:T(8,128)} async-done(((f32[32,168,256]{2,1,0:T(8,128)}), f32[32,168,256]{2,1,0:T(8,128)}, u32[]{:S(2)}, u32[]{:S(2)}) %all-to-all-start) | async-done | bytes 5505056 | tf_op jit(solution)/shard_map/all_to_all | solution.py:347
  143.6 10.0 %all-to-all-start.1 = ((f32[32,18,8,128]{3,2,1,0:T(8,128)}), f32[32,18,8,128]{3,2,1,0:T(8,128)S(1)}, u32[]{:S(2)}, u32[]{:S(2)}) async-start(f32[32,18,8,128]{3,2,1,0:T(8,128)} %copy-done), calls=%async_computation.1 | async-start | bytes 4718592 | tf_op jit(solution)/shard_map/all_to_all | solution.py:354
  153.7 19.8 %points_gram.1 = (f32[4,4,17,8,128]{4,3,2,1,0:T(8,128)S(1)}, f32[4,4,17,8,128]{4,3,2,1,0:T(8,128)S(1)}) custom-call(s32[4]{0:T(128)S(1)} %pad_add_fusion.where_ref, f32[128,256]{1,0:T(8,128)S(1)} %reshape.168.t_ref, f32[32,168,256]{2,1,0:T(8,128)} %all-to-all-done.x_ref, f32[168,128]{1,0:T(8,128)S(1)} %multiply_bitcast_fusion.c_ref), custom_call_target="tpu_custom_call" | custom-call | flops 6000000000 | bytes 20000000 | tf_op jit(solution)/shard_map/points_gram/pallas_call | solution.py:215
  173.6 2.7 %collective-permute-done.2 = f32[4,4,17,8,128]{4,3,2,1,0:T(8,128)S(1)} collective-permute-done((f32[4,4,17,8,128]{4,3,2,1,0:T(8,128)S(1)}, f32[4,4,17,8,128]{4,3,2,1,0:T(8,128)S(1)}, u32[]{:S(2)}, u32[]{:S(2)}) %collective-permute-start.2) | collective-permute-done | bytes 1114144 | tf_op jit(solution)/shard_map/ppermute | solution.py:315
  176.4 3.1 %collective-permute-start.5 = (f32[4,17,8,128]{3,2,1,0:T(8,128)S(1)}, f32[4,17,8,128]{3,2,1,0:T(8,128)S(1)}, u32[]{:S(2)}, u32[]{:S(2)}) collective-permute-start(f32[4,17,8,128]{3,2,1,0:T(8,128)S(1)} %get-tuple-element.39), channel_id=1, source_target_pairs={{0,192},{32,224},{64,0},{96,32},{128,64},{160,96},{192,128},{224,1... | collective-permute-start | bytes 835592 | tf_op jit(solution)/shard_map/ppermute | solution.py:311
  180.2 1.0 collective-permute-start.3
  181.1 10.6 %collective-permute-done.5 = f32[4,17,8,128]{3,2,1,0:T(8,128)S(1)} collective-permute-done((f32[4,17,8,128]{3,2,1,0:T(8,128)S(1)}, f32[4,17,8,128]{3,2,1,0:T(8,128)S(1)}, u32[]{:S(2)}, u32[]{:S(2)}) %collective-permute-start.5) | collective-permute-done | bytes 278560 | tf_op jit(solution)/shard_map/ppermute | solution.py:311
  191.7 3.7 %collective-permute-done.3 = f32[4,17,8,128]{3,2,1,0:T(8,128)S(1)} collective-permute-done((f32[4,17,8,128]{3,2,1,0:T(8,128)S(1)}, f32[4,17,8,128]{3,2,1,0:T(8,128)S(1)}, u32[]{:S(2)}, u32[]{:S(2)}) %collective-permute-start.3) | collective-permute-done | bytes 278560 | tf_op jit(solution)/shard_map/ppermute | solution.py:311
  195.8 2.7 %collective-permute-start.7 = (f32[17,8,128]{2,1,0:T(8,128)S(1)}, f32[17,8,128]{2,1,0:T(8,128)S(1)}, u32[]{:S(2)}, u32[]{:S(2)}) collective-permute-start(f32[17,8,128]{2,1,0:T(8,128)S(1)} %get-tuple-element.43), channel_id=1, source_target_pairs={{0,16},{1,17},{2,18},{3,19},{4,20},{5,21},{6,22},{7,23},{8,24},{9,... | collective-permute-start | bytes 208904 | tf_op jit(solution)/shard_map/ppermute | solution.py:311
  198.5 1.8 collective-permute-start.6
  200.3 4.6 %collective-permute-done.8 = f32[17,8,128]{2,1,0:T(8,128)S(1)} collective-permute-done((f32[17,8,128]{2,1,0:T(8,128)S(1)}, f32[17,8,128]{2,1,0:T(8,128)S(1)}, u32[]{:S(2)}, u32[]{:S(2)}) %collective-permute-start.8) | collective-permute-done | bytes 69664 | tf_op jit(solution)/shard_map/ppermute | solution.py:311
  204.9 1.7 collective-permute-done.7
  206.7 0.6 pad_maximum_fusion.1
  207.6 2.7 %bins_gram.1 = (f32[4,3,8,128]{3,2,1,0:T(8,128)S(1)}, f32[4,3,8,128]{3,2,1,0:T(8,128)S(1)}) custom-call(s32[4]{0:T(128)S(1)} %pad_add_fusion.where_ref, f32[4608,128]{1,0:T(8,128)S(1)} %bitcast.47), custom_call_target="tpu_custom_call" | custom-call | flops 500000000 | bytes 2000000 | tf_op jit(solution)/shard_map/bins_gram/pallas_call | solution.py:259
  210.4 6.9 %all-to-all-start.2 = ((f32[8,3,8,128]{3,2,1,0:T(8,128)}), f32[8,3,8,128]{3,2,1,0:T(8,128)S(1)}, u32[]{:S(2)}, u32[]{:S(2)}) async-start(f32[8,3,8,128]{3,2,1,0:T(8,128)} %pad_maximum_fusion.1), calls=%async_computation.2 | async-start | bytes 196608 | tf_op jit(solution)/shard_map/all_to_all | solution.py:361
  217.4 2.8 %collective-permute-start.11 = (f32[3,8,128]{2,1,0:T(8,128)S(1)}, f32[3,8,128]{2,1,0:T(8,128)S(1)}, u32[]{:S(2)}, u32[]{:S(2)}) collective-permute-start(f32[3,8,128]{2,1,0:T(8,128)S(1)} %get-tuple-element.45), channel_id=1, source_target_pairs={{0,128},{32,160},{64,192},{96,224},{128,0},{160,32},{192,64},{224,... | collective-permute-start | bytes 36872 | tf_op jit(solution)/shard_map/ppermute | solution.py:311
  220.2 1.9 collective-permute-start.12
  222.7 1.2 collective-permute-done.12.refs_3_
  223.9 2.5 %all-to-all-done.2.r_ref = f32[8,3,8,128]{3,2,1,0:T(8,128)S(1)} async-done(((f32[8,3,8,128]{3,2,1,0:T(8,128)}), f32[8,3,8,128]{3,2,1,0:T(8,128)S(1)}, u32[]{:S(2)}, u32[]{:S(2)}) %all-to-all-start.2) | async-done | bytes 98336 | tf_op jit(solution)/shard_map/all_to_all | solution.py:361
  226.3 1.4 normalize.1
  (40 shorter events, 3.4 us)
Async XLA Ops:
  0.0 9.1 %copy-start.3 = (f32[7680]{0:T(1024)S(1)}, f32[7680]{0:T(1024)}, u32[]{:S(2)}) copy-start(f32[7680]{0:T(1024)} %param.6) | copy-start | bytes 92164
  1.3 22.4 %collective-permute-start = (f32[128,1152]{1,0:T(8,128)S(1)}, f32[128,1152]{1,0:T(8,128)S(1)}, u32[]{:S(2)}, u32[]{:S(2)}) collective-permute-start(f32[128,1152]{1,0:T(8,128)S(1)} %get-tuple-element.20), channel_id=1, source_target_pairs={{1,0},{2,1},{3,2},{4,3},{5,4},{6,5},{7,6},{8,7},{9,8},{10,9},{11,1... | collective-permute-start | bytes 1769480 | tf_op jit(solution)/shard_map/ppermute | solution.py:322
  9.0 22.5 %collective-permute-start.1 = (f32[128,1152]{1,0:T(8,128)S(1)}, f32[128,1152]{1,0:T(8,128)S(1)}, u32[]{:S(2)}, u32[]{:S(2)}) collective-permute-start(f32[128,1152]{1,0:T(8,128)S(1)} %get-tuple-element.21), channel_id=1, source_target_pairs={{0,1},{1,2},{2,3},{3,4},{4,5},{5,6},{6,7},{7,8},{8,9},{9,10},{10,1... | collective-permute-start | bytes 1769480 | tf_op jit(solution)/shard_map/ppermute | solution.py:323
  14.2 17.3 %copy-start.5 = (s32[64]{0:T(128)S(1)}, s32[64]{0:T(128)}, u32[]{:S(2)}) copy-start(s32[64]{0:T(128)} %param.7) | copy-start | bytes 772
  14.2 129.3 %all-to-all-start = ((f32[32,168,256]{2,1,0:T(8,128)}), f32[32,168,256]{2,1,0:T(8,128)}, u32[]{:S(2)}, u32[]{:S(2)}) async-start(f32[32,168,256]{2,1,0:T(8,128)} %bitcast.48), calls=%async_computation | async-start | bytes 11010048 | tf_op jit(solution)/shard_map/all_to_all | solution.py:347
  31.5 0.8 copy-start.1
  32.4 1.8 copy-start.2
  40.1 1.4 copy-start
  41.5 5.5 %copy-start.4 = (f32[168]{0:T(256)S(1)}, f32[168]{0:T(256)}, u32[]{:S(2)}) copy-start(f32[168]{0:T(256)} %dynamic-slice.3) | copy-start | bytes 2020
  143.6 64.1 %all-to-all-start.1 = ((f32[32,18,8,128]{3,2,1,0:T(8,128)}), f32[32,18,8,128]{3,2,1,0:T(8,128)S(1)}, u32[]{:S(2)}, u32[]{:S(2)}) async-start(f32[32,18,8,128]{3,2,1,0:T(8,128)} %copy-done), calls=%async_computation.1 | async-start | bytes 4718592 | tf_op jit(solution)/shard_map/all_to_all | solution.py:354
  173.5 2.8 %collective-permute-start.2 = (f32[4,4,17,8,128]{4,3,2,1,0:T(8,128)S(1)}, f32[4,4,17,8,128]{4,3,2,1,0:T(8,128)S(1)}, u32[]{:S(2)}, u32[]{:S(2)}) collective-permute-start(f32[4,4,17,8,128]{4,3,2,1,0:T(8,128)S(1)} %get-tuple-element.30), channel_id=1, source_target_pairs={{0,32},{32,0},{64,96},{96,64},{128,160},{160,128},{192,224},{224,1... | collective-permute-start | bytes 3342344 | tf_op jit(solution)/shard_map/ppermute | solution.py:315
  176.4 15.3 %collective-permute-start.5 = (f32[4,17,8,128]{3,2,1,0:T(8,128)S(1)}, f32[4,17,8,128]{3,2,1,0:T(8,128)S(1)}, u32[]{:S(2)}, u32[]{:S(2)}) collective-permute-start(f32[4,17,8,128]{3,2,1,0:T(8,128)S(1)} %get-tuple-element.39), channel_id=1, source_target_pairs={{0,192},{32,224},{64,0},{96,32},{128,64},{160,96},{192,128},{224,1... | collective-permute-start | bytes 835592 | tf_op jit(solution)/shard_map/ppermute | solution.py:311
  179.5 12.2 %collective-permute-start.4 = (f32[4,17,8,128]{3,2,1,0:T(8,128)S(1)}, f32[4,17,8,128]{3,2,1,0:T(8,128)S(1)}, u32[]{:S(2)}, u32[]{:S(2)}) collective-permute-start(f32[4,17,8,128]{3,2,1,0:T(8,128)S(1)} %get-tuple-element.40), channel_id=1, source_target_pairs={{0,128},{32,160},{64,192},{96,224},{128,0},{160,32},{192,64},{224,... | collective-permute-start | bytes 835592 | tf_op jit(solution)/shard_map/ppermute | solution.py:311
  180.2 15.3 %collective-permute-start.3 = (f32[4,17,8,128]{3,2,1,0:T(8,128)S(1)}, f32[4,17,8,128]{3,2,1,0:T(8,128)S(1)}, u32[]{:S(2)}, u32[]{:S(2)}) collective-permute-start(f32[4,17,8,128]{3,2,1,0:T(8,128)S(1)} %get-tuple-element.38), channel_id=1, source_target_pairs={{0,64},{32,96},{64,128},{96,160},{128,192},{160,224},{192,0},{224,... | collective-permute-start | bytes 835592 | tf_op jit(solution)/shard_map/ppermute | solution.py:311
  195.5 9.4 %collective-permute-start.8 = (f32[17,8,128]{2,1,0:T(8,128)S(1)}, f32[17,8,128]{2,1,0:T(8,128)S(1)}, u32[]{:S(2)}, u32[]{:S(2)}) collective-permute-start(f32[17,8,128]{2,1,0:T(8,128)S(1)} %get-tuple-element.42), channel_id=1, source_target_pairs={{0,24},{1,25},{2,26},{3,27},{4,28},{5,29},{6,30},{7,31},{8,0},{9,1... | collective-permute-start | bytes 208904 | tf_op jit(solution)/shard_map/ppermute | solution.py:311
  195.8 10.8 %collective-permute-start.7 = (f32[17,8,128]{2,1,0:T(8,128)S(1)}, f32[17,8,128]{2,1,0:T(8,128)S(1)}, u32[]{:S(2)}, u32[]{:S(2)}) collective-permute-start(f32[17,8,128]{2,1,0:T(8,128)S(1)} %get-tuple-element.43), channel_id=1, source_target_pairs={{0,16},{1,17},{2,18},{3,19},{4,20},{5,21},{6,22},{7,23},{8,24},{9,... | collective-permute-start | bytes 208904 | tf_op jit(solution)/shard_map/ppermute | solution.py:311
  198.5 8.1 %collective-permute-start.6 = (f32[17,8,128]{2,1,0:T(8,128)S(1)}, f32[17,8,128]{2,1,0:T(8,128)S(1)}, u32[]{:S(2)}, u32[]{:S(2)}) collective-permute-start(f32[17,8,128]{2,1,0:T(8,128)S(1)} %get-tuple-element.41), channel_id=1, source_target_pairs={{0,8},{1,9},{2,10},{3,11},{4,12},{5,13},{6,14},{7,15},{8,16},{9,17... | collective-permute-start | bytes 208904 | tf_op jit(solution)/shard_map/ppermute | solution.py:311
  210.3 7.0 %collective-permute-start.9 = (f32[4,3,8,128]{3,2,1,0:T(8,128)S(1)}, f32[4,3,8,128]{3,2,1,0:T(8,128)S(1)}, u32[]{:S(2)}, u32[]{:S(2)}) collective-permute-start(f32[4,3,8,128]{3,2,1,0:T(8,128)S(1)} %get-tuple-element.34), channel_id=1, source_target_pairs={{0,32},{32,0},{64,96},{96,64},{128,160},{160,128},{192,224},{224,1... | collective-permute-start | bytes 147464 | tf_op jit(solution)/shard_map/ppermute | solution.py:315
  210.4 16.0 %all-to-all-start.2 = ((f32[8,3,8,128]{3,2,1,0:T(8,128)}), f32[8,3,8,128]{3,2,1,0:T(8,128)S(1)}, u32[]{:S(2)}, u32[]{:S(2)}) async-start(f32[8,3,8,128]{3,2,1,0:T(8,128)} %pad_maximum_fusion.1), calls=%async_computation.2 | async-start | bytes 196608 | tf_op jit(solution)/shard_map/all_to_all | solution.py:361
  217.3 5.0 %collective-permute-start.10 = (f32[3,8,128]{2,1,0:T(8,128)S(1)}, f32[3,8,128]{2,1,0:T(8,128)S(1)}, u32[]{:S(2)}, u32[]{:S(2)}) collective-permute-start(f32[3,8,128]{2,1,0:T(8,128)S(1)} %get-tuple-element.46), channel_id=1, source_target_pairs={{0,64},{32,96},{64,128},{96,160},{128,192},{160,224},{192,0},{224,... | collective-permute-start | bytes 36872 | tf_op jit(solution)/shard_map/ppermute | solution.py:311
  217.4 5.3 %collective-permute-start.11 = (f32[3,8,128]{2,1,0:T(8,128)S(1)}, f32[3,8,128]{2,1,0:T(8,128)S(1)}, u32[]{:S(2)}, u32[]{:S(2)}) collective-permute-start(f32[3,8,128]{2,1,0:T(8,128)S(1)} %get-tuple-element.45), channel_id=1, source_target_pairs={{0,128},{32,160},{64,192},{96,224},{128,0},{160,32},{192,64},{224,... | collective-permute-start | bytes 36872 | tf_op jit(solution)/shard_map/ppermute | solution.py:311
  220.2 3.7 %collective-permute-start.12 = (f32[3,8,128]{2,1,0:T(8,128)S(1)}, f32[3,8,128]{2,1,0:T(8,128)S(1)}, u32[]{:S(2)}, u32[]{:S(2)}) collective-permute-start(f32[3,8,128]{2,1,0:T(8,128)S(1)} %get-tuple-element.44), channel_id=1, source_target_pairs={{0,192},{32,224},{64,0},{96,32},{128,64},{160,96},{192,128},{224,1... | collective-permute-start | bytes 36872 | tf_op jit(solution)/shard_map/ppermute | solution.py:311

commit v9 on v8

--- a/solution.py
+++ b/solution.py
@@ -45,21 +45,41 @@
     return max(n * LANES for n in range(1, most + 1) if cols % (n * LANES) == 0)
 
 
-def turn_kernel(x_ref, w_ref, o_ref):
-    o_ref[...] = (x_ref[...] * w_ref[...]).T
+def turn_kernel(x_ref, w_ref, o_ref, in_ref, out_ref, in_sems, out_sems):
+    step = in_ref.shape[2]
+    steps = in_ref.shape[0]
+    ins = [
+        pltpu.make_async_copy(x_ref.at[:, pl.ds(n * step, step)], in_ref.at[n], in_sems.at[n])
+        for n in range(steps)
+    ]
+    outs = [
+        pltpu.make_async_copy(out_ref.at[n], o_ref.at[pl.ds(n * step, step)], out_sems.at[n])
+        for n in range(steps)
+    ]
+    for copy in ins:
+        copy.start()
+    for n in range(steps):
+        ins[n].wait()
+        out_ref[n] = (in_ref[n] * w_ref[:, n * step : (n + 1) * step]).T
+        outs[n].start()
+    for copy in outs:
+        copy.wait()
 
 
 def turned(x, roots, cols):
-    rows, step = x.shape[0], widest(cols, 24)
+    rows, step = x.shape[0], widest(cols, 6)
+    hbm = pl.BlockSpec(memory_space=pl.ANY)
     return pl.pallas_call(
         turn_kernel,
-        grid=(cols // step,),
-        in_specs=[
-            pl.BlockSpec((rows, step), lambda i: (0, i)),
-            pl.BlockSpec((1, step), lambda i: (0, i)),
+        in_specs=[hbm, pl.BlockSpec(memory_space=pltpu.VMEM)],
+        out_specs=hbm,
+        out_shape=jax.ShapeDtypeStruct((cols, rows), F32),
+        scratch_shapes=[
+            pltpu.VMEM((cols // step, rows, step), F32),
+            pltpu.VMEM((cols // step, step, rows), F32),
+            pltpu.SemaphoreType.DMA((cols // step,)),
+            pltpu.SemaphoreType.DMA((cols // step,)),
         ],
-        out_specs=pl.BlockSpec((step, rows), lambda i: (i, 0)),
-        out_shape=jax.ShapeDtypeStruct((cols, rows), F32),
         cost_estimate=pl.CostEstimate(flops=0, bytes_accessed=8 * rows * cols, transcendentals=0),
         compiler_params=pltpu.CompilerParams(vmem_limit_bytes=VMEM_BYTES),
         name="turn_samples",

time: 228 us -> 227 us (level)
    ppermute x1, waiting for transfers between devices: 7.79 us -> 10.3 us  [odd_blocks(): lax.ppermute(high, 'tm', [(t, (t + 1) % tm_count) for t in range(tm_count)])]
    all_to_all x1, waiting for transfers between devices: 95.6 us -> 93.3 us  [body(): samples = lax.all_to_all(sent, 'tm', 0, 0, tiled=True)]
  transfers between devices with their start and end apart: 16 -> 16, of which waited for: 12 -> 11; matrix products, arithmetic and copies ran while one was open for 5% -> 5% of each run, Pallas kernels for 13% -> 13%
where the time goes in v9:
time: 227 us; the launch traced here: 226 us
  waiting for transfers between devices  131 us (58%)
  starting transfers between devices  47.1 us (21%)
  Pallas kernels  33.8 us (15%)
  local copies, waits for them, and re-layouts  8.08 us (4%)
  other arithmetic  5.77 us (3%)
    all_to_all x1, waiting for transfers between devices, body(): samples = lax.all_to_all(sent, 'tm', 0, 0, tiled=True)  93.3 us
    ppermute x9, waiting for transfers between devices, sent_on(): lax.ppermute(near(d), axis, pairs(d))  22 us
    pallas_call x1, Pallas kernels, points_gram(): pl.pallas_call(points_kernel, in_specs=[pl.BlockSpec(memory_space=pltpu.S...  19.8 us
    ppermute x9, starting transfers between devices, sent_on(): lax.ppermute(near(d), axis, pairs(d))  14.4 us
    ppermute x1, waiting for transfers between devices, odd_blocks(): lax.ppermute(high, 'tm', [(t, (t + 1) % tm_count) for t in range(tm_count)])  10.3 us
    all_to_all x1, starting transfers between devices, body(): by_bin = lax.all_to_all(coef, 'tm', 0, 0, tiled=True)  9.27 us
    all_to_all x1, starting transfers between devices, body(): samples = lax.all_to_all(sent, 'tm', 0, 0, tiled=True)  8.63 us
    ppermute x1, starting transfers between devices, odd_blocks(): down = lax.ppermute(low, 'tm', [(t, t - 1) for t in range(1, tm_count)])  7.74 us
  transfers between devices with their start and end apart: 16, of which 11 were waited for; matrix products, arithmetic and copies ran while one was open for 5% of the time, Pallas kernels for 13%

profile of v9, /device:TPU:2, one launch (start us, length us, event | category | flops | bytes accessed | tf_op | source)
XLA Modules:
  0.0 226.1 jit_solution(2069456465806872758)
XLA Ops:
  0.0 1.3 halo_halves.1
  1.3 7.7 %collective-permute-start = (f32[128,1152]{1,0:T(8,128)S(1)}, f32[128,1152]{1,0:T(8,128)S(1)}, u32[]{:S(2)}, u32[]{:S(2)}) collective-permute-start(f32[128,1152]{1,0:T(8,128)S(1)} %get-tuple-element.20), channel_id=1, source_target_pairs={{1,0},{2,1},{3,2},{4,3},{5,4},{6,5},{7,6},{8,7},{9,8},{10,9},{11,1... | collective-permute-start | bytes 1769480 | tf_op jit(solution)/shard_map/ppermute | solution.py:342
  9.2 4.5 %turn_samples.1 = f32[5376,256]{1,0:T(8,128)} custom-call(f32[256,7680]{1,0:T(8,128)} %x_ref.5, f32[1,7680]{1,0:T(1,128)S(1)} %broadcast_in_dim.4.w_ref), custom_call_target="tpu_custom_call" | custom-call | bytes 11010048 | tf_op jit(solution)/shard_map/turn_samples/pallas_call | solution.py:72
  13.7 8.6 %all-to-all-start = ((f32[32,168,256]{2,1,0:T(8,128)}), f32[32,168,256]{2,1,0:T(8,128)}, u32[]{:S(2)}, u32[]{:S(2)}) async-start(f32[32,168,256]{2,1,0:T(8,128)} %bitcast.48), calls=%async_computation | async-start | bytes 11010048 | tf_op jit(solution)/shard_map/all_to_all | solution.py:367
  23.0 10.3 %collective-permute-done.1 = f32[128,1152]{1,0:T(8,128)S(1)} collective-permute-done((f32[128,1152]{1,0:T(8,128)S(1)}, f32[128,1152]{1,0:T(8,128)S(1)}, u32[]{:S(2)}, u32[]{:S(2)}) %collective-permute-start.1) | collective-permute-done | bytes 589856 | tf_op jit(solution)/shard_map/ppermute | solution.py:343
  34.2 1.8 fusion.21
  36.0 1.7 maximum_maximum_fusion.odd_ref
  37.7 4.2 %coefs_by_bin.1 = f32[32,18,8,128]{3,2,1,0:T(8,128)S(1)} custom-call(f32[128,256]{1,0:T(8,128)S(1)} %reshape.168.t_ref, f32[1,7680]{1,0:T(1,128)S(1)} %broadcast_in_dim.4.w_ref, f32[256,7680]{1,0:T(8,128)} %x_ref.5, f32[256,2304]{1,0:T(8,128)} %maximum_maximum_fusion.odd_ref), custom_call_target="tpu_custom_call" | custom-call | flops 399999991808 | bytes 5898240 | tf_op jit(solution)/shard_map/coefs_by_bin/pallas_call | solution.py:135
  41.9 1.4 copy-done
  43.3 5.5 %copy.7 = f32[128,7680]{0,1:T(8,128)} copy(f32[128,7680]{1,0:T(8,128)} %param.5) | data formatting | bytes 7864320 | tf_op jit(solution)/shard_map/optimization_barrier | solution.py:368
  48.8 1.0 multiply_bitcast_fusion.c_ref
  49.8 93.3 %all-to-all-done.x_ref = f32[32,168,256]{2,1,0:T(8,128)} async-done(((f32[32,168,256]{2,1,0:T(8,128)}), f32[32,168,256]{2,1,0:T(8,128)}, u32[]{:S(2)}, u32[]{:S(2)}) %all-to-all-start) | async-done | bytes 5505056 | tf_op jit(solution)/shard_map/all_to_all | solution.py:367
  143.1 9.3 %all-to-all-start.1 = ((f32[32,18,8,128]{3,2,1,0:T(8,128)}), f32[32,18,8,128]{3,2,1,0:T(8,128)S(1)}, u32[]{:S(2)}, u32[]{:S(2)}) async-start(f32[32,18,8,128]{3,2,1,0:T(8,128)} %copy-done), calls=%async_computation.1 | async-start | bytes 4718592 | tf_op jit(solution)/shard_map/all_to_all | solution.py:374
  152.4 19.8 %points_gram.1 = (f32[4,4,17,8,128]{4,3,2,1,0:T(8,128)S(1)}, f32[4,4,17,8,128]{4,3,2,1,0:T(8,128)S(1)}) custom-call(s32[4]{0:T(128)S(1)} %pad_add_fusion.where_ref, f32[128,256]{1,0:T(8,128)S(1)} %reshape.168.t_ref, f32[32,168,256]{2,1,0:T(8,128)} %all-to-all-done.x_ref, f32[168,128]{1,0:T(8,128)S(1)} %multiply_bitcast_fusion.c_ref), custom_call_target="tpu_custom_call" | custom-call | flops 6000000000 | bytes 20000000 | tf_op jit(solution)/shard_map/points_gram/pallas_call | solution.py:235
  172.3 2.7 %collective-permute-done.2 = f32[4,4,17,8,128]{4,3,2,1,0:T(8,128)S(1)} collective-permute-done((f32[4,4,17,8,128]{4,3,2,1,0:T(8,128)S(1)}, f32[4,4,17,8,128]{4,3,2,1,0:T(8,128)S(1)}, u32[]{:S(2)}, u32[]{:S(2)}) %collective-permute-start.2) | collective-permute-done | bytes 1114144 | tf_op jit(solution)/shard_map/ppermute | solution.py:335
  175.2 2.9 %collective-permute-start.5 = (f32[4,17,8,128]{3,2,1,0:T(8,128)S(1)}, f32[4,17,8,128]{3,2,1,0:T(8,128)S(1)}, u32[]{:S(2)}, u32[]{:S(2)}) collective-permute-start(f32[4,17,8,128]{3,2,1,0:T(8,128)S(1)} %get-tuple-element.39), channel_id=1, source_target_pairs={{0,192},{32,224},{64,0},{96,32},{128,64},{160,96},{192,128},{224,1... | collective-permute-start | bytes 835592 | tf_op jit(solution)/shard_map/ppermute | solution.py:331
  178.1 0.8 collective-permute-start.4
  178.9 0.8 collective-permute-start.3
  179.7 10.6 %collective-permute-done.5 = f32[4,17,8,128]{3,2,1,0:T(8,128)S(1)} collective-permute-done((f32[4,17,8,128]{3,2,1,0:T(8,128)S(1)}, f32[4,17,8,128]{3,2,1,0:T(8,128)S(1)}, u32[]{:S(2)}, u32[]{:S(2)}) %collective-permute-start.5) | collective-permute-done | bytes 278560 | tf_op jit(solution)/shard_map/ppermute | solution.py:331
  190.2 3.7 %collective-permute-done.3 = f32[4,17,8,128]{3,2,1,0:T(8,128)S(1)} collective-permute-done((f32[4,17,8,128]{3,2,1,0:T(8,128)S(1)}, f32[4,17,8,128]{3,2,1,0:T(8,128)S(1)}, u32[]{:S(2)}, u32[]{:S(2)}) %collective-permute-start.3) | collective-permute-done | bytes 278560 | tf_op jit(solution)/shard_map/ppermute | solution.py:331
  194.4 2.7 %collective-permute-start.7 = (f32[17,8,128]{2,1,0:T(8,128)S(1)}, f32[17,8,128]{2,1,0:T(8,128)S(1)}, u32[]{:S(2)}, u32[]{:S(2)}) collective-permute-start(f32[17,8,128]{2,1,0:T(8,128)S(1)} %get-tuple-element.43), channel_id=1, source_target_pairs={{0,16},{1,17},{2,18},{3,19},{4,20},{5,21},{6,22},{7,23},{8,24},{9,... | collective-permute-start | bytes 208904 | tf_op jit(solution)/shard_map/ppermute | solution.py:331
  197.1 1.8 collective-permute-start.6
  198.9 4.2 %collective-permute-done.8 = f32[17,8,128]{2,1,0:T(8,128)S(1)} collective-permute-done((f32[17,8,128]{2,1,0:T(8,128)S(1)}, f32[17,8,128]{2,1,0:T(8,128)S(1)}, u32[]{:S(2)}, u32[]{:S(2)}) %collective-permute-start.8) | collective-permute-done | bytes 69664 | tf_op jit(solution)/shard_map/ppermute | solution.py:331
  203.1 1.9 collective-permute-done.7
  205.1 0.6 pad_maximum_fusion.1
  206.0 2.7 %bins_gram.1 = (f32[4,3,8,128]{3,2,1,0:T(8,128)S(1)}, f32[4,3,8,128]{3,2,1,0:T(8,128)S(1)}) custom-call(s32[4]{0:T(128)S(1)} %pad_add_fusion.where_ref, f32[4608,128]{1,0:T(8,128)S(1)} %bitcast.47), custom_call_target="tpu_custom_call" | custom-call | flops 500000000 | bytes 2000000 | tf_op jit(solution)/shard_map/bins_gram/pallas_call | solution.py:279
  208.8 6.9 %all-to-all-start.2 = ((f32[8,3,8,128]{3,2,1,0:T(8,128)}), f32[8,3,8,128]{3,2,1,0:T(8,128)S(1)}, u32[]{:S(2)}, u32[]{:S(2)}) async-start(f32[8,3,8,128]{3,2,1,0:T(8,128)} %pad_maximum_fusion.1), calls=%async_computation.2 | async-start | bytes 196608 | tf_op jit(solution)/shard_map/all_to_all | solution.py:381
  215.9 2.8 %collective-permute-start.11 = (f32[3,8,128]{2,1,0:T(8,128)S(1)}, f32[3,8,128]{2,1,0:T(8,128)S(1)}, u32[]{:S(2)}, u32[]{:S(2)}) collective-permute-start(f32[3,8,128]{2,1,0:T(8,128)S(1)} %get-tuple-element.45), channel_id=1, source_target_pairs={{0,128},{32,160},{64,192},{96,224},{128,0},{160,32},{192,64},{224,... | collective-permute-start | bytes 36872 | tf_op jit(solution)/shard_map/ppermute | solution.py:331
  218.7 2.1 collective-permute-start.12
  221.1 1.3 collective-permute-done.12.refs_3_
  222.4 2.3 %all-to-all-done.2.r_ref = f32[8,3,8,128]{3,2,1,0:T(8,128)S(1)} async-done(((f32[8,3,8,128]{3,2,1,0:T(8,128)}), f32[8,3,8,128]{3,2,1,0:T(8,128)S(1)}, u32[]{:S(2)}, u32[]{:S(2)}) %all-to-all-start.2) | async-done | bytes 98336 | tf_op jit(solution)/shard_map/all_to_all | solution.py:381
  224.7 1.4 normalize.1
  (40 shorter events, 3.3 us)
Async XLA Ops:
  0.0 9.1 %copy-start.3 = (f32[7680]{0:T(1024)S(1)}, f32[7680]{0:T(1024)}, u32[]{:S(2)}) copy-start(f32[7680]{0:T(1024)} %param.6) | copy-start | bytes 92164
  1.3 21.7 %collective-permute-start = (f32[128,1152]{1,0:T(8,128)S(1)}, f32[128,1152]{1,0:T(8,128)S(1)}, u32[]{:S(2)}, u32[]{:S(2)}) collective-permute-start(f32[128,1152]{1,0:T(8,128)S(1)} %get-tuple-element.20), channel_id=1, source_target_pairs={{1,0},{2,1},{3,2},{4,3},{5,4},{6,5},{7,6},{8,7},{9,8},{10,9},{11,1... | collective-permute-start | bytes 1769480 | tf_op jit(solution)/shard_map/ppermute | solution.py:342
  9.0 24.3 %collective-permute-start.1 = (f32[128,1152]{1,0:T(8,128)S(1)}, f32[128,1152]{1,0:T(8,128)S(1)}, u32[]{:S(2)}, u32[]{:S(2)}) collective-permute-start(f32[128,1152]{1,0:T(8,128)S(1)} %get-tuple-element.21), channel_id=1, source_target_pairs={{0,1},{1,2},{2,3},{3,4},{4,5},{5,6},{6,7},{7,8},{8,9},{9,10},{10,1... | collective-permute-start | bytes 1769480 | tf_op jit(solution)/shard_map/ppermute | solution.py:343
  13.6 19.7 %copy-start.5 = (s32[64]{0:T(128)S(1)}, s32[64]{0:T(128)}, u32[]{:S(2)}) copy-start(s32[64]{0:T(128)} %param.7) | copy-start | bytes 772
  13.7 129.4 %all-to-all-start = ((f32[32,168,256]{2,1,0:T(8,128)}), f32[32,168,256]{2,1,0:T(8,128)}, u32[]{:S(2)}, u32[]{:S(2)}) async-start(f32[32,168,256]{2,1,0:T(8,128)} %bitcast.48), calls=%async_computation | async-start | bytes 11010048 | tf_op jit(solution)/shard_map/all_to_all | solution.py:367
  33.3 0.8 copy-start.1
  34.2 1.8 copy-start.2
  41.9 1.4 copy-start
  43.3 5.5 %copy-start.4 = (f32[168]{0:T(256)S(1)}, f32[168]{0:T(256)}, u32[]{:S(2)}) copy-start(f32[168]{0:T(256)} %dynamic-slice.3) | copy-start | bytes 2020
  143.1 63.0 %all-to-all-start.1 = ((f32[32,18,8,128]{3,2,1,0:T(8,128)}), f32[32,18,8,128]{3,2,1,0:T(8,128)S(1)}, u32[]{:S(2)}, u32[]{:S(2)}) async-start(f32[32,18,8,128]{3,2,1,0:T(8,128)} %copy-done), calls=%async_computation.1 | async-start | bytes 4718592 | tf_op jit(solution)/shard_map/all_to_all | solution.py:374
  172.2 2.8 %collective-permute-start.2 = (f32[4,4,17,8,128]{4,3,2,1,0:T(8,128)S(1)}, f32[4,4,17,8,128]{4,3,2,1,0:T(8,128)S(1)}, u32[]{:S(2)}, u32[]{:S(2)}) collective-permute-start(f32[4,4,17,8,128]{4,3,2,1,0:T(8,128)S(1)} %get-tuple-element.30), channel_id=1, source_target_pairs={{0,32},{32,0},{64,96},{96,64},{128,160},{160,128},{192,224},{224,1... | collective-permute-start | bytes 3342344 | tf_op jit(solution)/shard_map/ppermute | solution.py:335
  175.2 15.1 %collective-permute-start.5 = (f32[4,17,8,128]{3,2,1,0:T(8,128)S(1)}, f32[4,17,8,128]{3,2,1,0:T(8,128)S(1)}, u32[]{:S(2)}, u32[]{:S(2)}) collective-permute-start(f32[4,17,8,128]{3,2,1,0:T(8,128)S(1)} %get-tuple-element.39), channel_id=1, source_target_pairs={{0,192},{32,224},{64,0},{96,32},{128,64},{160,96},{192,128},{224,1... | collective-permute-start | bytes 835592 | tf_op jit(solution)/shard_map/ppermute | solution.py:331
  178.1 12.2 %collective-permute-start.4 = (f32[4,17,8,128]{3,2,1,0:T(8,128)S(1)}, f32[4,17,8,128]{3,2,1,0:T(8,128)S(1)}, u32[]{:S(2)}, u32[]{:S(2)}) collective-permute-start(f32[4,17,8,128]{3,2,1,0:T(8,128)S(1)} %get-tuple-element.40), channel_id=1, source_target_pairs={{0,128},{32,160},{64,192},{96,224},{128,0},{160,32},{192,64},{224,... | collective-permute-start | bytes 835592 | tf_op jit(solution)/shard_map/ppermute | solution.py:331
  178.9 15.1 %collective-permute-start.3 = (f32[4,17,8,128]{3,2,1,0:T(8,128)S(1)}, f32[4,17,8,128]{3,2,1,0:T(8,128)S(1)}, u32[]{:S(2)}, u32[]{:S(2)}) collective-permute-start(f32[4,17,8,128]{3,2,1,0:T(8,128)S(1)} %get-tuple-element.38), channel_id=1, source_target_pairs={{0,64},{32,96},{64,128},{96,160},{128,192},{160,224},{192,0},{224,... | collective-permute-start | bytes 835592 | tf_op jit(solution)/shard_map/ppermute | solution.py:331
  194.0 9.0 %collective-permute-start.8 = (f32[17,8,128]{2,1,0:T(8,128)S(1)}, f32[17,8,128]{2,1,0:T(8,128)S(1)}, u32[]{:S(2)}, u32[]{:S(2)}) collective-permute-start(f32[17,8,128]{2,1,0:T(8,128)S(1)} %get-tuple-element.42), channel_id=1, source_target_pairs={{0,24},{1,25},{2,26},{3,27},{4,28},{5,29},{6,30},{7,31},{8,0},{9,1... | collective-permute-start | bytes 208904 | tf_op jit(solution)/shard_map/ppermute | solution.py:331
  194.4 10.6 %collective-permute-start.7 = (f32[17,8,128]{2,1,0:T(8,128)S(1)}, f32[17,8,128]{2,1,0:T(8,128)S(1)}, u32[]{:S(2)}, u32[]{:S(2)}) collective-permute-start(f32[17,8,128]{2,1,0:T(8,128)S(1)} %get-tuple-element.43), channel_id=1, source_target_pairs={{0,16},{1,17},{2,18},{3,19},{4,20},{5,21},{6,22},{7,23},{8,24},{9,... | collective-permute-start | bytes 208904 | tf_op jit(solution)/shard_map/ppermute | solution.py:331
  197.1 7.9 %collective-permute-start.6 = (f32[17,8,128]{2,1,0:T(8,128)S(1)}, f32[17,8,128]{2,1,0:T(8,128)S(1)}, u32[]{:S(2)}, u32[]{:S(2)}) collective-permute-start(f32[17,8,128]{2,1,0:T(8,128)S(1)} %get-tuple-element.41), channel_id=1, source_target_pairs={{0,8},{1,9},{2,10},{3,11},{4,12},{5,13},{6,14},{7,15},{8,16},{9,17... | collective-permute-start | bytes 208904 | tf_op jit(solution)/shard_map/ppermute | solution.py:331
  208.8 7.0 %collective-permute-start.9 = (f32[4,3,8,128]{3,2,1,0:T(8,128)S(1)}, f32[4,3,8,128]{3,2,1,0:T(8,128)S(1)}, u32[]{:S(2)}, u32[]{:S(2)}) collective-permute-start(f32[4,3,8,128]{3,2,1,0:T(8,128)S(1)} %get-tuple-element.34), channel_id=1, source_target_pairs={{0,32},{32,0},{64,96},{96,64},{128,160},{160,128},{192,224},{224,1... | collective-permute-start | bytes 147464 | tf_op jit(solution)/shard_map/ppermute | solution.py:335
  208.8 15.9 %all-to-all-start.2 = ((f32[8,3,8,128]{3,2,1,0:T(8,128)}), f32[8,3,8,128]{3,2,1,0:T(8,128)S(1)}, u32[]{:S(2)}, u32[]{:S(2)}) async-start(f32[8,3,8,128]{3,2,1,0:T(8,128)} %pad_maximum_fusion.1), calls=%async_computation.2 | async-start | bytes 196608 | tf_op jit(solution)/shard_map/all_to_all | solution.py:381
  215.7 5.0 %collective-permute-start.10 = (f32[3,8,128]{2,1,0:T(8,128)S(1)}, f32[3,8,128]{2,1,0:T(8,128)S(1)}, u32[]{:S(2)}, u32[]{:S(2)}) collective-permute-start(f32[3,8,128]{2,1,0:T(8,128)S(1)} %get-tuple-element.46), channel_id=1, source_target_pairs={{0,64},{32,96},{64,128},{96,160},{128,192},{160,224},{192,0},{224,... | collective-permute-start | bytes 36872 | tf_op jit(solution)/shard_map/ppermute | solution.py:331
  215.9 5.2 %collective-permute-start.11 = (f32[3,8,128]{2,1,0:T(8,128)S(1)}, f32[3,8,128]{2,1,0:T(8,128)S(1)}, u32[]{:S(2)}, u32[]{:S(2)}) collective-permute-start(f32[3,8,128]{2,1,0:T(8,128)S(1)} %get-tuple-element.45), channel_id=1, source_target_pairs={{0,128},{32,160},{64,192},{96,224},{128,0},{160,32},{192,64},{224,... | collective-permute-start | bytes 36872 | tf_op jit(solution)/shard_map/ppermute | solution.py:331
  218.7 3.7 %collective-permute-start.12 = (f32[3,8,128]{2,1,0:T(8,128)S(1)}, f32[3,8,128]{2,1,0:T(8,128)S(1)}, u32[]{:S(2)}, u32[]{:S(2)}) collective-permute-start(f32[3,8,128]{2,1,0:T(8,128)S(1)} %get-tuple-element.44), channel_id=1, source_target_pairs={{0,192},{32,224},{64,0},{96,32},{128,64},{160,96},{192,128},{224,1... | collective-permute-start | bytes 36872 | tf_op jit(solution)/shard_map/ppermute | solution.py:331

commit v10 on v9

--- a/solution.py
+++ b/solution.py
@@ -30,6 +30,12 @@
 
 
 NN, NT = ((1,), (0,)), ((1,), (1,))
+
+
+def gram3(a):
+    dg = lambda u, v: lax.dot_general(u, v, (NT, ((), ())), preferred_element_type=F32)
+    mixed = dg(a[0], a[1])
+    return dg(a[0], a[0]) + mixed + mixed.T
 
 
 def table_rows(bin_index, length):
@@ -260,7 +266,7 @@
     for b in range(2):
         mine = pl.ds(2 * BLOCKS * b, 2 * BLOCKS)
         rows = split(jnp.concatenate([s_ref[n, mine] for n in range(tiles)], axis=1))
-        outs.append(re_im(dot3(rows, rows, NT)))
+        outs.append(re_im(gram3(rows)))
     y_at, core = where_ref[0], where_ref[1]
     for b in range(2):
         for y, near, far in by_core(outs[b], core):

time: 227 us -> 226 us (level)
  no operation moved by 1% of the time
where the time goes in v10:
time: 226 us
  waiting for transfers between devices  131 us (58%)
  starting transfers between devices  47.2 us (21%)
  Pallas kernels  33.3 us (15%)
  local copies, waits for them, and re-layouts  8.08 us (4%)
  other arithmetic  5.77 us (3%)
    all_to_all x1, waiting for transfers between devices, body(): samples = lax.all_to_all(sent, 'tm', 0, 0, tiled=True)  93.3 us
    ppermute x9, waiting for transfers between devices, sent_on(): lax.ppermute(near(d), axis, pairs(d))  22 us
    pallas_call x1, Pallas kernels, points_gram(): pl.pallas_call(points_kernel, in_specs=[pl.BlockSpec(memory_space=pltpu.S...  19.8 us
    ppermute x9, starting transfers between devices, sent_on(): lax.ppermute(near(d), axis, pairs(d))  14.4 us
    ppermute x1, waiting for transfers between devices, odd_blocks(): lax.ppermute(high, 'tm', [(t, (t + 1) % tm_count) for t in range(tm_count)])  10.3 us
    all_to_all x1, starting transfers between devices, body(): by_bin = lax.all_to_all(coef, 'tm', 0, 0, tiled=True)  9.27 us
    all_to_all x1, starting transfers between devices, body(): samples = lax.all_to_all(sent, 'tm', 0, 0, tiled=True)  8.63 us
    ppermute x1, starting transfers between devices, odd_blocks(): down = lax.ppermute(low, 'tm', [(t, t - 1) for t in range(1, tm_count)])  7.74 us
  transfers between devices with their start and end apart: 16, of which 11 were waited for; matrix products, arithmetic and copies ran while one was open for 5% of the time, Pallas kernels for 13%

profile of v10, /device:TPU:2, one launch (start us, length us, event | category | flops | bytes accessed | tf_op | source)
XLA Modules:
  0.0 225.7 jit_solution(10067384117232842546)
XLA Ops:
  0.0 1.3 halo_halves.1
  1.3 7.7 %collective-permute-start = (f32[128,1152]{1,0:T(8,128)S(1)}, f32[128,1152]{1,0:T(8,128)S(1)}, u32[]{:S(2)}, u32[]{:S(2)}) collective-permute-start(f32[128,1152]{1,0:T(8,128)S(1)} %get-tuple-element.20), channel_id=1, source_target_pairs={{1,0},{2,1},{3,2},{4,3},{5,4},{6,5},{7,6},{8,7},{9,8},{10,9},{11,1... | collective-permute-start | bytes 1769480 | tf_op jit(solution)/shard_map/ppermute | solution.py:348
  9.2 4.5 %turn_samples.1 = f32[5376,256]{1,0:T(8,128)} custom-call(f32[256,7680]{1,0:T(8,128)} %x_ref.5, f32[1,7680]{1,0:T(1,128)S(1)} %broadcast_in_dim.4.w_ref), custom_call_target="tpu_custom_call" | custom-call | bytes 11010048 | tf_op jit(solution)/shard_map/turn_samples/pallas_call | solution.py:78
  13.7 8.6 %all-to-all-start = ((f32[32,168,256]{2,1,0:T(8,128)}), f32[32,168,256]{2,1,0:T(8,128)}, u32[]{:S(2)}, u32[]{:S(2)}) async-start(f32[32,168,256]{2,1,0:T(8,128)} %bitcast.48), calls=%async_computation | async-start | bytes 11010048 | tf_op jit(solution)/shard_map/all_to_all | solution.py:373
  23.0 10.3 %collective-permute-done.1 = f32[128,1152]{1,0:T(8,128)S(1)} collective-permute-done((f32[128,1152]{1,0:T(8,128)S(1)}, f32[128,1152]{1,0:T(8,128)S(1)}, u32[]{:S(2)}, u32[]{:S(2)}) %collective-permute-start.1) | collective-permute-done | bytes 589856 | tf_op jit(solution)/shard_map/ppermute | solution.py:349
  34.2 1.8 fusion.21
  36.0 1.7 maximum_maximum_fusion.odd_ref
  37.7 4.2 %coefs_by_bin.1 = f32[32,18,8,128]{3,2,1,0:T(8,128)S(1)} custom-call(f32[128,256]{1,0:T(8,128)S(1)} %reshape.168.t_ref, f32[1,7680]{1,0:T(1,128)S(1)} %broadcast_in_dim.4.w_ref, f32[256,7680]{1,0:T(8,128)} %x_ref.5, f32[256,2304]{1,0:T(8,128)} %maximum_maximum_fusion.odd_ref), custom_call_target="tpu_custom_call" | custom-call | flops 399999991808 | bytes 5898240 | tf_op jit(solution)/shard_map/coefs_by_bin/pallas_call | solution.py:141
  41.9 1.4 copy-done
  43.3 5.5 %copy.7 = f32[128,7680]{0,1:T(8,128)} copy(f32[128,7680]{1,0:T(8,128)} %param.5) | data formatting | bytes 7864320 | tf_op jit(solution)/shard_map/optimization_barrier | solution.py:374
  48.8 1.0 multiply_bitcast_fusion.c_ref
  49.8 93.3 %all-to-all-done.x_ref = f32[32,168,256]{2,1,0:T(8,128)} async-done(((f32[32,168,256]{2,1,0:T(8,128)}), f32[32,168,256]{2,1,0:T(8,128)}, u32[]{:S(2)}, u32[]{:S(2)}) %all-to-all-start) | async-done | bytes 5505056 | tf_op jit(solution)/shard_map/all_to_all | solution.py:373
  143.1 9.3 %all-to-all-start.1 = ((f32[32,18,8,128]{3,2,1,0:T(8,128)}), f32[32,18,8,128]{3,2,1,0:T(8,128)S(1)}, u32[]{:S(2)}, u32[]{:S(2)}) async-start(f32[32,18,8,128]{3,2,1,0:T(8,128)} %copy-done), calls=%async_computation.1 | async-start | bytes 4718592 | tf_op jit(solution)/shard_map/all_to_all | solution.py:380
  152.4 19.8 %points_gram.1 = (f32[4,4,17,8,128]{4,3,2,1,0:T(8,128)S(1)}, f32[4,4,17,8,128]{4,3,2,1,0:T(8,128)S(1)}) custom-call(s32[4]{0:T(128)S(1)} %pad_add_fusion.where_ref, f32[128,256]{1,0:T(8,128)S(1)} %reshape.168.t_ref, f32[32,168,256]{2,1,0:T(8,128)} %all-to-all-done.x_ref, f32[168,128]{1,0:T(8,128)S(1)} %multiply_bitcast_fusion.c_ref), custom_call_target="tpu_custom_call" | custom-call | flops 6000000000 | bytes 20000000 | tf_op jit(solution)/shard_map/points_gram/pallas_call | solution.py:241
  172.3 2.7 %collective-permute-done.2 = f32[4,4,17,8,128]{4,3,2,1,0:T(8,128)S(1)} collective-permute-done((f32[4,4,17,8,128]{4,3,2,1,0:T(8,128)S(1)}, f32[4,4,17,8,128]{4,3,2,1,0:T(8,128)S(1)}, u32[]{:S(2)}, u32[]{:S(2)}) %collective-permute-start.2) | collective-permute-done | bytes 1114144 | tf_op jit(solution)/shard_map/ppermute | solution.py:341
  175.2 2.9 %collective-permute-start.5 = (f32[4,17,8,128]{3,2,1,0:T(8,128)S(1)}, f32[4,17,8,128]{3,2,1,0:T(8,128)S(1)}, u32[]{:S(2)}, u32[]{:S(2)}) collective-permute-start(f32[4,17,8,128]{3,2,1,0:T(8,128)S(1)} %get-tuple-element.39), channel_id=1, source_target_pairs={{0,192},{32,224},{64,0},{96,32},{128,64},{160,96},{192,128},{224,1... | collective-permute-start | bytes 835592 | tf_op jit(solution)/shard_map/ppermute | solution.py:337
  178.1 0.8 collective-permute-start.4
  178.9 0.8 collective-permute-start.3
  179.7 10.6 %collective-permute-done.5 = f32[4,17,8,128]{3,2,1,0:T(8,128)S(1)} collective-permute-done((f32[4,17,8,128]{3,2,1,0:T(8,128)S(1)}, f32[4,17,8,128]{3,2,1,0:T(8,128)S(1)}, u32[]{:S(2)}, u32[]{:S(2)}) %collective-permute-start.5) | collective-permute-done | bytes 278560 | tf_op jit(solution)/shard_map/ppermute | solution.py:337
  190.2 3.7 %collective-permute-done.3 = f32[4,17,8,128]{3,2,1,0:T(8,128)S(1)} collective-permute-done((f32[4,17,8,128]{3,2,1,0:T(8,128)S(1)}, f32[4,17,8,128]{3,2,1,0:T(8,128)S(1)}, u32[]{:S(2)}, u32[]{:S(2)}) %collective-permute-start.3) | collective-permute-done | bytes 278560 | tf_op jit(solution)/shard_map/ppermute | solution.py:337
  194.4 2.7 %collective-permute-start.7 = (f32[17,8,128]{2,1,0:T(8,128)S(1)}, f32[17,8,128]{2,1,0:T(8,128)S(1)}, u32[]{:S(2)}, u32[]{:S(2)}) collective-permute-start(f32[17,8,128]{2,1,0:T(8,128)S(1)} %get-tuple-element.43), channel_id=1, source_target_pairs={{0,16},{1,17},{2,18},{3,19},{4,20},{5,21},{6,22},{7,23},{8,24},{9,... | collective-permute-start | bytes 208904 | tf_op jit(solution)/shard_map/ppermute | solution.py:337
  197.1 1.8 collective-permute-start.6
  198.9 4.2 %collective-permute-done.8 = f32[17,8,128]{2,1,0:T(8,128)S(1)} collective-permute-done((f32[17,8,128]{2,1,0:T(8,128)S(1)}, f32[17,8,128]{2,1,0:T(8,128)S(1)}, u32[]{:S(2)}, u32[]{:S(2)}) %collective-permute-start.8) | collective-permute-done | bytes 69664 | tf_op jit(solution)/shard_map/ppermute | solution.py:337
  203.1 1.9 collective-permute-done.7
  205.1 0.6 pad_maximum_fusion.1
  206.0 2.3 %bins_gram.1 = (f32[4,3,8,128]{3,2,1,0:T(8,128)S(1)}, f32[4,3,8,128]{3,2,1,0:T(8,128)S(1)}) custom-call(s32[4]{0:T(128)S(1)} %pad_add_fusion.where_ref, f32[4608,128]{1,0:T(8,128)S(1)} %bitcast.47), custom_call_target="tpu_custom_call" | custom-call | flops 500000000 | bytes 2000000 | tf_op jit(solution)/shard_map/bins_gram/pallas_call | solution.py:285
  208.4 6.9 %all-to-all-start.2 = ((f32[8,3,8,128]{3,2,1,0:T(8,128)}), f32[8,3,8,128]{3,2,1,0:T(8,128)S(1)}, u32[]{:S(2)}, u32[]{:S(2)}) async-start(f32[8,3,8,128]{3,2,1,0:T(8,128)} %pad_maximum_fusion.1), calls=%async_computation.2 | async-start | bytes 196608 | tf_op jit(solution)/shard_map/all_to_all | solution.py:387
  215.5 2.8 %collective-permute-start.11 = (f32[3,8,128]{2,1,0:T(8,128)S(1)}, f32[3,8,128]{2,1,0:T(8,128)S(1)}, u32[]{:S(2)}, u32[]{:S(2)}) collective-permute-start(f32[3,8,128]{2,1,0:T(8,128)S(1)} %get-tuple-element.45), channel_id=1, source_target_pairs={{0,128},{32,160},{64,192},{96,224},{128,0},{160,32},{192,64},{224,... | collective-permute-start | bytes 36872 | tf_op jit(solution)/shard_map/ppermute | solution.py:337
  218.3 2.1 collective-permute-start.12
  220.7 1.3 collective-permute-done.12.refs_3_
  222.0 2.3 %all-to-all-done.2.r_ref = f32[8,3,8,128]{3,2,1,0:T(8,128)S(1)} async-done(((f32[8,3,8,128]{3,2,1,0:T(8,128)}), f32[8,3,8,128]{3,2,1,0:T(8,128)S(1)}, u32[]{:S(2)}, u32[]{:S(2)}) %all-to-all-start.2) | async-done | bytes 98336 | tf_op jit(solution)/shard_map/all_to_all | solution.py:387
  224.3 1.4 normalize.1
  (40 shorter events, 3.3 us)
Async XLA Ops:
  0.0 9.1 %copy-start.3 = (f32[7680]{0:T(1024)S(1)}, f32[7680]{0:T(1024)}, u32[]{:S(2)}) copy-start(f32[7680]{0:T(1024)} %param.6) | copy-start | bytes 92164
  1.3 21.7 %collective-permute-start = (f32[128,1152]{1,0:T(8,128)S(1)}, f32[128,1152]{1,0:T(8,128)S(1)}, u32[]{:S(2)}, u32[]{:S(2)}) collective-permute-start(f32[128,1152]{1,0:T(8,128)S(1)} %get-tuple-element.20), channel_id=1, source_target_pairs={{1,0},{2,1},{3,2},{4,3},{5,4},{6,5},{7,6},{8,7},{9,8},{10,9},{11,1... | collective-permute-start | bytes 1769480 | tf_op jit(solution)/shard_map/ppermute | solution.py:348
  9.0 24.3 %collective-permute-start.1 = (f32[128,1152]{1,0:T(8,128)S(1)}, f32[128,1152]{1,0:T(8,128)S(1)}, u32[]{:S(2)}, u32[]{:S(2)}) collective-permute-start(f32[128,1152]{1,0:T(8,128)S(1)} %get-tuple-element.21), channel_id=1, source_target_pairs={{0,1},{1,2},{2,3},{3,4},{4,5},{5,6},{6,7},{7,8},{8,9},{9,10},{10,1... | collective-permute-start | bytes 1769480 | tf_op jit(solution)/shard_map/ppermute | solution.py:349
  13.6 19.7 %copy-start.5 = (s32[64]{0:T(128)S(1)}, s32[64]{0:T(128)}, u32[]{:S(2)}) copy-start(s32[64]{0:T(128)} %param.7) | copy-start | bytes 772
  13.7 129.4 %all-to-all-start = ((f32[32,168,256]{2,1,0:T(8,128)}), f32[32,168,256]{2,1,0:T(8,128)}, u32[]{:S(2)}, u32[]{:S(2)}) async-start(f32[32,168,256]{2,1,0:T(8,128)} %bitcast.48), calls=%async_computation | async-start | bytes 11010048 | tf_op jit(solution)/shard_map/all_to_all | solution.py:373
  33.3 0.8 copy-start.1
  34.2 1.8 copy-start.2
  41.9 1.4 copy-start
  43.3 5.5 %copy-start.4 = (f32[168]{0:T(256)S(1)}, f32[168]{0:T(256)}, u32[]{:S(2)}) copy-start(f32[168]{0:T(256)} %dynamic-slice.3) | copy-start | bytes 2020
  143.1 63.0 %all-to-all-start.1 = ((f32[32,18,8,128]{3,2,1,0:T(8,128)}), f32[32,18,8,128]{3,2,1,0:T(8,128)S(1)}, u32[]{:S(2)}, u32[]{:S(2)}) async-start(f32[32,18,8,128]{3,2,1,0:T(8,128)} %copy-done), calls=%async_computation.1 | async-start | bytes 4718592 | tf_op jit(solution)/shard_map/all_to_all | solution.py:380
  172.2 2.8 %collective-permute-start.2 = (f32[4,4,17,8,128]{4,3,2,1,0:T(8,128)S(1)}, f32[4,4,17,8,128]{4,3,2,1,0:T(8,128)S(1)}, u32[]{:S(2)}, u32[]{:S(2)}) collective-permute-start(f32[4,4,17,8,128]{4,3,2,1,0:T(8,128)S(1)} %get-tuple-element.30), channel_id=1, source_target_pairs={{0,32},{32,0},{64,96},{96,64},{128,160},{160,128},{192,224},{224,1... | collective-permute-start | bytes 3342344 | tf_op jit(solution)/shard_map/ppermute | solution.py:341
  175.2 15.1 %collective-permute-start.5 = (f32[4,17,8,128]{3,2,1,0:T(8,128)S(1)}, f32[4,17,8,128]{3,2,1,0:T(8,128)S(1)}, u32[]{:S(2)}, u32[]{:S(2)}) collective-permute-start(f32[4,17,8,128]{3,2,1,0:T(8,128)S(1)} %get-tuple-element.39), channel_id=1, source_target_pairs={{0,192},{32,224},{64,0},{96,32},{128,64},{160,96},{192,128},{224,1... | collective-permute-start | bytes 835592 | tf_op jit(solution)/shard_map/ppermute | solution.py:337
  178.1 12.2 %collective-permute-start.4 = (f32[4,17,8,128]{3,2,1,0:T(8,128)S(1)}, f32[4,17,8,128]{3,2,1,0:T(8,128)S(1)}, u32[]{:S(2)}, u32[]{:S(2)}) collective-permute-start(f32[4,17,8,128]{3,2,1,0:T(8,128)S(1)} %get-tuple-element.40), channel_id=1, source_target_pairs={{0,128},{32,160},{64,192},{96,224},{128,0},{160,32},{192,64},{224,... | collective-permute-start | bytes 835592 | tf_op jit(solution)/shard_map/ppermute | solution.py:337
  178.9 15.1 %collective-permute-start.3 = (f32[4,17,8,128]{3,2,1,0:T(8,128)S(1)}, f32[4,17,8,128]{3,2,1,0:T(8,128)S(1)}, u32[]{:S(2)}, u32[]{:S(2)}) collective-permute-start(f32[4,17,8,128]{3,2,1,0:T(8,128)S(1)} %get-tuple-element.38), channel_id=1, source_target_pairs={{0,64},{32,96},{64,128},{96,160},{128,192},{160,224},{192,0},{224,... | collective-permute-start | bytes 835592 | tf_op jit(solution)/shard_map/ppermute | solution.py:337
  194.0 9.0 %collective-permute-start.8 = (f32[17,8,128]{2,1,0:T(8,128)S(1)}, f32[17,8,128]{2,1,0:T(8,128)S(1)}, u32[]{:S(2)}, u32[]{:S(2)}) collective-permute-start(f32[17,8,128]{2,1,0:T(8,128)S(1)} %get-tuple-element.42), channel_id=1, source_target_pairs={{0,24},{1,25},{2,26},{3,27},{4,28},{5,29},{6,30},{7,31},{8,0},{9,1... | collective-permute-start | bytes 208904 | tf_op jit(solution)/shard_map/ppermute | solution.py:337
  194.4 10.6 %collective-permute-start.7 = (f32[17,8,128]{2,1,0:T(8,128)S(1)}, f32[17,8,128]{2,1,0:T(8,128)S(1)}, u32[]{:S(2)}, u32[]{:S(2)}) collective-permute-start(f32[17,8,128]{2,1,0:T(8,128)S(1)} %get-tuple-element.43), channel_id=1, source_target_pairs={{0,16},{1,17},{2,18},{3,19},{4,20},{5,21},{6,22},{7,23},{8,24},{9,... | collective-permute-start | bytes 208904 | tf_op jit(solution)/shard_map/ppermute | solution.py:337
  197.1 7.9 %collective-permute-start.6 = (f32[17,8,128]{2,1,0:T(8,128)S(1)}, f32[17,8,128]{2,1,0:T(8,128)S(1)}, u32[]{:S(2)}, u32[]{:S(2)}) collective-permute-start(f32[17,8,128]{2,1,0:T(8,128)S(1)} %get-tuple-element.41), channel_id=1, source_target_pairs={{0,8},{1,9},{2,10},{3,11},{4,12},{5,13},{6,14},{7,15},{8,16},{9,17... | collective-permute-start | bytes 208904 | tf_op jit(solution)/shard_map/ppermute | solution.py:337
  208.3 7.0 %collective-permute-start.9 = (f32[4,3,8,128]{3,2,1,0:T(8,128)S(1)}, f32[4,3,8,128]{3,2,1,0:T(8,128)S(1)}, u32[]{:S(2)}, u32[]{:S(2)}) collective-permute-start(f32[4,3,8,128]{3,2,1,0:T(8,128)S(1)} %get-tuple-element.34), channel_id=1, source_target_pairs={{0,32},{32,0},{64,96},{96,64},{128,160},{160,128},{192,224},{224,1... | collective-permute-start | bytes 147464 | tf_op jit(solution)/shard_map/ppermute | solution.py:341
  208.4 15.9 %all-to-all-start.2 = ((f32[8,3,8,128]{3,2,1,0:T(8,128)}), f32[8,3,8,128]{3,2,1,0:T(8,128)S(1)}, u32[]{:S(2)}, u32[]{:S(2)}) async-start(f32[8,3,8,128]{3,2,1,0:T(8,128)} %pad_maximum_fusion.1), calls=%async_computation.2 | async-start | bytes 196608 | tf_op jit(solution)/shard_map/all_to_all | solution.py:387
  215.3 5.0 %collective-permute-start.10 = (f32[3,8,128]{2,1,0:T(8,128)S(1)}, f32[3,8,128]{2,1,0:T(8,128)S(1)}, u32[]{:S(2)}, u32[]{:S(2)}) collective-permute-start(f32[3,8,128]{2,1,0:T(8,128)S(1)} %get-tuple-element.46), channel_id=1, source_target_pairs={{0,64},{32,96},{64,128},{96,160},{128,192},{160,224},{192,0},{224,... | collective-permute-start | bytes 36872 | tf_op jit(solution)/shard_map/ppermute | solution.py:337
  215.5 5.2 %collective-permute-start.11 = (f32[3,8,128]{2,1,0:T(8,128)S(1)}, f32[3,8,128]{2,1,0:T(8,128)S(1)}, u32[]{:S(2)}, u32[]{:S(2)}) collective-permute-start(f32[3,8,128]{2,1,0:T(8,128)S(1)} %get-tuple-element.45), channel_id=1, source_target_pairs={{0,128},{32,160},{64,192},{96,224},{128,0},{160,32},{192,64},{224,... | collective-permute-start | bytes 36872 | tf_op jit(solution)/shard_map/ppermute | solution.py:337
  218.3 3.7 %collective-permute-start.12 = (f32[3,8,128]{2,1,0:T(8,128)S(1)}, f32[3,8,128]{2,1,0:T(8,128)S(1)}, u32[]{:S(2)}, u32[]{:S(2)}) collective-permute-start(f32[3,8,128]{2,1,0:T(8,128)S(1)} %get-tuple-element.44), channel_id=1, source_target_pairs={{0,192},{32,224},{64,0},{96,32},{128,64},{160,96},{192,128},{224,1... | collective-permute-start | bytes 36872 | tf_op jit(solution)/shard_map/ppermute | solution.py:337
